TPU v7x, 32 devices: a whole 2x2x4 slice. The times are simulated.
32 devices in a mesh: pair: 8 (over z, x), virt: 4 (over y, core).
Axes of the slice: x: 2, y: 2, z: 4, core: 2. Of those that a mesh axis runs over, the one named last changes fastest.
Arguments:
- amplitudes: bfloat16 [2048, 3, 4096], P('pair'), may hold values from -6 to 6
- screen: int32 [2048, 3], P('pair'), may hold values from 0 to 15, all different within a row; in each aligned block of 256 rows (0 to 255, 256 to 511, ...) at most 96 rows name the same one
- integrals: bfloat16 [16, 4096, 8192], P('pair', None, 'virt'), may hold values from -0.0546875 to 0.0546875
- other: float32 [2048, 8192], P('pair', 'virt'), may hold values from -6 to 6
- occ_first: float32 [32], replicated, may hold values from -2 to -0.4
- occ_second: float32 [64], replicated, may hold values from -2 to -0.4
- virt_first: float32 [2, 64], replicated, may hold values from 0.3 to 3
- virt_second: float32 [2, 64], replicated, may hold values from 0.3 to 3
Outputs:
- new_amplitudes: float32 [2048, 8192], P('pair', 'virt')
Inputs may be any that keep to these rules, and one draw needn't show every extreme that they name: `screen`: the 3 entries of a row differ. Within each aligned block of 256 rows (the rows of one pair index) no tile pair is named more than 96 times, and some tile pair is named exactly 96 times.
All inputs are finite; a program needn't handle non-finite values.
Results may differ from a plain program's by a relative error of at most 0.0003.
Values may be sent and summed in bfloat16 or wider, within the bound.
No kernel may reach another device: no remote copies, remote signals or barrier semaphores. Data moves between devices by JAX's collectives and lax.ppermute only.
A program may use at most 192 MiB of HBM per device.

v0:
```python
import jax
import jax.numpy as jnp
from jax import lax
from jax.sharding import PartitionSpec as P


def per_device(
    amplitudes, screen, integrals, other, occ_first, occ_second, virt_first, virt_second
):
    rows, top, width = amplitudes.shape
    n_pair = lax.axis_size("pair")
    cd_dev = integrals.shape[0]
    cols = integrals.shape[2]
    experts = cd_dev * n_pair
    capacity = rows * top * 2 // experts
    flat = screen.reshape(-1)
    onehot = (flat[:, None] == jnp.arange(experts, dtype=jnp.int32)[None, :]).astype(jnp.int32)
    slots = jnp.sum((jnp.cumsum(onehot, axis=0) - 1) * onehot, axis=1)
    buffer = jnp.zeros((experts, capacity, width), amplitudes.dtype)
    buffer = buffer.at[flat, slots].set(amplitudes.reshape(-1, width))
    buffer = buffer.reshape(n_pair, cd_dev, capacity, width)
    returned = lax.all_to_all(
        jnp.einsum(
            "scnk,ckm->scnm",
            lax.all_to_all(buffer, "pair", split_axis=0, concat_axis=0, tiled=True),
            integrals,
            preferred_element_type=jnp.float32,
        ),
        "pair",
        split_axis=0,
        concat_axis=0,
        tiled=True,
    )
    returned = returned.reshape(experts, capacity, cols)
    picked = returned[flat, slots]
    ladder = jnp.sum(picked.reshape(rows, top, cols), axis=1)
    tile = virt_first.shape[1]
    tile_sq = tile * tile
    start_col = lax.axis_index("virt") * cols
    tile_pair = start_col // tile_sq
    first_a = start_col % tile_sq // tile
    energy_a = lax.dynamic_slice(virt_first, (tile_pair, first_a), (1, cols // tile)).reshape(-1)
    energy_b = lax.dynamic_slice_in_dim(virt_second, tile_pair, 1, 0).reshape(-1)
    virt_sum = (energy_a[:, None] + energy_b[None, :]).reshape(cols)
    per_i = occ_second.shape[0]
    energy_i = lax.dynamic_slice_in_dim(
        occ_first, lax.axis_index("pair") * (rows // per_i), rows // per_i, 0
    )
    occ_sum = (energy_i[:, None] + occ_second[None, :]).reshape(rows)
    denom = occ_sum[:, None] - virt_sum[None, :]
    return (0.5 * ladder + other) / denom


def solution(mesh):
    return jax.shard_map(
        per_device,
        mesh=mesh,
        in_specs=(
            P("pair", None, None),
            P("pair", None),
            P("pair", None, "virt"),
            P("pair", "virt"),
            P(),
            P(),
            P(),
            P(),
        ),
        out_specs=P("pair", "virt"),
        check_vma=False,
    )
```

profile of v0, /device:TPU:0, one launch (start us, length us, event | category | flops | bytes accessed | tf_op | source)
XLA Modules:
  0.0 873.7 jit_solution(14293589841791560477)
XLA Ops:
  0.0 0.8 copy.16
  0.8 0.2 eq.27
  1.0 0.2 eq.31
  1.3 0.2 reshape.106
  1.5 1.7 reduce-window.6
  3.2 0.3 slice_reduce_fusion
  3.5 11.4 %copy.20 = bf16[256,3,4096]{2,1,0:T(4,128)(2,1)} copy(bf16[256,3,4096]{2,0,1:T(8,128)(2,1)} %param.8) | data formatting | bytes 12582912 | tf_op args[0]
  14.9 13.7 %reshape.120 = bf16[768,4096]{1,0:T(8,128)(2,1)} reshape(bf16[256,3,4096]{2,1,0:T(4,128)(2,1)} %copy.20) | data formatting | bytes 12582912 | tf_op jit(solution)/shard_map/reshape | solution.py:20
  28.6 0.1 fusion.9
  28.7 6.2 broadcast_in_dim.2
  34.9 199.9 %scatter_fusion = bf16[16,96,4096]{2,1,0:T(8,128)(2,1)} fusion(bf16[16,96,4096]{2,1,0:T(8,128)(2,1)} %broadcast_in_dim.2, s32[768]{0:T(1024)S(1)} %get-tuple-element.6, bf16[768,4096]{1,0:T(8,128)(2,1)} %reshape.120), kind=kCustom, calls=%fused_computation.1 | custom fusion | bytes 18880512 | tf_op jit(solution)/shard_map/scatter | solution.py:20
  234.8 280.5 %all_to_all.10 = bf16[8,2,96,4096]{3,2,1,0:T(8,128)(2,1)S(1)} all-to-all(bf16[8,2,96,4096]{3,2,1,0:T(8,128)(2,1)} %bitcast.31), channel_id=1, replica_groups=mesh['pair'=8,'virt'=4] {'pair'}, dimensions={0} | all-to-all | bytes 25165824 | tf_op jit(solution)/shard_map/all_to_all | solution.py:25
  515.3 32.0 %fusion.3 = f32[8,2,96,2048]{3,2,0,1:T(8,128)} fusion(bf16[2,4096,2048]{2,1,0:T(8,128)(2,1)} %param.10, bf16[8,2,96,4096]{3,2,1,0:T(8,128)(2,1)S(1)} %all_to_all.10), kind=kOutput, calls=%fused_computation.5 | convolution fusion | flops 25769803776 | bytes 58720256 | tf_op jit(solution)/shard_map/scnk,ckm->scnm/dot_general | solution.py:23
  547.3 11.2 %copy.22 = f32[8,2,96,2048]{3,2,1,0:T(8,128)} copy(f32[8,2,96,2048]{3,2,0,1:T(8,128)} %fusion.3) | data formatting | bytes 25165824 | tf_op jit(solution)/shard_map/scnk,ckm->scnm/transpose | solution.py:23
  558.6 5.7 all-to-all-start.1
  564.4 0.1 dynamic-slice_bitcast_fusion.1
  564.4 0.1 broadcast_add_fusion
  564.6 0.1 dynamic_slice.9
  564.7 0.1 add.95
  564.8 271.3 %all-to-all-done.1 = f32[8,2,96,2048]{3,2,1,0:T(8,128)} async-done(((f32[8,2,96,2048]{3,2,1,0:T(8,128)}), f32[8,2,96,2048]{3,2,1,0:T(8,128)}, u32[]{:S(2)}, u32[]{:S(2)}) %all-to-all-start.1) | async-done | bytes 12582944 | tf_op jit(solution)/shard_map/all_to_all | solution.py:22
  836.1 14.9 %gather_fusion = f32[768,2048]{1,0:T(8,128)} fusion(f32[16,96,2048]{2,1,0:T(8,128)} %bitcast.5, s32[768]{0:T(1024)S(1)} %get-tuple-element.5), kind=kCustom, calls=%fused_computation | custom fusion | bytes 12589056 | tf_op jit(solution)/shard_map/gather | solution.py:35
  851.0 10.5 %reshape.111 = f32[256,3,2048]{2,1,0:T(4,128)} reshape(f32[768,2048]{1,0:T(8,128)} %gather_fusion) | data formatting | bytes 12582912 | tf_op jit(solution)/shard_map/reshape | solution.py:36
  861.5 8.8 %reduce_sum.22 = f32[256,2048]{1,0:T(8,128)S(1)} reduce(f32[256,3,2048]{2,1,0:T(4,128)} %reshape.111, f32[]{:T(128)} %constant.57.clone.1), dimensions={1}, to_apply=%region_4.5 | reduce | flops 1048576 | bytes 8388612 | tf_op jit(solution)/shard_map/reduce_sum | solution.py:36
  870.3 3.4 subtract_divide_fusion
  (14 shorter events, 0.2 us)
Async XLA Ops:
  0.0 564.3 %copy-start = (f32[2,64]{1,0:T(2,128)S(1)}, f32[2,64]{1,0:T(2,128)}, u32[]{:S(2)}) copy-start(f32[2,64]{1,0:T(2,128)} %param.15) | copy-start | bytes 1540
  558.6 5.8 copy-start.2
  558.6 6.0 copy-start.3
  558.6 6.1 copy-start.1
  558.6 277.6 %all-to-all-start.1 = ((f32[8,2,96,2048]{3,2,1,0:T(8,128)}), f32[8,2,96,2048]{3,2,1,0:T(8,128)}, u32[]{:S(2)}, u32[]{:S(2)}) async-start(f32[8,2,96,2048]{3,2,1,0:T(8,128)} %copy.22), calls=%async_computation.1 | async-start | bytes 25165824 | tf_op jit(solution)/shard_map/all_to_all | solution.py:22
where the time goes:
time: 876 us; the launch traced here: 874 us
  blocking collectives  281 us (32%)
  waiting for transfers between devices  271 us (31%)
  local copies, waits for them, and re-layouts  270 us (31%)
  matrix products  32 us (4%)
  other arithmetic  14.2 us (2%)
    all_to_all x1, blocking collectives, per_device(): lax.all_to_all(buffer, 'pair', split_axis=0, concat_axis=0, tiled=True)  281 us
    all_to_all x1, waiting for transfers between devices, per_device(): lax.all_to_all(jnp.einsum('scnk,ckm->scnm', lax.all_to_all(buffer, 'pair'...  271 us
    scatter x1, local copies, waits for them, and re-layouts, per_device(): buffer = buffer.at[flat, slots].set(amplitudes.reshape(-1, width))  200 us
    dot_general x1, matrix products, per_device(): jnp.einsum('scnk,ckm->scnm', lax.all_to_all(buffer, 'pair', split_axis=0,...  32 us
  transfers between devices with their start and end apart: 1, of which 1 were waited for; matrix products, arithmetic and copies ran while one was open for 0% of the time, Pallas kernels for 0%

commit v1 on v0

v1 whole, which is shorter than its diff:
```python
import functools

import jax
import jax.numpy as jnp
from jax import lax
from jax.experimental import pallas as pl
from jax.experimental.pallas import tpu as pltpu
from jax.sharding import PartitionSpec as P

VMEM_LIMIT = 56 * 1024 * 1024
F32 = jnp.float32
BF16 = jnp.bfloat16
COL_CHUNKS = 2


def params():
    return pltpu.CompilerParams(vmem_limit_bytes=VMEM_LIMIT)


def cost(flops, nbytes):
    return pl.CostEstimate(flops=int(flops), bytes_accessed=int(nbytes), transcendentals=0)


def encode(v):
    w = v * 8.0
    sq = w * w
    quad = sq * sq
    return ((w * jnp.abs(w)) * (quad * sq)).astype(BF16)


def decode(code):
    c = code.astype(F32)
    a = jnp.abs(c)
    t = lax.rsqrt(jnp.maximum(a, 1e-37))
    u = lax.rsqrt(t)
    root = u * lax.rsqrt(u) * 0.125
    root = jnp.where(a < 1e-37, 0.0, root)
    return jnp.where(c < 0.0, -root, root)


def pack_kernel(code_ref, tiles_ref, out_ref):
    block = out_ref.shape[0]
    top, rows, _ = tiles_ref.shape
    want = lax.broadcasted_iota(jnp.int32, (block, rows), 0) + pl.program_id(0) * block
    total = None
    for k in range(top):
        pick = (want == code_ref[k : k + 1, :]).astype(F32).astype(BF16)
        part = jnp.dot(pick, tiles_ref[k], preferred_element_type=F32)
        total = part if total is None else total + part
    out_ref[...] = total.astype(BF16)


def pack(codes, tiles, n_slots):
    top, rows, width = tiles.shape
    steps = 4
    return pl.pallas_call(
        pack_kernel,
        grid=(steps,),
        in_specs=[
            pl.BlockSpec((top, rows), lambda i: (0, 0)),
            pl.BlockSpec((top, rows, width), lambda i: (0, 0, 0)),
        ],
        out_specs=pl.BlockSpec((n_slots // steps, width), lambda i: (i, 0)),
        out_shape=jax.ShapeDtypeStruct((n_slots, width), BF16),
        compiler_params=params(),
        cost_estimate=cost(2 * n_slots * top * rows * width, 4 * n_slots * width),
        name="pack_tiles",
    )(codes, tiles)


def product_kernel(cap, place_ref, *refs):
    *parts, w_ref, keep_ref, send_ref, acc_ref = refs
    quarter = parts[0].shape[1]
    total = None
    for j, lhs in enumerate(parts):
        q = lax.bitwise_xor(place_ref[0], j)
        rhs = w_ref[0, pl.ds(pl.multiple_of(q * quarter, quarter), quarter), :]
        part = jnp.dot(lhs[...], rhs, preferred_element_type=F32)
        total = part if total is None else total + part
    acc_ref[...] = total.reshape(acc_ref.shape)
    mine = place_ref[1]
    for g in range(acc_ref.shape[0] // 2):
        keep_ref[g] = acc_ref[2 * g + mine]
        send_ref[g] = encode(acc_ref[2 * g + 1 - mine])


def product(place, lhs, integrals, c, first, cols, cap):
    slots, quarter = lhs[0].shape
    width = integrals.shape[1]
    step = min(256, cols)
    sources = slots // cap
    half = sources // 2
    base = first // step
    return pl.pallas_call(
        functools.partial(product_kernel, cap),
        grid_spec=pltpu.PrefetchScalarGridSpec(
            num_scalar_prefetch=1,
            grid=(cols // step,),
            in_specs=[pl.BlockSpec((slots, quarter), lambda j, s: (0, 0))] * len(lhs)
            + [pl.BlockSpec((1, width, step), lambda j, s: (c, 0, base + j))],
            out_specs=[
                pl.BlockSpec((half, cap, step), lambda j, s: (0, 0, j)),
                pl.BlockSpec((half, cap, step), lambda j, s: (0, 0, j)),
            ],
            scratch_shapes=[pltpu.VMEM((sources, cap, step), F32)],
        ),
        out_shape=[
            jax.ShapeDtypeStruct((half, cap, cols), F32),
            jax.ShapeDtypeStruct((half, cap, cols), BF16),
        ],
        compiler_params=params(),
        cost_estimate=cost(2 * slots * width * cols, 2 * width * cols + 2 * slots * width + 4 * slots * cols),
        name="tile_products",
    )(place, *lhs, integrals)


def merge_kernel(place_ref, inv_ref, keep0, keep1, got0, got1, own_ref, send_ref):
    _, cap, _ = keep0.shape
    rows = inv_ref.shape[1]
    lane = lax.broadcasted_iota(jnp.int32, (rows, 4 * cap), 1)
    hit = None
    for c in range(4):
        slot = inv_ref[0, :, c : c + 1]
        one = lane == jnp.where(slot < 0, -1, slot + c * cap)
        hit = one if hit is None else hit | one
    pick = hit.astype(F32).astype(BF16)
    values = jnp.concatenate(
        [keep0[0], keep1[0], decode(got0[0]), decode(got1[0])], axis=0
    )
    high = values.astype(BF16)
    low = (values - high.astype(F32)).astype(BF16)
    dense = jnp.dot(pick, high, preferred_element_type=F32)
    dense = dense + jnp.dot(pick, low, preferred_element_type=F32)
    send_ref[0] = encode(dense)

    @pl.when(pl.program_id(1) == place_ref[2])
    def _():
        own_ref[...] = dense


def merge(place, inv, keep, got):
    groups, cap, cols = keep[0].shape
    rows = inv.shape[1]
    step = min(512, cols)
    spec = pl.BlockSpec((1, cap, step), lambda j, g, s: (g, 0, j))
    return pl.pallas_call(
        merge_kernel,
        grid_spec=pltpu.PrefetchScalarGridSpec(
            num_scalar_prefetch=1,
            grid=(cols // step, groups),
            in_specs=[pl.BlockSpec((1, rows, 4), lambda j, g, s: (g, 0, 0))] + [spec] * 4,
            out_specs=[
                pl.BlockSpec((rows, step), lambda j, g, s: (0, j)),
                pl.BlockSpec((1, rows, step), lambda j, g, s: (g, 0, j)),
            ],
        ),
        out_shape=[
            jax.ShapeDtypeStruct((rows, cols), F32),
            jax.ShapeDtypeStruct((groups, rows, cols), BF16),
        ],
        compiler_params=params(),
        cost_estimate=cost(16 * groups * rows * cap * cols, 14 * groups * cap * cols + 4 * groups * rows * cols),
        name="merge_rows",
    )(place, inv, *keep, *got)


def finish_kernel(chunks, place_ref, *refs):
    own, got = refs[:chunks], refs[chunks : 2 * chunks]
    other_ref, occ_ref, virt_ref, out_ref = refs[2 * chunks :]
    groups = got[0].shape[0]
    cols = own[0].shape[1]
    for j in range(chunks):
        total = own[j][...]
        for k in range(1, groups):
            total = total + decode(got[j][lax.rem(place_ref[2] + k, groups)])
        span = slice(j * cols, (j + 1) * cols)
        denom = occ_ref[...] - virt_ref[:, span]
        out_ref[:, span] = (0.5 * total + other_ref[:, span]) / denom


def finish(place, own, got, other, occ_sum, virt_sum):
    rows, width = other.shape
    chunks = len(own)
    groups, _, cols = got[0].shape
    step = 64
    return pl.pallas_call(
        functools.partial(finish_kernel, chunks),
        grid_spec=pltpu.PrefetchScalarGridSpec(
            num_scalar_prefetch=1,
            grid=(rows // step,),
            in_specs=[pl.BlockSpec((step, cols), lambda i, s: (i, 0))] * chunks
            + [pl.BlockSpec((groups, step, cols), lambda i, s: (0, i, 0))] * chunks
            + [
                pl.BlockSpec((step, width), lambda i, s: (i, 0)),
                pl.BlockSpec((step, 1), lambda i, s: (i, 0)),
                pl.BlockSpec((1, width), lambda i, s: (0, 0)),
            ],
            out_specs=pl.BlockSpec((step, width), lambda i, s: (i, 0)),
        ),
        out_shape=jax.ShapeDtypeStruct((rows, width), F32),
        compiler_params=params(),
        cost_estimate=cost(40 * rows * width, (12 + 2 * groups) * rows * width),
        name="finish_rows",
    )(place, *own, *got, other, occ_sum, virt_sum)


def ranks(named, experts):
    blocks, top, rows = named.shape
    flat = named.reshape(blocks, top * rows)
    onehot = flat[:, :, None] == jnp.arange(experts, dtype=jnp.int32)
    before = jnp.tri(top * rows, k=-1, dtype=BF16)
    count = jnp.einsum("ij,bje->bie", before, onehot.astype(BF16), preferred_element_type=F32)
    shape = (blocks, top, rows, experts)
    return onehot.reshape(shape), count.astype(jnp.int32).reshape(shape)


def per_device(
    amplitudes, screen, integrals, other, occ_first, occ_second, virt_first, virt_second
):
    rows, top, width = amplitudes.shape
    n_pair = lax.axis_size("pair")
    n_virt = lax.axis_size("virt")
    cd_dev, _, cols = integrals.shape
    experts = cd_dev * n_pair
    cap = rows * top * 2 // experts
    quarter = width // n_virt
    pair = lax.axis_index("pair")
    virt = lax.axis_index("virt")
    low, high = pair % 2, pair // 2
    groups = n_pair // 2
    place = jnp.stack([virt, low, high]).astype(jnp.int32)

    named = screen.T[None]
    onehot, rank = ranks(named, experts)
    slot = jnp.sum(jnp.where(onehot, rank, 0), axis=3)[0]
    expert = named[0]
    where = expert // cd_dev * cap + slot
    tiles = lax.dynamic_slice_in_dim(amplitudes, virt * quarter, quarter, 2)
    tiles = tiles.transpose(1, 0, 2)

    every = lax.all_gather(screen, "pair")

    swap_low = [(i, i ^ 1) for i in range(n_pair)]

    lhs = []
    earlier = None
    for c in range(cd_dev):
        codes = jnp.where(expert % cd_dev == c, where, -1)
        buffer = pack(codes, tiles, n_pair * cap)
        if earlier is not None:
            buffer, earlier = lax.optimization_barrier((buffer, earlier))
            lhs[-1] = earlier
        earlier = lax.all_to_all(buffer, "pair", 0, 0, tiled=True)
        lhs.append(earlier)
    quarters = []
    for c in range(cd_dev):
        held = {0: lhs[c]}
        bit = n_virt // 2
        while bit:
            swap = [(i, i ^ bit) for i in range(n_virt)]
            held.update({at | bit: lax.ppermute(x, "virt", swap) for at, x in held.items()})
            bit //= 2
        quarters.append([held[at] for at in range(n_virt)])

    owners = lax.dynamic_index_in_dim(
        every.reshape(groups, 2, rows, top), low, 1, False
    )
    all_hot, all_rank = ranks(owners.transpose(0, 2, 1), experts)
    inv = jnp.sum(jnp.where(all_hot, all_rank + 1, 0), axis=1) - 1
    mine = lax.dynamic_slice_in_dim(inv, pair * cd_dev, cd_dev, 2)
    theirs = lax.dynamic_slice_in_dim(inv, (pair + 1 - 2 * low) * cd_dev, cd_dev, 2)
    inv = jnp.concatenate([mine, theirs], axis=2)

    keep, got = [], []
    part = cols // COL_CHUNKS
    for c in range(cd_dev):
        keep.append([])
        got.append([])
        for j in range(COL_CHUNKS):
            kept, sent = product(place, quarters[c], integrals, c, j * part, part, cap)
            keep[c].append(kept)
            got[c].append(lax.ppermute(sent, "pair", swap_low))

    own, back = [], []
    lines = [[i for i in range(n_pair) if i % 2 == side] for side in range(2)]
    for j in range(COL_CHUNKS):
        dense, sent = merge(
            place, inv, [keep[c][j] for c in range(cd_dev)], [got[c][j] for c in range(cd_dev)]
        )
        own.append(dense)
        back.append(lax.all_to_all(sent, "pair", 0, 0, tiled=True, axis_index_groups=lines))

    tile = virt_first.shape[1]
    tile_sq = tile * tile
    start_col = virt * cols
    tile_pair = start_col // tile_sq
    first_a = start_col % tile_sq // tile
    energy_a = lax.dynamic_slice(virt_first, (tile_pair, first_a), (1, cols // tile)).reshape(-1)
    energy_b = lax.dynamic_slice_in_dim(virt_second, tile_pair, 1, 0).reshape(-1)
    virt_sum = (energy_a[:, None] + energy_b[None, :]).reshape(1, cols)
    per_i = occ_second.shape[0]
    energy_i = lax.dynamic_slice_in_dim(occ_first, pair * (rows // per_i), rows // per_i, 0)
    occ_sum = (energy_i[:, None] + occ_second[None, :]).reshape(rows, 1)
    return finish(place, own, back, other, occ_sum, virt_sum)


def solution(mesh):
    return jax.shard_map(
        per_device,
        mesh=mesh,
        in_specs=(
            P("pair", None, None),
            P("pair", None),
            P("pair", None, "virt"),
            P("pair", "virt"),
            P(),
            P(),
            P(),
            P(),
        ),
        out_specs=P("pair", "virt"),
        check_vma=False,
    )
```

time: 876 us -> 339 us (0.39)
  local copies, waits for them, and re-layouts: 270 us -> 9.36 us
  blocking collectives: 281 us -> 30.5 us
  waiting for transfers between devices: 271 us -> 176 us
  Pallas kernels: 0 us -> 90.3 us
  matrix products: 32 us -> 1.48 us
  starting transfers between devices: 5.69 us -> 27.2 us
  other arithmetic: 14.2 us -> 2.84 us
    all_to_all x1 -> x0, blocking collectives: 281 us -> none  [per_device(): lax.all_to_all(buffer, 'pair', split_axis=0, concat_axis=0, tiled=True)]
    scatter x1 -> x0, local copies, waits for them, and re-layouts: 200 us -> none  [per_device(): buffer = buffer.at[flat, slots].set(amplitudes.reshape(-1, width))]
    all_to_all x1 -> x4, waiting for transfers between devices: 271 us -> 111 us  [the longest x2 67.7 us: per_device(): earlier = lax.all_to_all(buffer, 'pair', 0, 0, tiled=True)]
    pallas_call x0 -> x9, Pallas kernels: none -> 90.3 us  [the longest x4 51 us: product(): pl.pallas_call(functools.partial(product_kernel, cap), grid_spec=pltpu.Pr...]
    ppermute x0 -> x10, waiting for transfers between devices: none -> 65.2 us  [the longest x6 33.2 us: per_device(): lax.ppermute(x, 'virt', swap)]
    dot_general x1 -> x2, matrix products: 32 us -> 1.48 us  [ranks(): jnp.einsum('ij,bje->bie', before, onehot.astype(BF16), preferred_element_...]
    all_gather x0 -> x1, blocking collectives: none -> 30.5 us  [per_device(): every = lax.all_gather(screen, 'pair')]
    reshape x3 -> x1, local copies, waits for them, and re-layouts: 24.4 us -> 0.03 us  [per_device(): every.reshape(groups, 2, rows, top)]
  transfers between devices with their start and end apart: 1 -> 14, of which waited for: 1 -> 8; matrix products, arithmetic and copies ran while one was open for 0% -> 1% of each run, Pallas kernels for 0% -> 20%
where the time goes in v1:
time: 339 us; the launch traced here: 338 us
  waiting for transfers between devices  176 us (52%)
  Pallas kernels  90.3 us (27%)
  blocking collectives  30.5 us (9%)
  starting transfers between devices  27.2 us (8%)
  local copies, waits for them, and re-layouts  9.36 us (3%)
    all_to_all x2, waiting for transfers between devices, per_device(): earlier = lax.all_to_all(buffer, 'pair', 0, 0, tiled=True)  67.7 us
    pallas_call x4, Pallas kernels, product(): pl.pallas_call(functools.partial(product_kernel, cap), grid_spec=pltpu.Pr...  51 us
    all_to_all x2, waiting for transfers between devices, per_device(): lax.all_to_all(sent, 'pair', 0, 0, tiled=True, axis_index_groups=lines)  43.4 us
    ppermute x6, waiting for transfers between devices, per_device(): lax.ppermute(x, 'virt', swap)  33.2 us
    ppermute x4, waiting for transfers between devices, per_device(): got[c].append(lax.ppermute(sent, 'pair', swap_low))  32 us
    all_gather x1, blocking collectives, per_device(): every = lax.all_gather(screen, 'pair')  30.5 us
    pallas_call x2, Pallas kernels, merge(): pl.pallas_call(merge_kernel, grid_spec=pltpu.PrefetchScalarGridSpec(num_s...  22.1 us
    all_to_all x2, starting transfers between devices, per_device(): earlier = lax.all_to_all(buffer, 'pair', 0, 0, tiled=True)  11 us
  transfers between devices with their start and end apart: 14, of which 8 were waited for; matrix products, arithmetic and copies ran while one was open for 1% of the time, Pallas kernels for 20%

profile of v1, /device:TPU:0, one launch (start us, length us, event | category | flops | bytes accessed | tf_op | source)
XLA Modules:
  0.0 338.1 jit_solution(9290672245215169829)
XLA Ops:
  2.8 2.7 dynamic-slice_bitcast_fusion.tiles_ref
  5.5 4.4 %pack_tiles.3 = bf16[768,1024]{1,0:T(8,128)(2,1)} custom-call(s32[3,256]{1,0:T(4,128)} %get-tuple-element.33.code_ref, bf16[3,256,1024]{2,1,0:T(8,128)(2,1)} %dynamic-slice_bitcast_fusion.tiles_ref), custom_call_target="tpu_custom_call" | custom-call | flops 1207959552 | bytes 3145728 | tf_op jit(solution)/shard_map/pack_tiles/pallas_call | solution.py:56
  9.9 7.4 %all-to-all-start = ((bf16[8,96,1024]{2,1,0:T(8,128)(2,1)}), bf16[8,96,1024]{2,1,0:T(8,128)(2,1)S(1)}, u32[]{:S(2)}, u32[]{:S(2)}) async-start(bf16[8,96,1024]{2,1,0:T(8,128)(2,1)} %bitcast.61), calls=%async_computation | async-start | bytes 3145728 | tf_op jit(solution)/shard_map/all_to_all | solution.py:253
  17.9 4.4 %pack_tiles.2 = bf16[768,1024]{1,0:T(8,128)(2,1)} custom-call(s32[3,256]{1,0:T(4,128)} %compare_select_fusion.1.code_ref, bf16[3,256,1024]{2,1,0:T(8,128)(2,1)} %dynamic-slice_bitcast_fusion.tiles_ref), custom_call_target="tpu_custom_call" | custom-call | flops 1207959552 | bytes 3145728 | tf_op jit(solution)/shard_map/pack_tiles/pallas_call | solution.py:56
  22.3 32.0 %all-to-all-done = bf16[8,96,1024]{2,1,0:T(8,128)(2,1)S(1)} async-done(((bf16[8,96,1024]{2,1,0:T(8,128)(2,1)}), bf16[8,96,1024]{2,1,0:T(8,128)(2,1)S(1)}, u32[]{:S(2)}, u32[]{:S(2)}) %all-to-all-start) | async-done | bytes 1572896 | tf_op jit(solution)/shard_map/all_to_all | solution.py:253
  54.3 3.6 %all-to-all-start.1 = ((bf16[8,96,1024]{2,1,0:T(8,128)(2,1)}), bf16[8,96,1024]{2,1,0:T(8,128)(2,1)S(1)}, u32[]{:S(2)}, u32[]{:S(2)}) async-start(bf16[8,96,1024]{2,1,0:T(8,128)(2,1)} %bitcast.60), calls=%async_computation.1 | async-start | bytes 3145728 | tf_op jit(solution)/shard_map/all_to_all | solution.py:253
  57.9 1.6 collective-permute-start.1
  59.5 35.6 %all-to-all-done.1 = bf16[8,96,1024]{2,1,0:T(8,128)(2,1)S(1)} async-done(((bf16[8,96,1024]{2,1,0:T(8,128)(2,1)}), bf16[8,96,1024]{2,1,0:T(8,128)(2,1)S(1)}, u32[]{:S(2)}, u32[]{:S(2)}) %all-to-all-start.1) | async-done | bytes 1572896 | tf_op jit(solution)/shard_map/all_to_all | solution.py:253
  97.2 33.2 %collective-permute-done.4.refs_2_ = bf16[768,1024]{1,0:T(8,128)(2,1)} collective-permute-done((bf16[768,1024]{1,0:T(8,128)(2,1)S(1)}, bf16[768,1024]{1,0:T(8,128)(2,1)}, u32[]{:S(2)}, u32[]{:S(2)}) %collective-permute-start.4) | collective-permute-done | bytes 1572896 | tf_op jit(solution)/shard_map/ppermute | solution.py:261
  130.4 30.5 %all-gather = s32[2048,3]{0,1:T(4,128)S(1)} all-gather(s32[256,3]{0,1:T(4,128)S(1)} %copy-done.4), channel_id=2, replica_groups=mesh['pair'=8,'virt'=4] {'pair'}, dimensions={0}, use_global_device_ids=true | all-gather | bytes 27648 | tf_op jit(solution)/shard_map/all_gather | solution.py:241
  161.7 12.8 %tile_products.6 = (f32[4,96,1024]{2,1,0:T(8,128)}, bf16[4,96,1024]{2,1,0:T(8,128)(2,1)}) custom-call(s32[3]{0:T(128)} %pad_add_fusion.1.place_ref, bf16[768,1024]{1,0:T(8,128)(2,1)} %bitcast.54, bf16[768,1024]{1,0:T(8,128)(2,1)} %collective-permute-done.refs_1_, bf16[768,1024]{1,0:T(8,128)(2,1)} %collective-permute-done.1.refs_2_, ...), custom_call_target="tpu_custom_call" | custom-call | flops 6442450944 | bytes 17825792 | tf_op jit(solution)/shard_map/tile_products/pallas_call | solution.py:94
  175.1 12.8 %tile_products.7 = (f32[4,96,1024]{2,1,0:T(8,128)}, bf16[4,96,1024]{2,1,0:T(8,128)(2,1)}) custom-call(s32[3]{0:T(128)} %pad_add_fusion.1.place_ref, bf16[768,1024]{1,0:T(8,128)(2,1)} %bitcast.58, bf16[768,1024]{1,0:T(8,128)(2,1)} %collective-permute-done.3.refs_1_, bf16[768,1024]{1,0:T(8,128)(2,1)} %collective-permute-done.4.refs_2_, ...), custom_call_target="tpu_custom_call" | custom-call | flops 6442450944 | bytes 17825792 | tf_op jit(solution)/shard_map/tile_products/pallas_call | solution.py:94
  191.9 13.2 %collective-permute-done.9.got1 = bf16[4,96,1024]{2,1,0:T(8,128)(2,1)S(1)} collective-permute-done((bf16[4,96,1024]{2,1,0:T(8,128)(2,1)}, bf16[4,96,1024]{2,1,0:T(8,128)(2,1)S(1)}, u32[]{:S(2)}, u32[]{:S(2)}) %collective-permute-start.9) | collective-permute-done | bytes 786464 | tf_op jit(solution)/shard_map/ppermute | solution.py:282
  206.0 11.1 %merge_rows.3 = (f32[256,1024]{1,0:T(8,128)}, bf16[4,256,1024]{2,1,0:T(8,128)(2,1)}) custom-call(s32[3]{0:T(128)} %pad_add_fusion.1.place_ref, s32[4,256,4]{2,1,0:T(8,128)} %copy.14.inv_ref, f32[4,96,1024]{2,1,0:T(8,128)} %get-tuple-element.26.keep0, f32[4,96,1024]{2,1,0:T(8,128)} %get-tuple-element.27.keep1, bf16[4,96,1024]{2,1,0:T(8,128)(2,1)} %copy-done.7, ...), custom_call_target="tpu_custom_call" | custom-call | flops 1610612736 | bytes 9699328 | tf_op jit(solution)/shard_map/merge_rows/pallas_call | solution.py:146
  217.1 3.6 %all-to-all-start.3 = ((bf16[4,256,1024]{2,1,0:T(8,128)(2,1)}), bf16[4,256,1024]{2,1,0:T(8,128)(2,1)S(1)}, u32[]{:S(2)}, u32[]{:S(2)}) async-start(bf16[4,256,1024]{2,1,0:T(8,128)(2,1)} %get-tuple-element.32), calls=%async_computation.3 | async-start | bytes 4194304 | tf_op jit(solution)/shard_map/all_to_all | solution.py:291
  220.7 12.8 %tile_products.4 = (f32[4,96,1024]{2,1,0:T(8,128)}, bf16[4,96,1024]{2,1,0:T(8,128)(2,1)}) custom-call(s32[3]{0:T(128)} %pad_add_fusion.1.place_ref, bf16[768,1024]{1,0:T(8,128)(2,1)} %bitcast.55, bf16[768,1024]{1,0:T(8,128)(2,1)} %collective-permute-done.refs_1_, bf16[768,1024]{1,0:T(8,128)(2,1)} %collective-permute-done.1.refs_2_, ...), custom_call_target="tpu_custom_call" | custom-call | flops 6442450944 | bytes 17825792 | tf_op jit(solution)/shard_map/tile_products/pallas_call | solution.py:94
  233.4 1.6 collective-permute-start.6
  235.0 12.7 %tile_products.5 = (f32[4,96,1024]{2,1,0:T(8,128)}, bf16[4,96,1024]{2,1,0:T(8,128)(2,1)}) custom-call(s32[3]{0:T(128)} %pad_add_fusion.1.place_ref, bf16[768,1024]{1,0:T(8,128)(2,1)} %bitcast.59, bf16[768,1024]{1,0:T(8,128)(2,1)} %collective-permute-done.3.refs_1_, bf16[768,1024]{1,0:T(8,128)(2,1)} %collective-permute-done.4.refs_2_, ...), custom_call_target="tpu_custom_call" | custom-call | flops 6442450944 | bytes 17825792 | tf_op jit(solution)/shard_map/tile_products/pallas_call | solution.py:94
  248.2 4.8 %collective-permute-done.6.got0 = bf16[4,96,1024]{2,1,0:T(8,128)(2,1)S(1)} collective-permute-done((bf16[4,96,1024]{2,1,0:T(8,128)(2,1)}, bf16[4,96,1024]{2,1,0:T(8,128)(2,1)S(1)}, u32[]{:S(2)}, u32[]{:S(2)}) %collective-permute-start.6) | collective-permute-done | bytes 786464 | tf_op jit(solution)/shard_map/ppermute | solution.py:282
  253.0 13.4 %collective-permute-done.7.got1 = bf16[4,96,1024]{2,1,0:T(8,128)(2,1)S(1)} collective-permute-done((bf16[4,96,1024]{2,1,0:T(8,128)(2,1)}, bf16[4,96,1024]{2,1,0:T(8,128)(2,1)S(1)}, u32[]{:S(2)}, u32[]{:S(2)}) %collective-permute-start.7) | collective-permute-done | bytes 786464 | tf_op jit(solution)/shard_map/ppermute | solution.py:282
  267.4 11.1 %merge_rows.2 = (f32[256,1024]{1,0:T(8,128)}, bf16[4,256,1024]{2,1,0:T(8,128)(2,1)}) custom-call(s32[3]{0:T(128)} %pad_add_fusion.1.place_ref, s32[4,256,4]{2,1,0:T(8,128)} %copy.14.inv_ref, f32[4,96,1024]{2,1,0:T(8,128)} %get-tuple-element.20.keep0, f32[4,96,1024]{2,1,0:T(8,128)} %get-tuple-element.22.keep1, bf16[4,96,1024]{2,1,0:T(8,128)(2,1)} %copy-done.9, ...), custom_call_target="tpu_custom_call" | custom-call | flops 1610612736 | bytes 9699328 | tf_op jit(solution)/shard_map/merge_rows/pallas_call | solution.py:146
  279.7 4.8 %all-to-all-start.2 = ((bf16[4,256,1024]{2,1,0:T(8,128)(2,1)}), bf16[4,256,1024]{2,1,0:T(8,128)(2,1)}, u32[]{:S(2)}, u32[]{:S(2)}) async-start(bf16[4,256,1024]{2,1,0:T(8,128)(2,1)} %get-tuple-element.31), calls=%async_computation.2 | async-start | bytes 4194304 | tf_op jit(solution)/shard_map/all_to_all | solution.py:291
  286.3 43.4 %all-to-all-done.2.refs_2_ = bf16[4,256,1024]{2,1,0:T(8,128)(2,1)} async-done(((bf16[4,256,1024]{2,1,0:T(8,128)(2,1)}), bf16[4,256,1024]{2,1,0:T(8,128)(2,1)}, u32[]{:S(2)}, u32[]{:S(2)}) %all-to-all-start.2) | async-done | bytes 2097184 | tf_op jit(solution)/shard_map/all_to_all | solution.py:291
  329.8 8.4 %finish_rows.1 = f32[256,2048]{1,0:T(8,128)} custom-call(s32[3]{0:T(128)} %pad_add_fusion.1.place_ref, f32[256,1024]{1,0:T(8,128)} %get-tuple-element.25.refs_0_, f32[256,1024]{1,0:T(8,128)} %get-tuple-element.30.refs_1_, bf16[4,256,1024]{2,1,0:T(8,128)(2,1)} %all-to-all-done.2.refs_2_, bf16[4,256,1024]{2,1,0:T(8,128)(2,1)} %copy-done.3, ...), custom_call_target="tpu_custom_call" | custom-call | flops 20971520 | bytes 10485760 | tf_op jit(solution)/shard_map/finish_rows/pallas_call | solution.py:186
  (64 shorter events, 16.1 us)
Async XLA Ops:
  0.0 284.5 %copy-start = (f32[2,64]{1,0:T(2,128)S(1)}, f32[2,64]{1,0:T(2,128)}, u32[]{:S(2)}) copy-start(f32[2,64]{1,0:T(2,128)} %param.15) | copy-start | bytes 1540
  9.9 7.4 %copy-start.4 = (s32[256,3]{0,1:T(4,128)S(1)}, s32[256,3]{0,1:T(4,128)}, u32[]{:S(2)}) copy-start(s32[256,3]{0,1:T(4,128)} %param.9) | copy-start | bytes 9220
  9.9 44.4 %all-to-all-start = ((bf16[8,96,1024]{2,1,0:T(8,128)(2,1)}), bf16[8,96,1024]{2,1,0:T(8,128)(2,1)S(1)}, u32[]{:S(2)}, u32[]{:S(2)}) async-start(bf16[8,96,1024]{2,1,0:T(8,128)(2,1)} %bitcast.61), calls=%async_computation | async-start | bytes 3145728 | tf_op jit(solution)/shard_map/all_to_all | solution.py:253
  54.3 42.3 %copy-start.1 = (bf16[8,96,1024]{2,1,0:T(8,128)(2,1)}, bf16[8,96,1024]{2,1,0:T(8,128)(2,1)S(1)}, u32[]{:S(2)}) copy-start(bf16[8,96,1024]{2,1,0:T(8,128)(2,1)S(1)} %all-to-all-done) | copy-start | bytes 4718596
  54.3 40.8 %all-to-all-start.1 = ((bf16[8,96,1024]{2,1,0:T(8,128)(2,1)}), bf16[8,96,1024]{2,1,0:T(8,128)(2,1)S(1)}, u32[]{:S(2)}, u32[]{:S(2)}) async-start(bf16[8,96,1024]{2,1,0:T(8,128)(2,1)} %bitcast.60), calls=%async_computation.1 | async-start | bytes 3145728 | tf_op jit(solution)/shard_map/all_to_all | solution.py:253
  57.9 38.7 %collective-permute-start.1 = (bf16[768,1024]{1,0:T(8,128)(2,1)S(1)}, bf16[768,1024]{1,0:T(8,128)(2,1)}, u32[]{:S(2)}, u32[]{:S(2)}) collective-permute-start(bf16[768,1024]{1,0:T(8,128)(2,1)S(1)} %bitcast.52), channel_id=1, source_target_pairs={{0,2},{1,3},{2,0},{3,1},{4,6},{5,7},{6,4},{7,5},{8,10},{9,11},{10,... | collective-permute-start | bytes 4718600 | tf_op jit(solution)/shard_map/ppermute | solution.py:261
  95.1 79.3 %copy-start.2 = (bf16[8,96,1024]{2,1,0:T(8,128)(2,1)}, bf16[8,96,1024]{2,1,0:T(8,128)(2,1)S(1)}, u32[]{:S(2)}) copy-start(bf16[8,96,1024]{2,1,0:T(8,128)(2,1)S(1)} %all-to-all-done.1) | copy-start | bytes 4718596
  95.1 35.3 %collective-permute-start.4 = (bf16[768,1024]{1,0:T(8,128)(2,1)S(1)}, bf16[768,1024]{1,0:T(8,128)(2,1)}, u32[]{:S(2)}, u32[]{:S(2)}) collective-permute-start(bf16[768,1024]{1,0:T(8,128)(2,1)S(1)} %bitcast.56), channel_id=1, source_target_pairs={{0,2},{1,3},{2,0},{3,1},{4,6},{5,7},{6,4},{7,5},{8,10},{9,11},{10,... | collective-permute-start | bytes 4718600 | tf_op jit(solution)/shard_map/ppermute | solution.py:261
  96.6 65.0 %collective-permute-start = (bf16[768,1024]{1,0:T(8,128)(2,1)S(1)}, bf16[768,1024]{1,0:T(8,128)(2,1)}, u32[]{:S(2)}, u32[]{:S(2)}) collective-permute-start(bf16[768,1024]{1,0:T(8,128)(2,1)S(1)} %bitcast.53), channel_id=1, source_target_pairs={{0,1},{1,0},{2,3},{3,2},{4,5},{5,4},{6,7},{7,6},{8,9},{9,8},{10,11... | collective-permute-start | bytes 4718600 | tf_op jit(solution)/shard_map/ppermute | solution.py:261
  96.6 65.0 %collective-permute-start.2 = (bf16[768,1024]{1,0:T(8,128)(2,1)}, bf16[768,1024]{1,0:T(8,128)(2,1)}, u32[]{:S(2)}, u32[]{:S(2)}) collective-permute-start(bf16[768,1024]{1,0:T(8,128)(2,1)} %collective-permute-done.1.refs_2_), channel_id=1, source_target_pairs={{0,1},{1,0},{2,3},{3,2},{4,5},{5,4},{6,7},{7,6},{8,9},{9,8},{10,11... | collective-permute-start | bytes 4718600 | tf_op jit(solution)/shard_map/ppermute | solution.py:261
  97.2 77.9 %collective-permute-start.3 = (bf16[768,1024]{1,0:T(8,128)(2,1)S(1)}, bf16[768,1024]{1,0:T(8,128)(2,1)}, u32[]{:S(2)}, u32[]{:S(2)}) collective-permute-start(bf16[768,1024]{1,0:T(8,128)(2,1)S(1)} %bitcast.57), channel_id=1, source_target_pairs={{0,1},{1,0},{2,3},{3,2},{4,5},{5,4},{6,7},{7,6},{8,9},{9,8},{10,11... | collective-permute-start | bytes 4718600 | tf_op jit(solution)/shard_map/ppermute | solution.py:261
  130.4 44.7 %collective-permute-start.5 = (bf16[768,1024]{1,0:T(8,128)(2,1)}, bf16[768,1024]{1,0:T(8,128)(2,1)}, u32[]{:S(2)}, u32[]{:S(2)}) collective-permute-start(bf16[768,1024]{1,0:T(8,128)(2,1)} %collective-permute-done.4.refs_2_), channel_id=1, source_target_pairs={{0,1},{1,0},{2,3},{3,2},{4,5},{5,4},{6,7},{7,6},{8,9},{9,8},{10,11... | collective-permute-start | bytes 4718600 | tf_op jit(solution)/shard_map/ppermute | solution.py:261
  174.4 17.4 %collective-permute-start.8 = (bf16[4,96,1024]{2,1,0:T(8,128)(2,1)}, bf16[4,96,1024]{2,1,0:T(8,128)(2,1)S(1)}, u32[]{:S(2)}, u32[]{:S(2)}) collective-permute-start(bf16[4,96,1024]{2,1,0:T(8,128)(2,1)} %get-tuple-element.28), channel_id=1, source_target_pairs={{0,4},{4,0},{8,12},{12,8},{16,20},{20,16},{24,28},{28,24},{1,5},{5... | collective-permute-start | bytes 2359304 | tf_op jit(solution)/shard_map/ppermute | solution.py:282
  187.9 17.2 %collective-permute-start.9 = (bf16[4,96,1024]{2,1,0:T(8,128)(2,1)}, bf16[4,96,1024]{2,1,0:T(8,128)(2,1)S(1)}, u32[]{:S(2)}, u32[]{:S(2)}) collective-permute-start(bf16[4,96,1024]{2,1,0:T(8,128)(2,1)} %get-tuple-element.29), channel_id=1, source_target_pairs={{0,4},{4,0},{8,12},{12,8},{16,20},{20,16},{24,28},{28,24},{1,5},{5... | collective-permute-start | bytes 2359304 | tf_op jit(solution)/shard_map/ppermute | solution.py:282
  191.9 13.2 %copy-start.7 = (bf16[4,96,1024]{2,1,0:T(8,128)(2,1)}, bf16[4,96,1024]{2,1,0:T(8,128)(2,1)S(1)}, u32[]{:S(2)}) copy-start(bf16[4,96,1024]{2,1,0:T(8,128)(2,1)S(1)} %collective-permute-done.8.got0) | copy-start | bytes 2359300
  217.1 61.3 %all-to-all-start.3 = ((bf16[4,256,1024]{2,1,0:T(8,128)(2,1)}), bf16[4,256,1024]{2,1,0:T(8,128)(2,1)S(1)}, u32[]{:S(2)}, u32[]{:S(2)}) async-start(bf16[4,256,1024]{2,1,0:T(8,128)(2,1)} %get-tuple-element.32), calls=%async_computation.3 | async-start | bytes 4194304 | tf_op jit(solution)/shard_map/all_to_all | solution.py:291
  233.4 19.5 %collective-permute-start.6 = (bf16[4,96,1024]{2,1,0:T(8,128)(2,1)}, bf16[4,96,1024]{2,1,0:T(8,128)(2,1)S(1)}, u32[]{:S(2)}, u32[]{:S(2)}) collective-permute-start(bf16[4,96,1024]{2,1,0:T(8,128)(2,1)} %get-tuple-element.23), channel_id=1, source_target_pairs={{0,4},{4,0},{8,12},{12,8},{16,20},{20,16},{24,28},{28,24},{1,5},{5... | collective-permute-start | bytes 2359304 | tf_op jit(solution)/shard_map/ppermute | solution.py:282
  247.7 18.7 %collective-permute-start.7 = (bf16[4,96,1024]{2,1,0:T(8,128)(2,1)}, bf16[4,96,1024]{2,1,0:T(8,128)(2,1)S(1)}, u32[]{:S(2)}, u32[]{:S(2)}) collective-permute-start(bf16[4,96,1024]{2,1,0:T(8,128)(2,1)} %get-tuple-element.24), channel_id=1, source_target_pairs={{0,4},{4,0},{8,12},{12,8},{16,20},{20,16},{24,28},{28,24},{1,5},{5... | collective-permute-start | bytes 2359304 | tf_op jit(solution)/shard_map/ppermute | solution.py:282
  253.0 13.5 %copy-start.9 = (bf16[4,96,1024]{2,1,0:T(8,128)(2,1)}, bf16[4,96,1024]{2,1,0:T(8,128)(2,1)S(1)}, u32[]{:S(2)}) copy-start(bf16[4,96,1024]{2,1,0:T(8,128)(2,1)S(1)} %collective-permute-done.6.got0) | copy-start | bytes 2359300
  278.4 1.3 copy-start.3
  278.4 6.1 %copy-start.6 = (f32[2,64]{1,0:T(2,128)S(1)}, f32[2,64]{1,0:T(2,128)}, u32[]{:S(2)}) copy-start(f32[2,64]{1,0:T(2,128)} %param.14) | copy-start | bytes 1540
  278.4 7.0 %copy-start.11 = (f32[32]{0:T(128)S(1)}, f32[32]{0:T(128)}, u32[]{:S(2)}) copy-start(f32[32]{0:T(128)} %param.12) | copy-start | bytes 388
  278.4 7.0 %copy-start.5 = (f32[64]{0:T(128)S(1)}, f32[64]{0:T(128)}, u32[]{:S(2)}) copy-start(f32[64]{0:T(128)} %param.13) | copy-start | bytes 772
  279.7 50.0 %all-to-all-start.2 = ((bf16[4,256,1024]{2,1,0:T(8,128)(2,1)}), bf16[4,256,1024]{2,1,0:T(8,128)(2,1)}, u32[]{:S(2)}, u32[]{:S(2)}) async-start(bf16[4,256,1024]{2,1,0:T(8,128)(2,1)} %get-tuple-element.31), calls=%async_computation.2 | async-start | bytes 4194304 | tf_op jit(solution)/shard_map/all_to_all | solution.py:291
  (2 other events, 1.8 us)

commit v2 on v1

v2 whole, which is shorter than its diff:
```python
import functools

import jax
import jax.numpy as jnp
from jax import lax
from jax.experimental import pallas as pl
from jax.experimental.pallas import tpu as pltpu
from jax.sharding import PartitionSpec as P

VMEM_LIMIT = 40 * 1024 * 1024
F32 = jnp.float32
BF16 = jnp.bfloat16
PARTS = (1, 2)
CHUNKS = (2, 3, 3)


def params():
    return pltpu.CompilerParams(vmem_limit_bytes=VMEM_LIMIT)


def cost(flops, nbytes):
    return pl.CostEstimate(flops=int(flops), bytes_accessed=int(nbytes), transcendentals=0)


def encode(v):
    w = v * 8.0
    sq = w * w
    quad = sq * sq
    return ((w * jnp.abs(w)) * (quad * sq)).astype(BF16)


def decode(code):
    c = code.astype(F32)
    a = jnp.abs(c)
    t = lax.rsqrt(jnp.maximum(a, 1e-37))
    u = lax.rsqrt(t)
    root = u * lax.rsqrt(u) * 0.125
    root = jnp.where(a < 1e-37, 0.0, root)
    return jnp.where(c < 0.0, -root, root)


def after(x, *earlier):
    earlier = [y for y in earlier if y is not None]
    return lax.optimization_barrier((x, *earlier))[0] if earlier else x


def pack_kernel(parts, codes_ref, tiles_ref, *outs):
    block = outs[0].shape[0]
    top, rows, _ = tiles_ref.shape
    want = lax.broadcasted_iota(jnp.int32, (block, rows), 0) + pl.program_id(0) * block
    for c in range(codes_ref.shape[0]):
        total = None
        for k in range(top):
            pick = (want == codes_ref[c, k : k + 1, :]).astype(F32).astype(BF16)
            part = jnp.dot(pick, tiles_ref[k], preferred_element_type=F32)
            total = part if total is None else total + part
        for out, (of, first, size) in zip(outs, parts):
            if of == c:
                out[...] = total[:, first : first + size].astype(BF16)


def pack(codes, tiles, n_slots, parts):
    top, rows, width = tiles.shape
    steps = 4
    return pl.pallas_call(
        functools.partial(pack_kernel, parts),
        grid=(steps,),
        in_specs=[
            pl.BlockSpec(codes.shape, lambda i: (0, 0, 0)),
            pl.BlockSpec((top, rows, width), lambda i: (0, 0, 0)),
        ],
        out_specs=[pl.BlockSpec((n_slots // steps, size), lambda i: (i, 0)) for _, _, size in parts],
        out_shape=[jax.ShapeDtypeStruct((n_slots, size), BF16) for _, _, size in parts],
        compiler_params=params(),
        cost_estimate=cost(4 * n_slots * top * rows * width, 8 * n_slots * width),
        name="pack_tiles",
    )(codes, tiles)


def product_kernel(offsets, place_ref, *refs):
    *parts, w_ref, keep_ref, send_ref, lhs_ref = refs
    half, cap, step = keep_ref.shape

    @pl.when(pl.program_id(0) == 0)
    def _():
        for part, (rel, stride, offset) in zip(parts, offsets):
            start = lax.bitwise_xor(place_ref[0], rel) * stride + offset
            size = part.shape[1]
            lhs_ref[:, pl.ds(pl.multiple_of(start, size), size)] = part[...]

    total = jnp.dot(lhs_ref[...], w_ref[0], preferred_element_type=F32)
    total = total.reshape(2 * half, cap, step)
    for g in range(half):
        first, second = total[2 * g], total[2 * g + 1]
        keep_ref[g] = jnp.where(place_ref[1] == 0, first, second)
        send_ref[g] = encode(jnp.where(place_ref[1] == 0, second, first))


def product(place, pieces, integrals, c, first, cols, cap, step):
    lhs = [piece for piece, _ in pieces]
    offsets = tuple(offset for _, offset in pieces)
    slots = lhs[0].shape[0]
    width = integrals.shape[1]
    half = slots // cap // 2
    base = first // step
    return pl.pallas_call(
        functools.partial(product_kernel, offsets),
        grid_spec=pltpu.PrefetchScalarGridSpec(
            num_scalar_prefetch=1,
            grid=(cols // step,),
            in_specs=[pl.BlockSpec(x.shape, lambda j, s: (0, 0)) for x in lhs]
            + [pl.BlockSpec((1, width, step), lambda j, s: (c, 0, base + j))],
            out_specs=[pl.BlockSpec((half, cap, step), lambda j, s: (0, 0, j))] * 2,
            scratch_shapes=[pltpu.VMEM((slots, width), BF16)],
        ),
        out_shape=[
            jax.ShapeDtypeStruct((half, cap, cols), F32),
            jax.ShapeDtypeStruct((half, cap, cols), BF16),
        ],
        compiler_params=params(),
        cost_estimate=cost(2 * slots * width * cols, 2 * width * cols + 2 * slots * width + 4 * slots * cols),
        name="tile_products",
    )(place, *lhs, integrals)


def dense_rows(inv_ref, values):
    rows = inv_ref.shape[1]
    slots = values.shape[0]
    cap = slots // 4
    lane = lax.broadcasted_iota(jnp.int32, (rows, slots), 1)
    hit = None
    for c in range(4):
        slot = inv_ref[0, :, c : c + 1]
        one = lane == jnp.where(slot < 0, -1, slot + c * cap)
        hit = one if hit is None else hit | one
    pick = hit.astype(F32).astype(BF16)
    high = values.astype(BF16)
    low = (values - high.astype(F32)).astype(BF16)
    dense = jnp.dot(pick, high, preferred_element_type=F32)
    return dense + jnp.dot(pick, low, preferred_element_type=F32)


def merge_kernel(place_ref, inv_ref, keep0, keep1, got0, got1, kept_ref, send_ref):
    values = [keep0[0], keep1[0], decode(got0[0]), decode(got1[0])]
    dense = dense_rows(inv_ref, jnp.concatenate(values, axis=0))

    @pl.when(pl.program_id(1) % 2 == 0)
    def _():
        kept_ref[0] = dense

    @pl.when(pl.program_id(1) % 2 == 1)
    def _():
        send_ref[0] = encode(dense)


def merge(place, inv, keep, got):
    groups, cap, cols = keep[0].shape
    rows = inv.shape[1]
    step = cols
    spec = pl.BlockSpec((1, cap, step), lambda j, r, s: (s[2] ^ r, 0, j))
    half = pl.BlockSpec((1, rows, step), lambda j, r, s: (r // 2, 0, j))
    shape = (groups // 2, rows, cols)
    return pl.pallas_call(
        merge_kernel,
        grid_spec=pltpu.PrefetchScalarGridSpec(
            num_scalar_prefetch=1,
            grid=(cols // step, groups),
            in_specs=[pl.BlockSpec((1, rows, 4), lambda j, r, s: (s[2] ^ r, 0, 0))] + [spec] * 4,
            out_specs=[half, half],
        ),
        out_shape=[jax.ShapeDtypeStruct(shape, F32), jax.ShapeDtypeStruct(shape, BF16)],
        compiler_params=params(),
        cost_estimate=cost(16 * groups * rows * cap * cols, 14 * groups * cap * cols + 4 * groups * rows * cols),
        name="merge_rows",
    )(place, inv, *keep, *got)


def halve_kernel(place_ref, kept_ref, got_ref, out_ref, send_ref):
    out_ref[0] = kept_ref[0] + decode(got_ref[0])
    send_ref[0] = encode(kept_ref[1] + decode(got_ref[1]))


def halve(place, kept, got):
    count, rows, cols = kept.shape
    step = rows // 2
    two = pl.BlockSpec((2, step, cols), lambda i, r, s: (i, r, 0))
    one = pl.BlockSpec((1, step, cols), lambda i, r, s: (i, r, 0))
    shape = (count // 2, rows, cols)
    return pl.pallas_call(
        halve_kernel,
        grid_spec=pltpu.PrefetchScalarGridSpec(
            num_scalar_prefetch=1,
            grid=(count // 2, rows // step),
            in_specs=[two, two],
            out_specs=[one, one],
        ),
        out_shape=[jax.ShapeDtypeStruct(shape, F32), jax.ShapeDtypeStruct(shape, BF16)],
        compiler_params=params(),
        cost_estimate=cost(30 * count * rows * cols, 9 * count * rows * cols),
        name="halve_rows",
    )(place, kept, got)


def finish_kernel(place_ref, own_ref, got_ref, other_ref, occ_ref, virt_ref, *refs):
    total = own_ref[0] + decode(got_ref[0])
    denom = occ_ref[...] - virt_ref[...]
    refs[-1][...] = (0.5 * total + other_ref[...]) / denom


def finish(place, own, got, other, occ_sum, virt_sum, first, step, out):
    rows, width = other.shape
    cols = own.shape[2]
    base = first // step
    here = pl.BlockSpec((1, rows, step), lambda j, s: (0, 0, j))
    there = pl.BlockSpec((rows, step), lambda j, s: (0, base + j))
    earlier = [] if out is None else [out]
    return pl.pallas_call(
        finish_kernel,
        grid_spec=pltpu.PrefetchScalarGridSpec(
            num_scalar_prefetch=1,
            grid=(cols // step,),
            in_specs=[
                here,
                here,
                there,
                pl.BlockSpec((rows, 1), lambda j, s: (0, 0)),
                pl.BlockSpec((1, step), lambda j, s: (0, base + j)),
            ]
            + [pl.BlockSpec(memory_space=pl.ANY)] * len(earlier),
            out_specs=there,
        ),
        out_shape=jax.ShapeDtypeStruct((rows, width), F32),
        input_output_aliases={6: 0} if earlier else {},
        compiler_params=params(),
        cost_estimate=cost(40 * rows * cols, 14 * rows * cols),
        name="finish_rows",
    )(place, own, got, other, occ_sum, virt_sum, *earlier)


def ranks(named, experts):
    blocks, top, rows = named.shape
    flat = named.reshape(blocks, top * rows)
    onehot = flat[:, :, None] == jnp.arange(experts, dtype=jnp.int32)
    before = jnp.tri(top * rows, k=-1, dtype=BF16)
    count = jnp.einsum("ij,bje->bie", before, onehot.astype(BF16), preferred_element_type=F32)
    shape = (blocks, top, rows, experts)
    return onehot.reshape(shape), count.astype(jnp.int32).reshape(shape)


def per_device(
    amplitudes, screen, integrals, other, occ_first, occ_second, virt_first, virt_second
):
    rows, top, width = amplitudes.shape
    n_pair = lax.axis_size("pair")
    n_virt = lax.axis_size("virt")
    cd_dev, _, cols = integrals.shape
    experts = cd_dev * n_pair
    cap = rows * top * 2 // experts
    quarter = width // n_virt
    pair = lax.axis_index("pair")
    virt = lax.axis_index("virt")
    low, high = pair % 2, pair // 2
    groups = n_pair // 2
    place = jnp.stack([virt, low, high]).astype(jnp.int32)

    named = screen.T[None]
    onehot, rank = ranks(named, experts)
    slot = jnp.sum(jnp.where(onehot, rank, 0), axis=3)[0]
    expert = named[0]
    where = expert // cd_dev * cap + slot
    tiles = lax.dynamic_slice_in_dim(amplitudes, virt * quarter, quarter, 2)
    tiles = tiles.transpose(1, 0, 2)

    every = [screen.T]
    for k in range(1, groups):
        around = [(i, (i + 2 * k) % n_pair) for i in range(n_pair)]
        every.append(lax.ppermute(every[0], "pair", around))

    swap_low = [(i, i ^ 1) for i in range(n_pair)]

    parts = []
    for c in range(cd_dev):
        size = quarter // PARTS[c]
        parts += [(c, first, size) for first in range(0, quarter, size)]
    codes = jnp.stack([jnp.where(expert % cd_dev == c, where, -1) for c in range(cd_dev)])
    arrived = []
    for x in pack(codes, tiles, n_pair * cap, parts):
        arrived.append(lax.all_to_all(after(x, *arrived[-1:]), "pair", 0, 0, tiled=True))

    owners = jnp.roll(jnp.stack(every[::-1]), high + 1, axis=0)
    all_hot, all_rank = ranks(owners, experts)
    inv = jnp.sum(jnp.where(all_hot, all_rank + 1, 0), axis=1) - 1
    mine = lax.dynamic_slice_in_dim(inv, pair * cd_dev, cd_dev, 2)
    theirs = lax.dynamic_slice_in_dim(inv, (pair + 1 - 2 * low) * cd_dev, cd_dev, 2)
    inv = jnp.concatenate([mine, theirs], axis=2)

    def share(x, *waits):
        held = {0: x}
        bit = n_virt // 2
        while bit:
            swap = [(i, i ^ bit) for i in range(n_virt)]
            if bit == 1:
                held = {at: after(x, *waits) if at else x for at, x in held.items()}
            held.update({at | bit: lax.ppermute(x, "virt", swap) for at, x in held.items()})
            bit //= 2
        return held

    def share(x, *waits):
        held = {0: x}
        bit = n_virt // 2
        while bit:
            swap = [(i, i ^ bit) for i in range(n_virt)]
            if bit == 1:
                held = {at: after(x, *waits) if at else x for at, x in held.items()}
            held.update({at | bit: lax.ppermute(x, "virt", swap) for at, x in held.items()})
            bit //= 2
        return held

    def hop(x, bit):
        return lax.ppermute(x, "pair", [(i, i ^ bit) for i in range(n_pair)])

    unit = cols // sum(CHUNKS)
    spans = [(unit * sum(CHUNKS[:j]), unit * size) for j, size in enumerate(CHUNKS)]
    keep, got = [[] for _ in spans], [[] for _ in spans]
    count = len(spans)
    made, moved = [], []

    def make(c, j, pieces, *waits):
        first, size = spans[j]
        waits = [*made[-1:], *moved[-2:-1], *waits]
        kept, sent = product(after(place, *waits), pieces, integrals, c, first, size, cap, unit)
        made.append(kept)
        moved.append(hop(sent, 1))
        keep[j].append(kept)
        got[j].append(moved[-1])

    pieces = [[], []]
    for n, ((c, first, _), x) in enumerate(zip(parts, arrived)):
        held = share(x, *(made[-1:] if n + 1 == len(parts) else []))
        pieces[c] += [(y, (at, quarter, first)) for at, y in held.items()]
        if n == 0:
            for j in range(count):
                make(0, j, pieces[0], arrived[1 if j + 1 < count else -1])
    computed = made[-1]

    levels = groups.bit_length() - 1
    state = {}

    def advance(j, level, *waits):
        if level == 0:
            kept, sent = merge(after(place, *waits), inv, keep[j], got[j])
        else:
            kept, sent = halve(after(place, *waits), *state[j])
        state[j] = (kept, hop(sent, 2 << level))
        return kept

    make(1, 0, pieces[1], computed)
    computed = made[-1]
    for turn in range(count + levels):
        if turn + 1 < count:
            make(1, turn + 1, pieces[1], computed)
            computed = made[-1]
        for level in range(levels):
            j = turn - level
            if 0 <= j < count:
                computed = advance(j, level, computed)

    tile = virt_first.shape[1]
    tile_sq = tile * tile
    start_col = virt * cols
    tile_pair = start_col // tile_sq
    first_a = start_col % tile_sq // tile
    energy_a = lax.dynamic_slice(virt_first, (tile_pair, first_a), (1, cols // tile)).reshape(-1)
    energy_b = lax.dynamic_slice_in_dim(virt_second, tile_pair, 1, 0).reshape(-1)
    virt_sum = (energy_a[:, None] + energy_b[None, :]).reshape(1, cols)
    per_i = occ_second.shape[0]
    energy_i = lax.dynamic_slice_in_dim(occ_first, pair * (rows // per_i), rows // per_i, 0)
    occ_sum = (energy_i[:, None] + occ_second[None, :]).reshape(rows, 1)
    out = None
    for j, (first, _) in enumerate(spans):
        out = finish(place, *state[j], other, occ_sum, virt_sum, first, unit, out)
    return out


def solution(mesh):
    return jax.shard_map(
        per_device,
        mesh=mesh,
        in_specs=(
            P("pair", None, None),
            P("pair", None),
            P("pair", None, "virt"),
            P("pair", "virt"),
            P(),
            P(),
            P(),
            P(),
        ),
        out_specs=P("pair", "virt"),
        check_vma=False,
    )
```

time: 339 us -> 275 us (0.81)
  waiting for transfers between devices: 176 us -> 98.5 us
  blocking collectives: 30.5 us -> 44 us
    all_to_all x4 -> x2, waiting for transfers between devices: 111 us -> 0.55 us  [per_device(): lax.all_to_all(after(x, *arrived[-1:]), 'pair', 0, 0, tiled=True)]
    all_to_all x0 -> x1, blocking collectives: none -> 44 us  [per_device(): lax.all_to_all(after(x, *arrived[-1:]), 'pair', 0, 0, tiled=True)]
    ppermute x10 -> x24, waiting for transfers between devices: 65.2 us -> 98 us  [the longest x12 55.2 us: hop(): return lax.ppermute(x, 'pair', [(i, i ^ bit) for i in range(n_pair)])]
    all_gather x1 -> x0, blocking collectives: 30.5 us -> none  [per_device(): every = lax.all_gather(screen, 'pair')]
    ppermute x10 -> x24, starting transfers between devices: 7.73 us -> 21.7 us  [the longest x12 11.8 us: hop(): return lax.ppermute(x, 'pair', [(i, i ^ bit) for i in range(n_pair)])]
    all_to_all x4 -> x2, starting transfers between devices: 19.4 us -> 8.64 us  [per_device(): lax.all_to_all(after(x, *arrived[-1:]), 'pair', 0, 0, tiled=True)]
    pallas_call x2 -> x3, Pallas kernels: 22.1 us -> 16.6 us  [merge(): pl.pallas_call(merge_kernel, grid_spec=pltpu.PrefetchScalarGridSpec(num_s...]
    unnamed x25 -> x63, local copies, waits for them, and re-layouts: 3.13 us -> 7.81 us
  transfers between devices with their start and end apart: 14 -> 26, of which waited for: 8 -> 11; matrix products, arithmetic and copies ran while one was open for 1% -> 1% of each run, Pallas kernels for 20% -> 30%
where the time goes in v2:
time: 275 us; the launch traced here: 274 us
  waiting for transfers between devices  98.5 us (36%)
  Pallas kernels  87.1 us (32%)
  blocking collectives  44 us (16%)
  starting transfers between devices  30.3 us (11%)
  local copies, waits for them, and re-layouts  10.8 us (4%)
    ppermute x12, waiting for transfers between devices, hop(): return lax.ppermute(x, 'pair', [(i, i ^ bit) for i in range(n_pair)])  55.2 us
    pallas_call x6, Pallas kernels, product(): pl.pallas_call(functools.partial(product_kernel, offsets), grid_spec=pltp...  54 us
    all_to_all x1, blocking collectives, per_device(): lax.all_to_all(after(x, *arrived[-1:]), 'pair', 0, 0, tiled=True)  44 us
    ppermute x9, waiting for transfers between devices, share(): lax.ppermute(x, 'virt', swap)  35.7 us
    pallas_call x3, Pallas kernels, merge(): pl.pallas_call(merge_kernel, grid_spec=pltpu.PrefetchScalarGridSpec(num_s...  16.6 us
    ppermute x12, starting transfers between devices, hop(): return lax.ppermute(x, 'pair', [(i, i ^ bit) for i in range(n_pair)])  11.8 us
    all_to_all x2, starting transfers between devices, per_device(): lax.all_to_all(after(x, *arrived[-1:]), 'pair', 0, 0, tiled=True)  8.64 us
    unnamed x63, local copies, waits for them, and re-layouts  7.81 us
  transfers between devices with their start and end apart: 26, of which 11 were waited for; matrix products, arithmetic and copies ran while one was open for 1% of the time, Pallas kernels for 30%

profile of v2, /device:TPU:0, one launch (start us, length us, event | category | flops | bytes accessed | tf_op | source)
XLA Modules:
  0.0 274.5 jit_solution(5481933738675368053)
XLA Ops:
  4.5 3.2 %pack_tiles.1 = (bf16[768,1024]{1,0:T(8,128)(2,1)S(1)}, bf16[768,512]{1,0:T(8,128)(2,1)S(1)}, bf16[768,512]{1,0:T(8,128)(2,1)S(1)}) custom-call(s32[2,3,256]{2,1,0:T(4,128)S(1)} %pad_add_fusion.1.codes_ref, bf16[3,256,1024]{2,1,0:T(8,128)(2,1)S(1)} %dynamic-slice_bitcast_fusion.tiles_ref), custom_call_target="tpu_custom_call" | custom-call | flops 2415919104 | bytes 6291456 | tf_op jit(solution)/shard_map/pack_tiles/pallas_call | solution.py:65
  7.7 44.0 %all_to_all.33 = bf16[8,96,1024]{2,1,0:T(8,128)(2,1)S(1)} all-to-all(bf16[8,96,1024]{2,1,0:T(8,128)(2,1)S(1)} %bitcast.69), channel_id=1, replica_groups=mesh['pair'=8,'virt'=4] {'pair'}, dimensions={0} | all-to-all | bytes 3145728 | tf_op jit(solution)/shard_map/all_to_all | solution.py:288
  53.4 4.2 %all-to-all-start.1 = ((bf16[8,96,512]{2,1,0:T(8,128)(2,1)}), bf16[8,96,512]{2,1,0:T(8,128)(2,1)}, u32[]{:S(2)}, u32[]{:S(2)}) async-start(bf16[8,96,512]{2,1,0:T(8,128)(2,1)} %bitcast.71), calls=%async_computation.1 | async-start | bytes 1572864 | tf_op jit(solution)/shard_map/all_to_all | solution.py:288
  57.6 3.7 %collective-permute-start.13 = (s32[3,256]{1,0:T(4,128)S(1)}, s32[3,256]{1,0:T(4,128)S(1)}, u32[]{:S(2)}, u32[]{:S(2)}) collective-permute-start(s32[3,256]{1,0:T(4,128)S(1)} %bitcast.73), channel_id=1, source_target_pairs={{0,24},{4,28},{8,0},{12,4},{16,8},{20,12},{24,16},{28,20},{1,25},{... | collective-permute-start | bytes 9224 | tf_op jit(solution)/shard_map/ppermute | solution.py:277
  62.5 7.0 %collective-permute-done.13 = s32[3,256]{1,0:T(4,128)S(1)} collective-permute-done((s32[3,256]{1,0:T(4,128)S(1)}, s32[3,256]{1,0:T(4,128)S(1)}, u32[]{:S(2)}, u32[]{:S(2)}) %collective-permute-start.13) | collective-permute-done | bytes 3104 | tf_op jit(solution)/shard_map/ppermute | solution.py:277
  69.6 17.3 %collective-permute-done.refs_1_ = bf16[768,1024]{1,0:T(8,128)(2,1)S(1)} collective-permute-done((bf16[768,1024]{1,0:T(8,128)(2,1)S(1)}, bf16[768,1024]{1,0:T(8,128)(2,1)S(1)}, u32[]{:S(2)}, u32[]{:S(2)}) %collective-permute-start) | collective-permute-done | bytes 1572896 | tf_op jit(solution)/shard_map/ppermute | solution.py:315
  86.9 4.4 %all-to-all-start.2 = ((bf16[8,96,512]{2,1,0:T(8,128)(2,1)}), bf16[8,96,512]{2,1,0:T(8,128)(2,1)}, u32[]{:S(2)}, u32[]{:S(2)}) async-start(bf16[8,96,512]{2,1,0:T(8,128)(2,1)} %bitcast.70), calls=%async_computation.2 | async-start | bytes 1572864 | tf_op jit(solution)/shard_map/all_to_all | solution.py:288
  93.2 18.4 %collective-permute-done.5.refs_1_ = bf16[768,512]{1,0:T(8,128)(2,1)} collective-permute-done((bf16[768,512]{1,0:T(8,128)(2,1)}, bf16[768,512]{1,0:T(8,128)(2,1)}, u32[]{:S(2)}, u32[]{:S(2)}) %collective-permute-start.5) | collective-permute-done | bytes 786464 | tf_op jit(solution)/shard_map/ppermute | solution.py:315
  113.7 7.2 %tile_products.6 = (f32[4,96,512]{2,1,0:T(8,128)S(1)}, bf16[4,96,512]{2,1,0:T(8,128)(2,1)S(1)}) custom-call(s32[3]{0:T(128)S(1)} %pad_add_fusion.2.place_ref, bf16[768,1024]{1,0:T(8,128)(2,1)S(1)} %bitcast.66, bf16[768,1024]{1,0:T(8,128)(2,1)S(1)} %collective-permute-done.refs_1_, bf16[768,1024]{1,0:T(8,128)(2,1)} %collective-permute-done.1.refs_2_, ...), custom_call_target="tpu_custom_call" | custom-call | flops 3221225472 | bytes 12058624 | tf_op jit(solution)/shard_map/tile_products/pallas_call | solution.py:106
  123.3 9.8 %tile_products.7 = (f32[4,96,768]{2,1,0:T(8,128)S(1)}, bf16[4,96,768]{2,1,0:T(8,128)(2,1)}) custom-call(s32[3]{0:T(128)S(1)} %pad_add_fusion.2.place_ref, bf16[768,1024]{1,0:T(8,128)(2,1)S(1)} %bitcast.67, bf16[768,1024]{1,0:T(8,128)(2,1)S(1)} %collective-permute-done.refs_1_, bf16[768,1024]{1,0:T(8,128)(2,1)} %collective-permute-done.1.refs_2_, ...), custom_call_target="tpu_custom_call" | custom-call | flops 4831838208 | bytes 14942208 | tf_op jit(solution)/shard_map/tile_products/pallas_call | solution.py:106
  134.8 9.1 %tile_products.8 = (f32[4,96,768]{2,1,0:T(8,128)S(1)}, bf16[4,96,768]{2,1,0:T(8,128)(2,1)S(1)}) custom-call(s32[3]{0:T(128)S(1)} %pad_add_fusion.2.place_ref, bf16[768,1024]{1,0:T(8,128)(2,1)S(1)} %bitcast.68, bf16[768,1024]{1,0:T(8,128)(2,1)S(1)} %collective-permute-done.refs_1_, bf16[768,1024]{1,0:T(8,128)(2,1)} %collective-permute-done.1.refs_2_, ...), custom_call_target="tpu_custom_call" | custom-call | flops 4831838208 | bytes 14942208 | tf_op jit(solution)/shard_map/tile_products/pallas_call | solution.py:106
  146.8 3.0 %collective-permute-done.4.got0 = bf16[4,96,768]{2,1,0:T(8,128)(2,1)} collective-permute-done((bf16[4,96,768]{2,1,0:T(8,128)(2,1)}, bf16[4,96,768]{2,1,0:T(8,128)(2,1)}, u32[]{:S(2)}, u32[]{:S(2)}) %collective-permute-start.4) | collective-permute-done | bytes 589856 | tf_op jit(solution)/shard_map/ppermute | solution.py:320
  150.8 8.0 %tile_products.9 = (f32[4,96,512]{2,1,0:T(8,128)S(1)}, bf16[4,96,512]{2,1,0:T(8,128)(2,1)S(1)}) custom-call(s32[3]{0:T(128)S(1)} %pad_add_fusion.2.place_ref, bf16[768,512]{1,0:T(8,128)(2,1)} %bitcast.12.refs_0_, bf16[768,512]{1,0:T(8,128)(2,1)} %collective-permute-done.5.refs_1_, bf16[768,512]{1,0:T(8,128)(2,1)} %collective-permute-done.6.refs_2_, ...), custom_call_target="tpu_custom_call" | custom-call | flops 3221225472 | bytes 12058624 | tf_op jit(solution)/shard_map/tile_products/pallas_call | solution.py:106
  158.8 5.7 %collective-permute-done.11.got0 = bf16[4,96,768]{2,1,0:T(8,128)(2,1)S(1)} collective-permute-done((bf16[4,96,768]{2,1,0:T(8,128)(2,1)S(1)}, bf16[4,96,768]{2,1,0:T(8,128)(2,1)S(1)}, u32[]{:S(2)}, u32[]{:S(2)}) %collective-permute-start.11) | collective-permute-done | bytes 589856 | tf_op jit(solution)/shard_map/ppermute | solution.py:320
  164.9 9.9 %tile_products.10 = (f32[4,96,768]{2,1,0:T(8,128)S(1)}, bf16[4,96,768]{2,1,0:T(8,128)(2,1)S(1)}) custom-call(s32[3]{0:T(128)S(1)} %pad_add_fusion.2.place_ref, bf16[768,512]{1,0:T(8,128)(2,1)} %bitcast.12.refs_0_, bf16[768,512]{1,0:T(8,128)(2,1)} %collective-permute-done.5.refs_1_, bf16[768,512]{1,0:T(8,128)(2,1)} %collective-permute-done.6.refs_2_, ...), custom_call_target="tpu_custom_call" | custom-call | flops 4831838208 | bytes 14942208 | tf_op jit(solution)/shard_map/tile_products/pallas_call | solution.py:106
  176.5 4.1 %merge_rows.3 = (f32[2,256,512]{2,1,0:T(8,128)S(1)}, bf16[2,256,512]{2,1,0:T(8,128)(2,1)S(1)}) custom-call(s32[3]{0:T(128)S(1)} %pad_add_fusion.2.place_ref, s32[4,256,4]{2,1,0:T(8,128)S(1)} %copy.14.inv_ref, f32[4,96,512]{2,1,0:T(8,128)S(1)} %copy-done.17, f32[4,96,512]{2,1,0:T(8,128)S(1)} %get-tuple-element.62.keep1, bf16[4,96,512]{2,1,0:T(8,128)(2,1)S(1)} %copy-done.21, ...), custom_call_target="tpu_custom_call" | custom-call | flops 805306368 | bytes 4849664 | tf_op jit(solution)/shard_map/merge_rows/pallas_call | solution.py:163
  180.5 10.1 %tile_products.11 = (f32[4,96,768]{2,1,0:T(8,128)S(1)}, bf16[4,96,768]{2,1,0:T(8,128)(2,1)S(1)}) custom-call(s32[3]{0:T(128)S(1)} %pad_add_fusion.2.place_ref, bf16[768,512]{1,0:T(8,128)(2,1)} %bitcast.12.refs_0_, bf16[768,512]{1,0:T(8,128)(2,1)} %collective-permute-done.5.refs_1_, bf16[768,512]{1,0:T(8,128)(2,1)} %collective-permute-done.6.refs_2_, ...), custom_call_target="tpu_custom_call" | custom-call | flops 4831838208 | bytes 14942208 | tf_op jit(solution)/shard_map/tile_products/pallas_call | solution.py:106
  191.9 6.8 %merge_rows.4 = (f32[2,256,768]{2,1,0:T(8,128)S(1)}, bf16[2,256,768]{2,1,0:T(8,128)(2,1)}) custom-call(s32[3]{0:T(128)S(1)} %pad_add_fusion.2.place_ref, s32[4,256,4]{2,1,0:T(8,128)S(1)} %copy.14.inv_ref, f32[4,96,768]{2,1,0:T(8,128)S(1)} %copy-done.15, f32[4,96,768]{2,1,0:T(8,128)S(1)} %get-tuple-element.65.keep1, ...), custom_call_target="tpu_custom_call" | custom-call | flops 1207959552 | bytes 7274496 | tf_op jit(solution)/shard_map/merge_rows/pallas_call | solution.py:163
  199.9 6.1 %collective-permute-done.17.got_ref = bf16[2,256,512]{2,1,0:T(8,128)(2,1)S(1)} collective-permute-done((bf16[2,256,512]{2,1,0:T(8,128)(2,1)S(1)}, bf16[2,256,512]{2,1,0:T(8,128)(2,1)S(1)}, u32[]{:S(2)}, u32[]{:S(2)}) %collective-permute-start.17) | collective-permute-done | bytes 524320 | tf_op jit(solution)/shard_map/ppermute | solution.py:320
  208.2 5.8 %merge_rows.5 = (f32[2,256,768]{2,1,0:T(8,128)S(1)}, bf16[2,256,768]{2,1,0:T(8,128)(2,1)}) custom-call(s32[3]{0:T(128)S(1)} %pad_add_fusion.2.place_ref, s32[4,256,4]{2,1,0:T(8,128)S(1)} %copy.14.inv_ref, f32[4,96,768]{2,1,0:T(8,128)S(1)} %copy-done.13, f32[4,96,768]{2,1,0:T(8,128)S(1)} %get-tuple-element.70.keep1, ...), custom_call_target="tpu_custom_call" | custom-call | flops 1207959552 | bytes 7274496 | tf_op jit(solution)/shard_map/merge_rows/pallas_call | solution.py:163
  215.5 3.0 %collective-permute-start.23 = (bf16[1,256,512]{2,1,0:T(8,128)(2,1)}, bf16[1,256,512]{2,1,0:T(8,128)(2,1)}, u32[]{:S(2)}, u32[]{:S(2)}) collective-permute-start(bf16[1,256,512]{2,1,0:T(8,128)(2,1)} %copy-done.22), channel_id=1, source_target_pairs={{0,16},{4,20},{8,24},{12,28},{16,0},{20,4},{24,8},{28,12},{1,17},{... | collective-permute-start | bytes 786440 | tf_op jit(solution)/shard_map/ppermute | solution.py:320
  218.4 14.3 %collective-permute-done.19.got_ref = bf16[2,256,768]{2,1,0:T(8,128)(2,1)S(1)} collective-permute-done((bf16[2,256,768]{2,1,0:T(8,128)(2,1)}, bf16[2,256,768]{2,1,0:T(8,128)(2,1)S(1)}, u32[]{:S(2)}, u32[]{:S(2)}) %collective-permute-start.19) | collective-permute-done | bytes 786464 | tf_op jit(solution)/shard_map/ppermute | solution.py:320
  235.8 10.6 %collective-permute-done.20.got_ref = bf16[2,256,768]{2,1,0:T(8,128)(2,1)S(1)} collective-permute-done((bf16[2,256,768]{2,1,0:T(8,128)(2,1)}, bf16[2,256,768]{2,1,0:T(8,128)(2,1)S(1)}, u32[]{:S(2)}, u32[]{:S(2)}) %collective-permute-start.20) | collective-permute-done | bytes 786464 | tf_op jit(solution)/shard_map/ppermute | solution.py:320
  254.1 13.3 %collective-permute-done.22.got_ref = bf16[1,256,768]{2,1,0:T(8,128)(2,1)S(1)} collective-permute-done((bf16[1,256,768]{2,1,0:T(8,128)(2,1)}, bf16[1,256,768]{2,1,0:T(8,128)(2,1)S(1)}, u32[]{:S(2)}, u32[]{:S(2)}) %collective-permute-start.22) | collective-permute-done | bytes 393248 | tf_op jit(solution)/shard_map/ppermute | solution.py:320
  (133 shorter events, 45.1 us)
Async XLA Ops:
  51.8 35.1 %collective-permute-start = (bf16[768,1024]{1,0:T(8,128)(2,1)S(1)}, bf16[768,1024]{1,0:T(8,128)(2,1)S(1)}, u32[]{:S(2)}, u32[]{:S(2)}) collective-permute-start(bf16[768,1024]{1,0:T(8,128)(2,1)S(1)} %bitcast.64), channel_id=1, source_target_pairs={{0,2},{1,3},{2,0},{3,1},{4,6},{5,7},{6,4},{7,5},{8,10},{9,11},{10,... | collective-permute-start | bytes 4718600 | tf_op jit(solution)/shard_map/ppermute | solution.py:315
  53.4 33.5 %all-to-all-start.1 = ((bf16[8,96,512]{2,1,0:T(8,128)(2,1)}), bf16[8,96,512]{2,1,0:T(8,128)(2,1)}, u32[]{:S(2)}, u32[]{:S(2)}) async-start(bf16[8,96,512]{2,1,0:T(8,128)(2,1)} %bitcast.71), calls=%async_computation.1 | async-start | bytes 1572864 | tf_op jit(solution)/shard_map/all_to_all | solution.py:288
  61.3 25.5 %collective-permute-start.14 = (s32[3,256]{1,0:T(4,128)S(1)}, s32[3,256]{1,0:T(4,128)S(1)}, u32[]{:S(2)}, u32[]{:S(2)}) collective-permute-start(s32[3,256]{1,0:T(4,128)S(1)} %bitcast.74), channel_id=1, source_target_pairs={{0,16},{4,20},{8,24},{12,28},{16,0},{20,4},{24,8},{28,12},{1,17},{... | collective-permute-start | bytes 9224 | tf_op jit(solution)/shard_map/ppermute | solution.py:277
  61.3 30.0 %collective-permute-start.15 = (s32[3,256]{1,0:T(4,128)S(1)}, s32[3,256]{1,0:T(4,128)S(1)}, u32[]{:S(2)}, u32[]{:S(2)}) collective-permute-start(s32[3,256]{1,0:T(4,128)S(1)} %bitcast.75), channel_id=1, source_target_pairs={{0,8},{4,12},{8,16},{12,20},{16,24},{20,28},{24,0},{28,4},{1,9},{5... | collective-permute-start | bytes 9224 | tf_op jit(solution)/shard_map/ppermute | solution.py:277
  69.6 44.2 %collective-permute-start.1 = (bf16[768,1024]{1,0:T(8,128)(2,1)S(1)}, bf16[768,1024]{1,0:T(8,128)(2,1)}, u32[]{:S(2)}, u32[]{:S(2)}) collective-permute-start(bf16[768,1024]{1,0:T(8,128)(2,1)S(1)} %bitcast.65), channel_id=1, source_target_pairs={{0,1},{1,0},{2,3},{3,2},{4,5},{5,4},{6,7},{7,6},{8,9},{9,8},{10,11... | collective-permute-start | bytes 4718600 | tf_op jit(solution)/shard_map/ppermute | solution.py:315
  86.8 26.9 %collective-permute-start.2 = (bf16[768,1024]{1,0:T(8,128)(2,1)S(1)}, bf16[768,1024]{1,0:T(8,128)(2,1)}, u32[]{:S(2)}, u32[]{:S(2)}) collective-permute-start(bf16[768,1024]{1,0:T(8,128)(2,1)S(1)} %collective-permute-done.refs_1_), channel_id=1, source_target_pairs={{0,1},{1,0},{2,3},{3,2},{4,5},{5,4},{6,7},{7,6},{8,9},{9,8},{10,11... | collective-permute-start | bytes 4718600 | tf_op jit(solution)/shard_map/ppermute | solution.py:315
  86.9 25.3 %all-to-all-start.2 = ((bf16[8,96,512]{2,1,0:T(8,128)(2,1)}), bf16[8,96,512]{2,1,0:T(8,128)(2,1)}, u32[]{:S(2)}, u32[]{:S(2)}) async-start(bf16[8,96,512]{2,1,0:T(8,128)(2,1)} %bitcast.70), calls=%async_computation.2 | async-start | bytes 1572864 | tf_op jit(solution)/shard_map/all_to_all | solution.py:288
  91.3 20.3 %collective-permute-start.5 = (bf16[768,512]{1,0:T(8,128)(2,1)}, bf16[768,512]{1,0:T(8,128)(2,1)}, u32[]{:S(2)}, u32[]{:S(2)}) collective-permute-start(bf16[768,512]{1,0:T(8,128)(2,1)} %bitcast.12.refs_0_), channel_id=1, source_target_pairs={{0,2},{1,3},{2,0},{3,1},{4,6},{5,7},{6,4},{7,5},{8,10},{9,11},{10,... | collective-permute-start | bytes 2359304 | tf_op jit(solution)/shard_map/ppermute | solution.py:315
  93.0 57.8 %collective-permute-start.6 = (bf16[768,512]{1,0:T(8,128)(2,1)}, bf16[768,512]{1,0:T(8,128)(2,1)}, u32[]{:S(2)}, u32[]{:S(2)}) collective-permute-start(bf16[768,512]{1,0:T(8,128)(2,1)} %bitcast.12.refs_0_), channel_id=1, source_target_pairs={{0,1},{1,0},{2,3},{3,2},{4,5},{5,4},{6,7},{7,6},{8,9},{9,8},{10,11... | collective-permute-start | bytes 2359304 | tf_op jit(solution)/shard_map/ppermute | solution.py:315
  111.6 39.1 %collective-permute-start.7 = (bf16[768,512]{1,0:T(8,128)(2,1)}, bf16[768,512]{1,0:T(8,128)(2,1)}, u32[]{:S(2)}, u32[]{:S(2)}) collective-permute-start(bf16[768,512]{1,0:T(8,128)(2,1)} %collective-permute-done.5.refs_1_), channel_id=1, source_target_pairs={{0,1},{1,0},{2,3},{3,2},{4,5},{5,4},{6,7},{7,6},{8,9},{9,8},{10,11... | collective-permute-start | bytes 2359304 | tf_op jit(solution)/shard_map/ppermute | solution.py:315
  112.2 33.6 %collective-permute-start.8 = (bf16[768,512]{1,0:T(8,128)(2,1)}, bf16[768,512]{1,0:T(8,128)(2,1)}, u32[]{:S(2)}, u32[]{:S(2)}) collective-permute-start(bf16[768,512]{1,0:T(8,128)(2,1)} %bitcast.14.refs_4_), channel_id=1, source_target_pairs={{0,2},{1,3},{2,0},{3,1},{4,6},{5,7},{6,4},{7,5},{8,10},{9,11},{10,... | collective-permute-start | bytes 2359304 | tf_op jit(solution)/shard_map/ppermute | solution.py:315
  113.7 37.0 %collective-permute-start.9 = (bf16[768,512]{1,0:T(8,128)(2,1)}, bf16[768,512]{1,0:T(8,128)(2,1)}, u32[]{:S(2)}, u32[]{:S(2)}) collective-permute-start(bf16[768,512]{1,0:T(8,128)(2,1)} %bitcast.14.refs_4_), channel_id=1, source_target_pairs={{0,1},{1,0},{2,3},{3,2},{4,5},{5,4},{6,7},{7,6},{8,9},{9,8},{10,11... | collective-permute-start | bytes 2359304 | tf_op jit(solution)/shard_map/ppermute | solution.py:315
  121.9 12.2 %collective-permute-start.3 = (bf16[4,96,512]{2,1,0:T(8,128)(2,1)S(1)}, bf16[4,96,512]{2,1,0:T(8,128)(2,1)S(1)}, u32[]{:S(2)}, u32[]{:S(2)}) collective-permute-start(bf16[4,96,512]{2,1,0:T(8,128)(2,1)S(1)} %get-tuple-element.54), channel_id=1, source_target_pairs={{0,4},{4,0},{8,12},{12,8},{16,20},{20,16},{24,28},{28,24},{1,5},{5... | collective-permute-start | bytes 1179656 | tf_op jit(solution)/shard_map/ppermute | solution.py:320
  134.1 15.8 %collective-permute-start.4 = (bf16[4,96,768]{2,1,0:T(8,128)(2,1)}, bf16[4,96,768]{2,1,0:T(8,128)(2,1)}, u32[]{:S(2)}, u32[]{:S(2)}) collective-permute-start(bf16[4,96,768]{2,1,0:T(8,128)(2,1)} %get-tuple-element.59), channel_id=1, source_target_pairs={{0,4},{4,0},{8,12},{12,8},{16,20},{20,16},{24,28},{28,24},{1,5},{5... | collective-permute-start | bytes 1769480 | tf_op jit(solution)/shard_map/ppermute | solution.py:320
  149.8 14.6 %collective-permute-start.11 = (bf16[4,96,768]{2,1,0:T(8,128)(2,1)S(1)}, bf16[4,96,768]{2,1,0:T(8,128)(2,1)S(1)}, u32[]{:S(2)}, u32[]{:S(2)}) collective-permute-start(bf16[4,96,768]{2,1,0:T(8,128)(2,1)S(1)} %copy-done.19), channel_id=1, source_target_pairs={{0,4},{4,0},{8,12},{12,8},{16,20},{20,16},{24,28},{28,24},{1,5},{5... | collective-permute-start | bytes 1769480 | tf_op jit(solution)/shard_map/ppermute | solution.py:320
  164.5 12.0 %collective-permute-start.12 = (bf16[4,96,512]{2,1,0:T(8,128)(2,1)S(1)}, bf16[4,96,512]{2,1,0:T(8,128)(2,1)S(1)}, u32[]{:S(2)}, u32[]{:S(2)}) collective-permute-start(bf16[4,96,512]{2,1,0:T(8,128)(2,1)S(1)} %get-tuple-element.66), channel_id=1, source_target_pairs={{0,4},{4,0},{8,12},{12,8},{16,20},{20,16},{24,28},{28,24},{1,5},{5... | collective-permute-start | bytes 1179656 | tf_op jit(solution)/shard_map/ppermute | solution.py:320
  174.8 17.1 %collective-permute-start.16 = (bf16[4,96,768]{2,1,0:T(8,128)(2,1)S(1)}, bf16[4,96,768]{2,1,0:T(8,128)(2,1)S(1)}, u32[]{:S(2)}, u32[]{:S(2)}) collective-permute-start(bf16[4,96,768]{2,1,0:T(8,128)(2,1)S(1)} %get-tuple-element.72), channel_id=1, source_target_pairs={{0,4},{4,0},{8,12},{12,8},{16,20},{20,16},{24,28},{28,24},{1,5},{5... | collective-permute-start | bytes 1769480 | tf_op jit(solution)/shard_map/ppermute | solution.py:320
  190.6 17.5 %collective-permute-start.18 = (bf16[4,96,768]{2,1,0:T(8,128)(2,1)S(1)}, bf16[4,96,768]{2,1,0:T(8,128)(2,1)S(1)}, u32[]{:S(2)}, u32[]{:S(2)}) collective-permute-start(bf16[4,96,768]{2,1,0:T(8,128)(2,1)S(1)} %get-tuple-element.78), channel_id=1, source_target_pairs={{0,4},{4,0},{8,12},{12,8},{16,20},{20,16},{24,28},{28,24},{1,5},{5... | collective-permute-start | bytes 1769480 | tf_op jit(solution)/shard_map/ppermute | solution.py:320
  191.1 14.9 %collective-permute-start.17 = (bf16[2,256,512]{2,1,0:T(8,128)(2,1)S(1)}, bf16[2,256,512]{2,1,0:T(8,128)(2,1)S(1)}, u32[]{:S(2)}, u32[]{:S(2)}) collective-permute-start(bf16[2,256,512]{2,1,0:T(8,128)(2,1)S(1)} %get-tuple-element.75), channel_id=1, source_target_pairs={{0,8},{4,12},{8,0},{12,4},{16,24},{20,28},{24,16},{28,20},{1,9},{5... | collective-permute-start | bytes 1572872 | tf_op jit(solution)/shard_map/ppermute | solution.py:320
  198.7 34.0 %collective-permute-start.19 = (bf16[2,256,768]{2,1,0:T(8,128)(2,1)}, bf16[2,256,768]{2,1,0:T(8,128)(2,1)S(1)}, u32[]{:S(2)}, u32[]{:S(2)}) collective-permute-start(bf16[2,256,768]{2,1,0:T(8,128)(2,1)} %get-tuple-element.81), channel_id=1, source_target_pairs={{0,8},{4,12},{8,0},{12,4},{16,24},{20,28},{24,16},{28,20},{1,9},{5... | collective-permute-start | bytes 2359304 | tf_op jit(solution)/shard_map/ppermute | solution.py:320
  215.1 31.3 %collective-permute-start.20 = (bf16[2,256,768]{2,1,0:T(8,128)(2,1)}, bf16[2,256,768]{2,1,0:T(8,128)(2,1)S(1)}, u32[]{:S(2)}, u32[]{:S(2)}) collective-permute-start(bf16[2,256,768]{2,1,0:T(8,128)(2,1)} %get-tuple-element.84), channel_id=1, source_target_pairs={{0,8},{4,12},{8,0},{12,4},{16,24},{20,28},{24,16},{28,20},{1,9},{5... | collective-permute-start | bytes 2359304 | tf_op jit(solution)/shard_map/ppermute | solution.py:320
  215.5 34.9 %collective-permute-start.23 = (bf16[1,256,512]{2,1,0:T(8,128)(2,1)}, bf16[1,256,512]{2,1,0:T(8,128)(2,1)}, u32[]{:S(2)}, u32[]{:S(2)}) collective-permute-start(bf16[1,256,512]{2,1,0:T(8,128)(2,1)} %copy-done.22), channel_id=1, source_target_pairs={{0,16},{4,20},{8,24},{12,28},{16,0},{20,4},{24,8},{28,12},{1,17},{... | collective-permute-start | bytes 786440 | tf_op jit(solution)/shard_map/ppermute | solution.py:320
  234.9 32.5 %collective-permute-start.22 = (bf16[1,256,768]{2,1,0:T(8,128)(2,1)}, bf16[1,256,768]{2,1,0:T(8,128)(2,1)S(1)}, u32[]{:S(2)}, u32[]{:S(2)}) collective-permute-start(bf16[1,256,768]{2,1,0:T(8,128)(2,1)} %get-tuple-element.87), channel_id=1, source_target_pairs={{0,16},{4,20},{8,24},{12,28},{16,0},{20,4},{24,8},{28,12},{1,17},{... | collective-permute-start | bytes 1179656 | tf_op jit(solution)/shard_map/ppermute | solution.py:320
  249.5 22.5 %collective-permute-start.21 = (bf16[1,256,768]{2,1,0:T(8,128)(2,1)}, bf16[1,256,768]{2,1,0:T(8,128)(2,1)S(1)}, u32[]{:S(2)}, u32[]{:S(2)}) collective-permute-start(bf16[1,256,768]{2,1,0:T(8,128)(2,1)} %get-tuple-element.86), channel_id=1, source_target_pairs={{0,16},{4,20},{8,24},{12,28},{16,0},{20,4},{24,8},{28,12},{1,17},{... | collective-permute-start | bytes 1179656 | tf_op jit(solution)/shard_map/ppermute | solution.py:320
  (29 other events, 531.4 us)

commit v3 on v0

v3 whole, which is shorter than its diff:
```python
import functools
import math

import jax
import jax.numpy as jnp
from jax import lax
from jax.experimental import pallas as pl
from jax.experimental.pallas import tpu as pltpu
from jax.sharding import PartitionSpec as P

MIB = 1024 * 1024
F32 = jnp.float32
BF16 = jnp.bfloat16
CHUNKS = (4, 4)
HEAVY = 1e11
EARLY_JOINED = True


def params(mib=16):
    return pltpu.CompilerParams(vmem_limit_bytes=mib * MIB)


def cost(flops, nbytes):
    return pl.CostEstimate(flops=int(flops), bytes_accessed=int(nbytes), transcendentals=0)


def encode(v):
    w = v * 8.0
    sq = w * w
    quad = sq * sq
    return ((w * jnp.abs(w)) * (quad * sq)).astype(BF16)


def decode(code):
    c = code.astype(F32)
    a = jnp.abs(c)
    t = lax.rsqrt(jnp.maximum(a, 1e-37))
    u = lax.rsqrt(t)
    root = u * lax.rsqrt(u) * 0.125
    root = jnp.where(a < 1e-37, 0.0, root)
    return jnp.where(c < 0.0, -root, root)


def after(x, *earlier):
    earlier = [y for y in earlier if y is not None]
    return lax.optimization_barrier((x, *earlier))[0] if earlier else x


def pin_kernel(place_ref, out_ref):
    out_ref[0] = place_ref[0]


def pin(place, *earlier):
    scalar = pl.BlockSpec(memory_space=pltpu.SMEM)
    return pl.pallas_call(
        pin_kernel,
        in_specs=[scalar],
        out_specs=scalar,
        out_shape=jax.ShapeDtypeStruct((1,), jnp.int32),
        cost_estimate=cost(HEAVY, 8),
        name="pin",
    )(after(place, *earlier))


def pack_kernel(codes_ref, tiles_ref, *outs):
    top, rows, _ = tiles_ref.shape
    block = outs[0].shape[0]
    lane = lax.broadcasted_iota(jnp.int32, (block, rows), 0)
    for at, out in enumerate(outs):
        total = None
        for k in range(top):
            pick = (lane == codes_ref[k : k + 1, :] - at * block).astype(F32).astype(BF16)
            part = jnp.dot(pick, tiles_ref[k], preferred_element_type=F32)
            total = part if total is None else total + part
        out[...] = total.astype(BF16)


def pack(codes, tiles, count, block):
    top, rows, width = tiles.shape
    n_slots = count * block
    return pl.pallas_call(
        pack_kernel,
        out_shape=[jax.ShapeDtypeStruct((block, width), BF16)] * count,
        compiler_params=params(),
        cost_estimate=cost(0, 0),
        name="pack_tiles",
    )(codes, tiles)


def product_kernel(layout, place_ref, *refs):
    *parts, w_ref, keep_ref, send_ref = refs
    cap = keep_ref.shape[2]
    sides = {}
    for part, (rel, ks) in zip(parts, layout):
        sides.setdefault(rel, []).append((part, ks))
    total = None
    for rel, blocks in sides.items():
        lhs = [part[:, 0].reshape(-1, part.shape[3]) for part, _ in blocks]
        lhs = jnp.concatenate(lhs, axis=0) if len(lhs) > 1 else lhs[0]
        size = lhs.shape[1]
        start = pl.multiple_of(lax.bitwise_xor(place_ref[0], rel) * size, size)
        more = jnp.dot(lhs, w_ref[0, pl.ds(start, size), :], preferred_element_type=F32)
        total = more if total is None else total + more
    for n, k in enumerate([k for _, ks in sides[0] for k in ks]):
        block = total[n * cap : (n + 1) * cap]
        if k % 2:
            send_ref[0, k // 4] = encode(block)
        else:
            keep_ref[0, k // 4] = block


def product(place, pieces, integrals, first, cols, cap):
    lhs = [piece[0] for piece in pieces]
    layout = tuple(piece[1:] for piece in pieces)
    experts, width, _ = integrals.shape
    half = sum(x.shape[0] for x, rel, _ in pieces if rel == 0) // 2
    step = math.gcd(first, cols) if first else cols
    base, steps = first // step, cols // step
    out = pl.BlockSpec((1, half, cap, step), lambda t, s: (t // steps, 0, 0, t % steps))
    shape = (experts, half, cap, cols)
    return pl.pallas_call(
        functools.partial(product_kernel, layout),
        grid_spec=pltpu.PrefetchScalarGridSpec(
            num_scalar_prefetch=1,
            grid=(experts * steps,),
            in_specs=[
                pl.BlockSpec((x.shape[0], 1, *x.shape[2:]), lambda t, s: (0, t // steps, 0, 0))
                for x in lhs
            ]
            + [pl.BlockSpec((1, width, step), lambda t, s: (t // steps, 0, base + t % steps))],
            out_specs=[out, out],
        ),
        out_shape=[jax.ShapeDtypeStruct(shape, F32), jax.ShapeDtypeStruct(shape, BF16)],
        compiler_params=params(36),
        cost_estimate=cost(HEAVY, 2 * experts * width * cols),
        name="tile_products",
    )(place, *lhs, integrals)


def dense_rows(inv_ref, values):
    rows = inv_ref.shape[1]
    slots = values.shape[0]
    cap = slots // 4
    lane = lax.broadcasted_iota(jnp.int32, (rows, slots), 1)
    hit = None
    for c in range(4):
        slot = inv_ref[0, :, c : c + 1]
        one = lane == jnp.where(slot < 0, -1, slot + c * cap)
        hit = one if hit is None else hit | one
    pick = hit.astype(F32).astype(BF16)
    high = values.astype(BF16)
    low = (values - high.astype(F32)).astype(BF16)
    dense = jnp.dot(pick, high, preferred_element_type=F32)
    return dense + jnp.dot(pick, low, preferred_element_type=F32)


def merge_kernel(place_ref, inv_ref, keep0, keep1, got0, got1, *refs):
    values = [keep0[0, 0], keep1[0, 0], decode(got0[0, 0]), decode(got1[0, 0])]
    dense = dense_rows(inv_ref, jnp.concatenate(values, axis=0))
    if len(refs) == 1:
        refs[0][0] = encode(dense)
        return
    near_ref, kept_ref, send_ref = refs
    dense = dense + decode(near_ref[0])

    @pl.when(pl.program_id(0) % 2 == 0)
    def _():
        kept_ref[0] = dense

    @pl.when(pl.program_id(0) % 2 == 1)
    def _():
        send_ref[0] = encode(dense)


def merge(place, inv, keep, got, near):
    _, half, cap, cols = keep.shape
    rows = inv.shape[1]
    odd = near is None

    def spec(c):
        return pl.BlockSpec((1, 1, cap, cols), lambda i, s: (c, i, 0, 0))

    each = pl.BlockSpec((1, rows, cols), lambda i, s: (i, 0, 0))
    second = pl.BlockSpec((1, rows, cols), lambda i, s: (i // 2, 0, 0))
    shape = functools.partial(jax.ShapeDtypeStruct, (half // 2, rows, cols))
    return pl.pallas_call(
        merge_kernel,
        grid_spec=pltpu.PrefetchScalarGridSpec(
            num_scalar_prefetch=1,
            grid=(half,),
            in_specs=[pl.BlockSpec((1, rows, 4), lambda i, s: (2 * i + odd, 0, 0))]
            + [spec(0), spec(1)] * 2
            + [each] * (not odd),
            out_specs=each if odd else [second, second],
        ),
        out_shape=jax.ShapeDtypeStruct((half, rows, cols), BF16) if odd else [shape(F32), shape(BF16)],
        compiler_params=params(),
        cost_estimate=cost(0, 0),
        name="merge_rows",
    )(place, inv, keep, keep, got, got, *([] if odd else [near]))


def halve_kernel(kept_ref, got_ref, out_ref, send_ref):
    out_ref[0] = kept_ref[0] + decode(got_ref[0])
    send_ref[0] = encode(kept_ref[1] + decode(got_ref[1]))


def halve(kept, got):
    count, rows, cols = kept.shape
    step = rows // 2
    two = pl.BlockSpec((2, step, cols), lambda i, r: (i, r, 0))
    one = pl.BlockSpec((1, step, cols), lambda i, r: (i, r, 0))
    shape = (count // 2, rows, cols)
    return pl.pallas_call(
        halve_kernel,
        grid=(count // 2, rows // step),
        in_specs=[two, two],
        out_specs=[one, one],
        out_shape=[jax.ShapeDtypeStruct(shape, F32), jax.ShapeDtypeStruct(shape, BF16)],
        compiler_params=params(),
        cost_estimate=cost(0, 0),
        name="halve_rows",
    )(kept, got)


def finish_kernel(own_ref, got_ref, other_ref, occ_ref, virt_ref, *refs):
    total = own_ref[0] + decode(got_ref[0])
    denom = occ_ref[...] - virt_ref[...]
    refs[-1][...] = (0.5 * total + other_ref[...]) / denom


def finish(own, got, other, occ_sum, virt_sum, first, step, out):
    rows, width = other.shape
    cols = own.shape[2]
    base = first // step
    here = pl.BlockSpec((1, rows, step), lambda j: (0, 0, j))
    there = pl.BlockSpec((rows, step), lambda j: (0, base + j))
    earlier = [] if out is None else [out]
    return pl.pallas_call(
        finish_kernel,
        grid=(cols // step,),
        in_specs=[
            here,
            here,
            there,
            pl.BlockSpec((rows, 1), lambda j: (0, 0)),
            pl.BlockSpec((1, step), lambda j: (0, base + j)),
        ]
        + [pl.BlockSpec(memory_space=pl.ANY)] * len(earlier),
        out_specs=there,
        out_shape=jax.ShapeDtypeStruct((rows, width), F32),
        input_output_aliases={5: 0} if earlier else {},
        compiler_params=params(),
        cost_estimate=cost(0, 0),
        name="finish_rows",
    )(own, got, other, occ_sum, virt_sum, *earlier)


def ranks(named, experts):
    blocks, top, rows = named.shape
    flat = named.reshape(blocks, top * rows)
    onehot = flat[:, :, None] == jnp.arange(experts, dtype=jnp.int32)
    before = jnp.tri(top * rows, k=-1, dtype=BF16)
    count = jnp.einsum("ij,bje->bie", before, onehot.astype(BF16), preferred_element_type=F32)
    shape = (blocks, top, rows, experts)
    return onehot.reshape(shape), count.astype(jnp.int32).reshape(shape)


def per_device(
    amplitudes, screen, integrals, other, occ_first, occ_second, virt_first, virt_second
):
    rows, top, width = amplitudes.shape
    n_pair = lax.axis_size("pair")
    n_virt = lax.axis_size("virt")
    cd_dev, _, cols = integrals.shape
    experts = cd_dev * n_pair
    cap = rows * top * 2 // experts
    quarter = width // n_virt
    pair = lax.axis_index("pair")
    virt = lax.axis_index("virt")
    groups = n_pair // 2
    place = virt.astype(jnp.int32).reshape(1)
    block = cd_dev * cap

    def hop(x, bits):
        return lax.ppermute(x, "pair", [(i, i ^ bits) for i in range(n_pair)])

    def swap(x, bits):
        return lax.ppermute(x, "virt", [(i, i ^ bits) for i in range(n_virt)])

    named = screen.T
    onehot, rank = ranks(named[None], experts)
    slot = jnp.sum(jnp.where(onehot, rank, 0), axis=3)[0]
    partner = lax.bitwise_xor(named // cd_dev, pair.astype(jnp.int32))
    codes = partner * block + named % cd_dev * cap + slot
    tiles = lax.dynamic_slice_in_dim(amplitudes, virt * quarter, quarter, 2)
    tiles = tiles.transpose(1, 0, 2)
    packed = pack(codes, tiles, n_pair, block)

    early = [k for k in range(n_pair) if k // 2 % 2]
    late = [k for k in range(1, n_pair) if not k // 2 % 2]
    far = [k for ks in (early, late) for k in ks if k >= n_pair // 2]
    close = [k for ks in (early, late) for k in ks if k < n_pair // 2]
    held = {k: {0: x} for k, x in enumerate(packed)}
    shared = []

    def share(k, *waits):
        bits = n_virt // 2
        while bits > 1:
            more = {at | bits: swap(after(x, *waits), bits) for at, x in held[k].items()}
            held[k].update(more)
            bits //= 2
        shared.append(list(held[k].values())[-1])

    def send(ks, n):
        if n < len(ks):
            waits = [held[ks[n - 1]][0]] if n else []
            held[ks[n]] = {0: hop(after(packed[ks[n]], *waits), ks[n])}
            return [held[ks[n]][0]]
        return []

    share(0)
    for n in range(len(far) - 1):
        under_way = send(far, n) + send(close, n) + shared[-1:]
        if n:
            share(close[n - 1])
            share(far[n - 1])
            under_way += shared[-2:]
        if n == 1:
            at = after(named, held[close[0]][0])
            owners = [named] + [hop(at, 2 * r) for r in range(1, groups)]
            under_way += owners[1:]
        place = pin(place, *under_way)
    shares = [0] + [k for both in zip(far, close) for k in both] + far[-1:]

    all_hot, all_rank = ranks(jnp.stack(owners), experts)
    inv = jnp.sum(jnp.where(all_hot, all_rank + 1, 0), axis=1) - 1
    mine = lax.dynamic_slice_in_dim(inv, pair * cd_dev, cd_dev, 2)
    theirs = lax.dynamic_slice_in_dim(inv, lax.bitwise_xor(pair, 1) * cd_dev, cd_dev, 2)
    inv = jnp.concatenate([mine, theirs], axis=2)

    unit = cols // sum(CHUNKS)
    spans = [(unit * sum(CHUNKS[:j]), unit * size) for j, size in enumerate(CHUNKS)]
    count = len(spans)
    levels = groups.bit_length() - 1
    made, moved, near, state = {}, {}, {}, {}
    done, hops = [], []

    def make(pieces, j, *waits):
        at = after(place, *done[-1:], *hops[-2:-1], *waits)
        kept, sent = product(at, pieces, integrals, *spans[j], cap)
        made[j], moved[j] = kept, hop(sent, 1)
        hops.append(moved[j])
        done.append(kept)

    def first_rows(j):
        sent = merge(after(place, *done[-1:]), inv, made[j], moved[j], None)
        near[j] = hop(sent, 2)
        done.append(sent)

    def second_rows(j):
        kept, sent = merge(after(place, *done[-1:]), inv, made[j], moved[j], near[j])
        state[j] = (kept, hop(sent, 4))
        done.append(kept)

    def more_rows(j, level):
        kept, sent = halve(after(state[j][0], *done[-1:]), state[j][1])
        state[j] = (kept, hop(sent, 2 << level))
        done.append(kept)

    rows_early = [k for k in shares if k in early]
    rows_late = [k for k in shares if k not in early]

    def gather(ks, joined, *waits):
        pieces = []
        for ks in [ks] if joined else [[k] for k in ks]:
            for at in held[ks[0]]:
                x = jnp.concatenate([held[k][at] for k in ks])
                if at and ks[-1] == far[-1]:
                    x = after(x, *waits)
                for bit, y in ((0, x), (1, swap(x, 1))):
                    pieces.append((y.reshape(len(ks), cd_dev, cap, quarter), at | bit, tuple(ks)))
        return pieces

    last = len(far) - 1
    send(far, last)
    share(close[last - 1])
    share(far[last - 1])
    pieces = gather(rows_early, EARLY_JOINED)
    make(pieces, 0)
    waits = [held[far[last]][0], *shared[-2:]]
    for j in range(1, count):
        make(pieces, j, *waits)
        if j == 1:
            share(far[last])
        waits = shared[-1:]
        first_rows(j - 1)
    pieces = gather(rows_late, False, made[1])
    make(pieces, 0)
    first_rows(count - 1)
    for j in range(count):
        if j + 1 < count:
            make(pieces, j + 1, near[j])
        second_rows(j)
    for level in range(2, levels):
        for j in range(count):
            more_rows(j, level)

    tile = virt_first.shape[1]
    tile_sq = tile * tile
    start_col = virt * cols
    tile_pair = start_col // tile_sq
    first_a = start_col % tile_sq // tile
    energy_a = lax.dynamic_slice(virt_first, (tile_pair, first_a), (1, cols // tile)).reshape(-1)
    energy_b = lax.dynamic_slice_in_dim(virt_second, tile_pair, 1, 0).reshape(-1)
    virt_sum = (energy_a[:, None] + energy_b[None, :]).reshape(1, cols)
    per_i = occ_second.shape[0]
    energy_i = lax.dynamic_slice_in_dim(occ_first, pair * (rows // per_i), rows // per_i, 0)
    occ_sum = (energy_i[:, None] + occ_second[None, :]).reshape(rows, 1)
    out = None
    for j, (first, _) in enumerate(spans):
        own = after(state[j][0], *done[-1:])
        out = finish(own, state[j][1], other, occ_sum, virt_sum, first, unit, out)
    return out


def solution(mesh):
    return jax.shard_map(
        per_device,
        mesh=mesh,
        in_specs=(
            P("pair", None, None),
            P("pair", None),
            P("pair", None, "virt"),
            P("pair", "virt"),
            P(),
            P(),
            P(),
            P(),
        ),
        out_specs=P("pair", "virt"),
        check_vma=False,
    )
```

time: 876 us -> 224 us (0.26)
  blocking collectives: 281 us -> 0 us
  local copies, waits for them, and re-layouts: 270 us -> 20.3 us
  waiting for transfers between devices: 271 us -> 77.8 us
  Pallas kernels: 0 us -> 80 us
  starting transfers between devices: 5.69 us -> 41.6 us
  matrix products: 32 us -> 2.16 us
  other arithmetic: 14.2 us -> 1 us
    all_to_all x1 -> x0, blocking collectives: 281 us -> none  [per_device(): lax.all_to_all(buffer, 'pair', split_axis=0, concat_axis=0, tiled=True)]
    all_to_all x1 -> x0, waiting for transfers between devices: 271 us -> none  [per_device(): lax.all_to_all(jnp.einsum('scnk,ckm->scnm', lax.all_to_all(buffer, 'pair'...]
    scatter x1 -> x0, local copies, waits for them, and re-layouts: 200 us -> none  [per_device(): buffer = buffer.at[flat, slots].set(amplitudes.reshape(-1, width))]
    pallas_call x0 -> x14, Pallas kernels: none -> 80 us  [the longest x4 49.8 us: product(): pl.pallas_call(functools.partial(product_kernel, layout), grid_spec=pltpu...]
    ppermute x0 -> x36, waiting for transfers between devices: none -> 77.8 us  [the longest x18 72.9 us: hop(): return lax.ppermute(x, 'pair', [(i, i ^ bits) for i in range(n_pair)])]
    ppermute x0 -> x36, starting transfers between devices: none -> 41.6 us  [the longest x18 32.4 us: hop(): return lax.ppermute(x, 'pair', [(i, i ^ bits) for i in range(n_pair)])]
    dot_general x1 -> x2, matrix products: 32 us -> 2.16 us  [ranks(): jnp.einsum('ij,bje->bie', before, onehot.astype(BF16), preferred_element_...]
    reshape x3 -> x0, local copies, waits for them, and re-layouts: 24.4 us -> none  [the longest x1 13.7 us: per_device(): buffer = buffer.at[flat, slots].set(amplitudes.reshape(-1, width))]
  transfers between devices with their start and end apart: 1 -> 36, of which waited for: 1 -> 14; matrix products, arithmetic and copies ran while one was open for 0% -> 4% of each run, Pallas kernels for 0% -> 33%
where the time goes in v3:
time: 224 us; the launch traced here: 223 us
  Pallas kernels  80 us (36%)
  waiting for transfers between devices  77.8 us (35%)
  starting transfers between devices  41.6 us (19%)
  local copies, waits for them, and re-layouts  20.3 us (9%)
    ppermute x18, waiting for transfers between devices, hop(): return lax.ppermute(x, 'pair', [(i, i ^ bits) for i in range(n_pair)])  72.9 us
    pallas_call x4, Pallas kernels, product(): pl.pallas_call(functools.partial(product_kernel, layout), grid_spec=pltpu...  49.8 us
    ppermute x18, starting transfers between devices, hop(): return lax.ppermute(x, 'pair', [(i, i ^ bits) for i in range(n_pair)])  32.4 us
    pallas_call x4, Pallas kernels, merge(): pl.pallas_call(merge_kernel, grid_spec=pltpu.PrefetchScalarGridSpec(num_s...  18.4 us
    unnamed x59, local copies, waits for them, and re-layouts  15.3 us
    ppermute x18, starting transfers between devices, swap(): return lax.ppermute(x, 'virt', [(i, i ^ bits) for i in range(n_virt)])  9.18 us
    pallas_call x2, Pallas kernels, finish(): pl.pallas_call(finish_kernel, grid=(cols // step,), in_specs=[here, here,...  5.83 us
    ppermute x18, waiting for transfers between devices, swap(): return lax.ppermute(x, 'virt', [(i, i ^ bits) for i in range(n_virt)])  4.85 us
  transfers between devices with their start and end apart: 36, of which 14 were waited for; matrix products, arithmetic and copies ran while one was open for 4% of the time, Pallas kernels for 33%

profile of v3, /device:TPU:0, one launch (start us, length us, event | category | flops | bytes accessed | tf_op | source)
XLA Modules:
  0.0 223.2 jit_solution(7091679672122775292)
XLA Ops:
  3.1 3.1 %pack_tiles.1 = (bf16[192,1024]{1,0:T(8,128)(2,1)}, bf16[192,1024]{1,0:T(8,128)(2,1)}, bf16[192,1024]{1,0:T(8,128)(2,1)S(1)}, bf16[192,1024]{1,0:T(8,128)(2,1)S(...) custom-call(s32[3,256]{1,0:T(4,128)S(1)} %fusion.26.codes_ref, ...), custom_call_target="tpu_custom_call" | custom-call | tf_op jit(solution)/shard_map/pack_tiles/pallas_call | solution.py:81
  7.0 3.0 %collective-permute-start.1 = (bf16[192,1024]{1,0:T(8,128)(2,1)S(1)}, bf16[192,1024]{1,0:T(8,128)(2,1)S(1)}, u32[]{:S(2)}, u32[]{:S(2)}) collective-permute-start(bf16[192,1024]{1,0:T(8,128)(2,1)S(1)} %get-tuple-element.45), channel_id=1, source_target_pairs={{0,8},{4,12},{8,0},{12,4},{16,24},{20,28},{24,16},{28,20},{1,9},{5... | collective-permute-start | bytes 1179656 | tf_op jit(solution)/shard_map/ppermute | solution.py:286
  14.1 5.5 %collective-permute-done.1 = bf16[192,1024]{1,0:T(8,128)(2,1)S(1)} collective-permute-done((bf16[192,1024]{1,0:T(8,128)(2,1)S(1)}, bf16[192,1024]{1,0:T(8,128)(2,1)S(1)}, u32[]{:S(2)}, u32[]{:S(2)}) %collective-permute-start.1) | collective-permute-done | bytes 393248 | tf_op jit(solution)/shard_map/ppermute | solution.py:286
  22.1 9.9 %collective-permute-start.8 = (s32[3,256]{1,0:T(4,128)S(1)}, s32[3,256]{1,0:T(4,128)S(1)}, u32[]{:S(2)}, u32[]{:S(2)}) collective-permute-start(s32[3,256]{1,0:T(4,128)S(1)} %bitcast.69), channel_id=1, source_target_pairs={{0,16},{4,20},{8,24},{12,28},{16,0},{20,4},{24,8},{28,12},{1,17},{... | collective-permute-start | bytes 9224 | tf_op jit(solution)/shard_map/ppermute | solution.py:286
  34.1 3.3 %collective-permute-start.3 = (bf16[192,1024]{1,0:T(8,128)(2,1)S(1)}, bf16[192,1024]{1,0:T(8,128)(2,1)}, u32[]{:S(2)}, u32[]{:S(2)}) collective-permute-start(bf16[192,1024]{1,0:T(8,128)(2,1)S(1)} %get-tuple-element.49), channel_id=1, source_target_pairs={{0,28},{4,24},{8,20},{12,16},{16,12},{20,8},{24,4},{28,0},{1,29},{... | collective-permute-start | bytes 1179656 | tf_op jit(solution)/shard_map/ppermute | solution.py:286
  42.9 2.5 %collective-permute-done.4 = bf16[192,1024]{1,0:T(8,128)(2,1)} collective-permute-done((bf16[192,1024]{1,0:T(8,128)(2,1)S(1)}, bf16[192,1024]{1,0:T(8,128)(2,1)}, u32[]{:S(2)}, u32[]{:S(2)}) %collective-permute-start.4) | collective-permute-done | bytes 393248 | tf_op jit(solution)/shard_map/ppermute | solution.py:286
  45.4 10.9 %collective-permute-done.3 = bf16[192,1024]{1,0:T(8,128)(2,1)} collective-permute-done((bf16[192,1024]{1,0:T(8,128)(2,1)S(1)}, bf16[192,1024]{1,0:T(8,128)(2,1)}, u32[]{:S(2)}, u32[]{:S(2)}) %collective-permute-start.3) | collective-permute-done | bytes 393248 | tf_op jit(solution)/shard_map/ppermute | solution.py:286
  66.8 6.8 %collective-permute-done.10 = bf16[192,1024]{1,0:T(8,128)(2,1)} collective-permute-done((bf16[192,1024]{1,0:T(8,128)(2,1)}, bf16[192,1024]{1,0:T(8,128)(2,1)}, u32[]{:S(2)}, u32[]{:S(2)}) %collective-permute-start.10) | collective-permute-done | bytes 393248 | tf_op jit(solution)/shard_map/ppermute | solution.py:286
  73.7 3.1 %collective-permute-done.13 = bf16[192,1024]{1,0:T(8,128)(2,1)S(1)} collective-permute-done((bf16[192,1024]{1,0:T(8,128)(2,1)}, bf16[192,1024]{1,0:T(8,128)(2,1)S(1)}, u32[]{:S(2)}, u32[]{:S(2)}) %collective-permute-start.13) | collective-permute-done | bytes 393248 | tf_op jit(solution)/shard_map/ppermute | solution.py:289
  78.1 2.5 %collective-permute-start.16 = (bf16[192,1024]{1,0:T(8,128)(2,1)}, bf16[192,1024]{1,0:T(8,128)(2,1)}, u32[]{:S(2)}, u32[]{:S(2)}) collective-permute-start(bf16[192,1024]{1,0:T(8,128)(2,1)} %copy-done.18), channel_id=1, source_target_pairs={{0,20},{4,16},{8,28},{12,24},{16,4},{20,0},{24,12},{28,8},{1,21},{... | collective-permute-start | bytes 1179656 | tf_op jit(solution)/shard_map/ppermute | solution.py:286
  85.4 11.9 %tile_products.4 = (f32[2,2,96,1024]{3,2,1,0:T(8,128)S(1)}, bf16[2,2,96,1024]{3,2,1,0:T(8,128)(2,1)S(1)}) custom-call(s32[1]{0:T(128)} %pin.5.place_ref, bf16[4,2,96,1024]{3,2,1,0:T(8,128)(2,1)S(1)} %bitcast.60, bf16[4,2,96,1024]{3,2,1,0:T(8,128)(2,1)} %bitcast.6.refs_1_, bf16[4,2,96,1024]{3,2,1,0:T(8,128)(2,1)S(1)} %bitcast.58, ...), custom_call_target="tpu_custom_call" | custom-call | flops 99999997952 | bytes 16777216 | tf_op jit(solution)/shard_map/tile_products/pallas_call | solution.py:121
  102.0 11.7 %tile_products.5 = (f32[2,2,96,1024]{3,2,1,0:T(8,128)S(1)}, bf16[2,2,96,1024]{3,2,1,0:T(8,128)(2,1)S(1)}) custom-call(s32[1]{0:T(128)} %pin.5.place_ref, bf16[4,2,96,1024]{3,2,1,0:T(8,128)(2,1)S(1)} %bitcast.61, bf16[4,2,96,1024]{3,2,1,0:T(8,128)(2,1)} %bitcast.6.refs_1_, bf16[4,2,96,1024]{3,2,1,0:T(8,128)(2,1)S(1)} %bitcast.59, ...), custom_call_target="tpu_custom_call" | custom-call | flops 99999997952 | bytes 16777216 | tf_op jit(solution)/shard_map/tile_products/pallas_call | solution.py:121
  119.5 3.4 %merge_rows.4 = bf16[2,256,1024]{2,1,0:T(8,128)(2,1)S(1)} custom-call(s32[1]{0:T(128)} %pin.5.place_ref, s32[4,256,4]{2,1,0:T(8,128)S(1)} %copy.12.inv_ref, f32[2,2,96,1024]{3,2,1,0:T(8,128)S(1)} %get-tuple-element.59.keep0.keep1, f32[2,2,96,1024]{3,2,1,0:T(8,128)S(1)} %get-tuple-element.59.keep0.keep1, ...), custom_call_target="tpu_custom_call" | custom-call | tf_op jit(solution)/shard_map/merge_rows/pallas_call | solution.py:186
  124.6 13.0 %tile_products.6 = (f32[2,2,96,1024]{3,2,1,0:T(8,128)S(1)}, bf16[2,2,96,1024]{3,2,1,0:T(8,128)(2,1)}) custom-call(s32[1]{0:T(128)} %pin.5.place_ref, bf16[1,2,96,1024]{3,2,1,0:T(8,128)(2,1)} %bitcast.15.refs_0_, bf16[1,2,96,1024]{3,2,1,0:T(8,128)(2,1)} %bitcast.16.refs_1_, bf16[1,2,96,1024]{3,2,1,0:T(8,128)(2,1)} %bitcast.17.refs_2_, ...), custom_call_target="tpu_custom_call" | custom-call | flops 99999997952 | bytes 16777216 | tf_op jit(solution)/shard_map/tile_products/pallas_call | solution.py:121
  138.1 5.1 %collective-permute-done.29.got0.got1 = bf16[2,2,96,1024]{3,2,1,0:T(8,128)(2,1)S(1)} collective-permute-done((bf16[2,2,96,1024]{3,2,1,0:T(8,128)(2,1)S(1)}, bf16[2,2,96,1024]{3,2,1,0:T(8,128)(2,1)S(1)}, u32[]{:S(2)}, u32[]{:S(2)}) %collective-permute-start.29) | collective-permute-done | bytes 786464 | tf_op jit(solution)/shard_map/ppermute | solution.py:286
  143.3 4.1 %merge_rows.5 = bf16[2,256,1024]{2,1,0:T(8,128)(2,1)} custom-call(s32[1]{0:T(128)} %pin.5.place_ref, s32[4,256,4]{2,1,0:T(8,128)S(1)} %copy.12.inv_ref, f32[2,2,96,1024]{3,2,1,0:T(8,128)S(1)} %copy-done.5, f32[2,2,96,1024]{3,2,1,0:T(8,128)S(1)} %copy-done.5, bf16[2,2,96,1024]{3,2,1,0:T(8,128)(2,1)S(1)} %collective-permute-done.29.got0.got1, ...), custom_call_target="tpu_custom_call" | custom-call | tf_op jit(solution)/shard_map/merge_rows/pallas_call | solution.py:186
  147.3 2.9 %collective-permute-done.30.refs_0_ = bf16[2,256,1024]{2,1,0:T(8,128)(2,1)S(1)} collective-permute-done((bf16[2,256,1024]{2,1,0:T(8,128)(2,1)S(1)}, bf16[2,256,1024]{2,1,0:T(8,128)(2,1)S(1)}, u32[]{:S(2)}, u32[]{:S(2)}) %collective-permute-start.30) | collective-permute-done | bytes 1048608 | tf_op jit(solution)/shard_map/ppermute | solution.py:286
  150.2 13.1 %tile_products.7 = (f32[2,2,96,1024]{3,2,1,0:T(8,128)S(1)}, bf16[2,2,96,1024]{3,2,1,0:T(8,128)(2,1)}) custom-call(s32[1]{0:T(128)} %pin.5.place_ref, bf16[1,2,96,1024]{3,2,1,0:T(8,128)(2,1)} %bitcast.15.refs_0_, bf16[1,2,96,1024]{3,2,1,0:T(8,128)(2,1)} %bitcast.16.refs_1_, bf16[1,2,96,1024]{3,2,1,0:T(8,128)(2,1)} %bitcast.17.refs_2_, ...), custom_call_target="tpu_custom_call" | custom-call | flops 99999997952 | bytes 16777216 | tf_op jit(solution)/shard_map/tile_products/pallas_call | solution.py:121
  165.9 4.8 %merge_rows.6 = (f32[1,256,1024]{2,1,0:T(8,128)S(1)}, bf16[1,256,1024]{2,1,0:T(8,128)(2,1)}) custom-call(s32[1]{0:T(128)} %pin.5.place_ref, s32[4,256,4]{2,1,0:T(8,128)S(1)} %copy.12.inv_ref, f32[2,2,96,1024]{3,2,1,0:T(8,128)S(1)} %get-tuple-element.68.keep0.keep1, f32[2,2,96,1024]{3,2,1,0:T(8,128)S(1)} %get-tuple-element.68.keep0.keep1, ...), custom_call_target="tpu_custom_call" | custom-call | tf_op jit(solution)/shard_map/merge_rows/pallas_call | solution.py:186
  172.5 10.8 %collective-permute-done.32.got0.got1 = bf16[2,2,96,1024]{3,2,1,0:T(8,128)(2,1)} collective-permute-done((bf16[2,2,96,1024]{3,2,1,0:T(8,128)(2,1)}, bf16[2,2,96,1024]{3,2,1,0:T(8,128)(2,1)}, u32[]{:S(2)}, u32[]{:S(2)}) %collective-permute-start.32) | collective-permute-done | bytes 786464 | tf_op jit(solution)/shard_map/ppermute | solution.py:286
  183.4 6.2 %merge_rows.7 = (f32[1,256,1024]{2,1,0:T(8,128)S(1)}, bf16[1,256,1024]{2,1,0:T(8,128)(2,1)}) custom-call(s32[1]{0:T(128)} %pin.5.place_ref, s32[4,256,4]{2,1,0:T(8,128)S(1)} %copy.12.inv_ref, f32[2,2,96,1024]{3,2,1,0:T(8,128)S(1)} %copy-done.3, f32[2,2,96,1024]{3,2,1,0:T(8,128)S(1)} %copy-done.3, bf16[2,2,96,1024]{3,2,1,0:T(8,128)(2,1)} %collective-permute-done.32.got0.got1, ...), custom_call_target="tpu_custom_call" | custom-call | tf_op jit(solution)/shard_map/merge_rows/pallas_call | solution.py:186
  191.4 17.0 %collective-permute-done.35.got_ref = bf16[1,256,1024]{2,1,0:T(8,128)(2,1)S(1)} collective-permute-done((bf16[1,256,1024]{2,1,0:T(8,128)(2,1)}, bf16[1,256,1024]{2,1,0:T(8,128)(2,1)S(1)}, u32[]{:S(2)}, u32[]{:S(2)}) %collective-permute-start.35) | collective-permute-done | bytes 524320 | tf_op jit(solution)/shard_map/ppermute | solution.py:286
  211.8 7.8 %collective-permute-done.34.got_ref = bf16[1,256,1024]{2,1,0:T(8,128)(2,1)} collective-permute-done((bf16[1,256,1024]{2,1,0:T(8,128)(2,1)}, bf16[1,256,1024]{2,1,0:T(8,128)(2,1)}, u32[]{:S(2)}, u32[]{:S(2)}) %collective-permute-start.34) | collective-permute-done | bytes 524320 | tf_op jit(solution)/shard_map/ppermute | solution.py:286
  219.6 3.6 %finish_rows.3 = f32[256,2048]{1,0:T(8,128)} custom-call(f32[1,256,1024]{2,1,0:T(8,128)S(1)} %copy-done.9, bf16[1,256,1024]{2,1,0:T(8,128)(2,1)} %collective-permute-done.34.got_ref, f32[256,2048]{1,0:T(8,128)S(1)} %copy-done.1, f32[256,1]{1,0:T(8,128)S(1)} %add.133.occ_ref, f32[1,2048]{1,0:T(1,128)S(1)} %add.132.virt_ref, ...), custom_call_target="tpu_custom_call", output_to_operand_aliasing={{}: (5, {})} | custom-call | tf_op jit(solution)/shard_map/finish_rows/pallas_call | solution.py:239
  (149 shorter events, 56.6 us)
Async XLA Ops:
  10.1 21.9 %collective-permute-start.2 = (bf16[192,1024]{1,0:T(8,128)(2,1)}, bf16[192,1024]{1,0:T(8,128)(2,1)}, u32[]{:S(2)}, u32[]{:S(2)}) collective-permute-start(bf16[192,1024]{1,0:T(8,128)(2,1)} %get-tuple-element.46), channel_id=1, source_target_pairs={{0,2},{1,3},{2,0},{3,1},{4,6},{5,7},{6,4},{7,5},{8,10},{9,11},{10,... | collective-permute-start | bytes 1179656 | tf_op jit(solution)/shard_map/ppermute | solution.py:289
  11.6 20.4 %collective-permute-start = (bf16[192,1024]{1,0:T(8,128)(2,1)S(1)}, bf16[192,1024]{1,0:T(8,128)(2,1)S(1)}, u32[]{:S(2)}, u32[]{:S(2)}) collective-permute-start(bf16[192,1024]{1,0:T(8,128)(2,1)S(1)} %get-tuple-element.44), channel_id=1, source_target_pairs={{0,24},{4,28},{8,16},{12,20},{16,8},{20,12},{24,0},{28,4},{1,25},{... | collective-permute-start | bytes 1179656 | tf_op jit(solution)/shard_map/ppermute | solution.py:286
  14.0 101.7 %collective-permute-start.20 = (bf16[192,1024]{1,0:T(8,128)(2,1)}, bf16[192,1024]{1,0:T(8,128)(2,1)}, u32[]{:S(2)}, u32[]{:S(2)}) collective-permute-start(bf16[192,1024]{1,0:T(8,128)(2,1)} %get-tuple-element.46), channel_id=1, source_target_pairs={{0,1},{1,0},{2,3},{3,2},{4,5},{5,4},{6,7},{7,6},{8,9},{9,8},{10,11... | collective-permute-start | bytes 1179656 | tf_op jit(solution)/shard_map/ppermute | solution.py:289
  19.6 14.6 %collective-permute-start.7 = (s32[3,256]{1,0:T(4,128)S(1)}, s32[3,256]{1,0:T(4,128)S(1)}, u32[]{:S(2)}, u32[]{:S(2)}) collective-permute-start(s32[3,256]{1,0:T(4,128)S(1)} %bitcast.68), channel_id=1, source_target_pairs={{0,8},{4,12},{8,0},{12,4},{16,24},{20,28},{24,16},{28,20},{1,9},{5... | collective-permute-start | bytes 9224 | tf_op jit(solution)/shard_map/ppermute | solution.py:286
  22.1 15.4 %collective-permute-start.8 = (s32[3,256]{1,0:T(4,128)S(1)}, s32[3,256]{1,0:T(4,128)S(1)}, u32[]{:S(2)}, u32[]{:S(2)}) collective-permute-start(s32[3,256]{1,0:T(4,128)S(1)} %bitcast.69), channel_id=1, source_target_pairs={{0,16},{4,20},{8,24},{12,28},{16,0},{20,4},{24,8},{28,12},{1,17},{... | collective-permute-start | bytes 9224 | tf_op jit(solution)/shard_map/ppermute | solution.py:286
  34.1 22.2 %collective-permute-start.3 = (bf16[192,1024]{1,0:T(8,128)(2,1)S(1)}, bf16[192,1024]{1,0:T(8,128)(2,1)}, u32[]{:S(2)}, u32[]{:S(2)}) collective-permute-start(bf16[192,1024]{1,0:T(8,128)(2,1)S(1)} %get-tuple-element.49), channel_id=1, source_target_pairs={{0,28},{4,24},{8,20},{12,16},{16,12},{20,8},{24,4},{28,0},{1,29},{... | collective-permute-start | bytes 1179656 | tf_op jit(solution)/shard_map/ppermute | solution.py:286
  37.5 18.8 %collective-permute-start.5 = (bf16[192,1024]{1,0:T(8,128)(2,1)S(1)}, bf16[192,1024]{1,0:T(8,128)(2,1)}, u32[]{:S(2)}, u32[]{:S(2)}) collective-permute-start(bf16[192,1024]{1,0:T(8,128)(2,1)S(1)} %collective-permute-done.1), channel_id=1, source_target_pairs={{0,2},{1,3},{2,0},{3,1},{4,6},{5,7},{6,4},{7,5},{8,10},{9,11},{10,... | collective-permute-start | bytes 1179656 | tf_op jit(solution)/shard_map/ppermute | solution.py:289
  39.1 17.2 %collective-permute-start.6 = (bf16[192,1024]{1,0:T(8,128)(2,1)S(1)}, bf16[192,1024]{1,0:T(8,128)(2,1)}, u32[]{:S(2)}, u32[]{:S(2)}) collective-permute-start(bf16[192,1024]{1,0:T(8,128)(2,1)S(1)} %collective-permute-done), channel_id=1, source_target_pairs={{0,2},{1,3},{2,0},{3,1},{4,6},{5,7},{6,4},{7,5},{8,10},{9,11},{10,... | collective-permute-start | bytes 1179656 | tf_op jit(solution)/shard_map/ppermute | solution.py:289
  59.6 14.0 %collective-permute-start.12 = (bf16[192,1024]{1,0:T(8,128)(2,1)}, bf16[192,1024]{1,0:T(8,128)(2,1)S(1)}, u32[]{:S(2)}, u32[]{:S(2)}) collective-permute-start(bf16[192,1024]{1,0:T(8,128)(2,1)} %collective-permute-done.4), channel_id=1, source_target_pairs={{0,2},{1,3},{2,0},{3,1},{4,6},{5,7},{6,4},{7,5},{8,10},{9,11},{10,... | collective-permute-start | bytes 1179656 | tf_op jit(solution)/shard_map/ppermute | solution.py:289
  59.6 17.1 %collective-permute-start.13 = (bf16[192,1024]{1,0:T(8,128)(2,1)}, bf16[192,1024]{1,0:T(8,128)(2,1)S(1)}, u32[]{:S(2)}, u32[]{:S(2)}) collective-permute-start(bf16[192,1024]{1,0:T(8,128)(2,1)} %collective-permute-done.3), channel_id=1, source_target_pairs={{0,2},{1,3},{2,0},{3,1},{4,6},{5,7},{6,4},{7,5},{8,10},{9,11},{10,... | collective-permute-start | bytes 1179656 | tf_op jit(solution)/shard_map/ppermute | solution.py:289
  66.8 49.5 %collective-permute-start.21 = (bf16[192,1024]{1,0:T(8,128)(2,1)}, bf16[192,1024]{1,0:T(8,128)(2,1)}, u32[]{:S(2)}, u32[]{:S(2)}) collective-permute-start(bf16[192,1024]{1,0:T(8,128)(2,1)} %collective-permute-done.2), channel_id=1, source_target_pairs={{0,1},{1,0},{2,3},{3,2},{4,5},{5,4},{6,7},{7,6},{8,9},{9,8},{10,11... | collective-permute-start | bytes 1179656 | tf_op jit(solution)/shard_map/ppermute | solution.py:289
  78.1 20.2 %collective-permute-start.16 = (bf16[192,1024]{1,0:T(8,128)(2,1)}, bf16[192,1024]{1,0:T(8,128)(2,1)}, u32[]{:S(2)}, u32[]{:S(2)}) collective-permute-start(bf16[192,1024]{1,0:T(8,128)(2,1)} %copy-done.18), channel_id=1, source_target_pairs={{0,20},{4,16},{8,28},{12,24},{16,4},{20,0},{24,12},{28,8},{1,21},{... | collective-permute-start | bytes 1179656 | tf_op jit(solution)/shard_map/ppermute | solution.py:286
  80.6 17.7 %collective-permute-start.17 = (bf16[192,1024]{1,0:T(8,128)(2,1)S(1)}, bf16[192,1024]{1,0:T(8,128)(2,1)}, u32[]{:S(2)}, u32[]{:S(2)}) collective-permute-start(bf16[192,1024]{1,0:T(8,128)(2,1)S(1)} %collective-permute-done.11), channel_id=1, source_target_pairs={{0,2},{1,3},{2,0},{3,1},{4,6},{5,7},{6,4},{7,5},{8,10},{9,11},{10,... | collective-permute-start | bytes 1179656 | tf_op jit(solution)/shard_map/ppermute | solution.py:289
  80.9 19.5 %collective-permute-start.18 = (bf16[192,1024]{1,0:T(8,128)(2,1)}, bf16[192,1024]{1,0:T(8,128)(2,1)}, u32[]{:S(2)}, u32[]{:S(2)}) collective-permute-start(bf16[192,1024]{1,0:T(8,128)(2,1)} %collective-permute-done.10), channel_id=1, source_target_pairs={{0,2},{1,3},{2,0},{3,1},{4,6},{5,7},{6,4},{7,5},{8,10},{9,11},{10,... | collective-permute-start | bytes 1179656 | tf_op jit(solution)/shard_map/ppermute | solution.py:289
  98.2 18.2 %collective-permute-start.24 = (bf16[192,1024]{1,0:T(8,128)(2,1)S(1)}, bf16[192,1024]{1,0:T(8,128)(2,1)S(1)}, u32[]{:S(2)}, u32[]{:S(2)}) collective-permute-start(bf16[192,1024]{1,0:T(8,128)(2,1)S(1)} %collective-permute-done.11), channel_id=1, source_target_pairs={{0,1},{1,0},{2,3},{3,2},{4,5},{5,4},{6,7},{7,6},{8,9},{9,8},{10,11... | collective-permute-start | bytes 1179656 | tf_op jit(solution)/shard_map/ppermute | solution.py:289
  98.3 17.5 %collective-permute-start.27 = (bf16[192,1024]{1,0:T(8,128)(2,1)}, bf16[192,1024]{1,0:T(8,128)(2,1)}, u32[]{:S(2)}, u32[]{:S(2)}) collective-permute-start(bf16[192,1024]{1,0:T(8,128)(2,1)} %collective-permute-done.16), channel_id=1, source_target_pairs={{0,2},{1,3},{2,0},{3,1},{4,6},{5,7},{6,4},{7,5},{8,10},{9,11},{10,... | collective-permute-start | bytes 1179656 | tf_op jit(solution)/shard_map/ppermute | solution.py:289
  100.3 18.8 %collective-permute-start.19 = (bf16[2,2,96,1024]{3,2,1,0:T(8,128)(2,1)S(1)}, bf16[2,2,96,1024]{3,2,1,0:T(8,128)(2,1)S(1)}, u32[]{:S(2)}, u32[]{:S(2)}) collective-permute-start(bf16[2,2,96,1024]{3,2,1,0:T(8,128)(2,1)S(1)} %get-tuple-element.65), channel_id=1, source_target_pairs={{0,4},{4,0},{8,12},{12,8},{16,20},{20,16},{24,28},{28,24},{1,5},{5... | collective-permute-start | bytes 2359304 | tf_op jit(solution)/shard_map/ppermute | solution.py:286
  122.8 20.4 %collective-permute-start.29 = (bf16[2,2,96,1024]{3,2,1,0:T(8,128)(2,1)S(1)}, bf16[2,2,96,1024]{3,2,1,0:T(8,128)(2,1)S(1)}, u32[]{:S(2)}, u32[]{:S(2)}) collective-permute-start(bf16[2,2,96,1024]{3,2,1,0:T(8,128)(2,1)S(1)} %copy-done.17), channel_id=1, source_target_pairs={{0,4},{4,0},{8,12},{12,8},{16,20},{20,16},{24,28},{28,24},{1,5},{5... | collective-permute-start | bytes 2359304 | tf_op jit(solution)/shard_map/ppermute | solution.py:286
  124.6 25.6 %collective-permute-start.30 = (bf16[2,256,1024]{2,1,0:T(8,128)(2,1)S(1)}, bf16[2,256,1024]{2,1,0:T(8,128)(2,1)S(1)}, u32[]{:S(2)}, u32[]{:S(2)}) collective-permute-start(bf16[2,256,1024]{2,1,0:T(8,128)(2,1)S(1)} %merge_rows.4), channel_id=1, source_target_pairs={{0,8},{4,12},{8,0},{12,4},{16,24},{20,28},{24,16},{28,20},{1,9},{5... | collective-permute-start | bytes 3145736 | tf_op jit(solution)/shard_map/ppermute | solution.py:286
  137.7 26.9 %collective-permute-start.31 = (bf16[2,2,96,1024]{3,2,1,0:T(8,128)(2,1)}, bf16[2,2,96,1024]{3,2,1,0:T(8,128)(2,1)S(1)}, u32[]{:S(2)}, u32[]{:S(2)}) collective-permute-start(bf16[2,2,96,1024]{3,2,1,0:T(8,128)(2,1)} %get-tuple-element.74), channel_id=1, source_target_pairs={{0,4},{4,0},{8,12},{12,8},{16,20},{20,16},{24,28},{28,24},{1,5},{5... | collective-permute-start | bytes 2359304 | tf_op jit(solution)/shard_map/ppermute | solution.py:286
  147.3 25.2 %collective-permute-start.33 = (bf16[2,256,1024]{2,1,0:T(8,128)(2,1)}, bf16[2,256,1024]{2,1,0:T(8,128)(2,1)}, u32[]{:S(2)}, u32[]{:S(2)}) collective-permute-start(bf16[2,256,1024]{2,1,0:T(8,128)(2,1)} %merge_rows.5), channel_id=1, source_target_pairs={{0,8},{4,12},{8,0},{12,4},{16,24},{20,28},{24,16},{28,20},{1,9},{5... | collective-permute-start | bytes 3145736 | tf_op jit(solution)/shard_map/ppermute | solution.py:286
  164.5 18.8 %collective-permute-start.32 = (bf16[2,2,96,1024]{3,2,1,0:T(8,128)(2,1)}, bf16[2,2,96,1024]{3,2,1,0:T(8,128)(2,1)}, u32[]{:S(2)}, u32[]{:S(2)}) collective-permute-start(bf16[2,2,96,1024]{3,2,1,0:T(8,128)(2,1)} %get-tuple-element.77), channel_id=1, source_target_pairs={{0,4},{4,0},{8,12},{12,8},{16,20},{20,16},{24,28},{28,24},{1,5},{5... | collective-permute-start | bytes 2359304 | tf_op jit(solution)/shard_map/ppermute | solution.py:286
  171.7 36.7 %collective-permute-start.35 = (bf16[1,256,1024]{2,1,0:T(8,128)(2,1)}, bf16[1,256,1024]{2,1,0:T(8,128)(2,1)S(1)}, u32[]{:S(2)}, u32[]{:S(2)}) collective-permute-start(bf16[1,256,1024]{2,1,0:T(8,128)(2,1)} %get-tuple-element.82), channel_id=1, source_target_pairs={{0,16},{4,20},{8,24},{12,28},{16,0},{20,4},{24,8},{28,12},{1,17},{... | collective-permute-start | bytes 1572872 | tf_op jit(solution)/shard_map/ppermute | solution.py:286
  190.6 29.0 %collective-permute-start.34 = (bf16[1,256,1024]{2,1,0:T(8,128)(2,1)}, bf16[1,256,1024]{2,1,0:T(8,128)(2,1)}, u32[]{:S(2)}, u32[]{:S(2)}) collective-permute-start(bf16[1,256,1024]{2,1,0:T(8,128)(2,1)} %get-tuple-element.80), channel_id=1, source_target_pairs={{0,16},{4,20},{8,24},{12,28},{16,0},{20,4},{24,8},{28,12},{1,17},{... | collective-permute-start | bytes 1572872 | tf_op jit(solution)/shard_map/ppermute | solution.py:286
  (38 other events, 484.9 us)

commit v4 on v3

--- a/solution.py
+++ b/solution.py
@@ -12,8 +12,13 @@
 F32 = jnp.float32
 BF16 = jnp.bfloat16
 CHUNKS = (4, 4)
+SPLIT = (2, 2)
+GATES = {("M", 2): (0,)}
+HM = 2
 HEAVY = 1e11
 EARLY_JOINED = True
+MAX_STEP = 512
+SECOND = 8e9
 
 
 def params(mib=16):
@@ -109,12 +114,12 @@
             keep_ref[0, k // 4] = block
 
 
-def product(place, pieces, integrals, first, cols, cap):
+def product(place, pieces, integrals, first, cols, cap, flops):
     lhs = [piece[0] for piece in pieces]
     layout = tuple(piece[1:] for piece in pieces)
     experts, width, _ = integrals.shape
     half = sum(x.shape[0] for x, rel, _ in pieces if rel == 0) // 2
-    step = math.gcd(first, cols) if first else cols
+    step = math.gcd(first, cols, MAX_STEP)
     base, steps = first // step, cols // step
     out = pl.BlockSpec((1, half, cap, step), lambda t, s: (t // steps, 0, 0, t % steps))
     shape = (experts, half, cap, cols)
@@ -132,7 +137,7 @@
         ),
         out_shape=[jax.ShapeDtypeStruct(shape, F32), jax.ShapeDtypeStruct(shape, BF16)],
         compiler_params=params(36),
-        cost_estimate=cost(HEAVY, 2 * experts * width * cols),
+        cost_estimate=cost(flops, 0),
         name="tile_products",
     )(place, *lhs, integrals)
 
@@ -172,7 +177,7 @@
         send_ref[0] = encode(dense)
 
 
-def merge(place, inv, keep, got, near):
+def merge(place, inv, keep, got, near, at=0, flops=0):
     _, half, cap, cols = keep.shape
     rows = inv.shape[1]
     odd = near is None
@@ -190,12 +195,12 @@
             grid=(half,),
             in_specs=[pl.BlockSpec((1, rows, 4), lambda i, s: (2 * i + odd, 0, 0))]
             + [spec(0), spec(1)] * 2
-            + [each] * (not odd),
+            + [pl.BlockSpec((1, rows, cols), lambda i, s: (i, 0, at))] * (not odd),
             out_specs=each if odd else [second, second],
         ),
         out_shape=jax.ShapeDtypeStruct((half, rows, cols), BF16) if odd else [shape(F32), shape(BF16)],
         compiler_params=params(),
-        cost_estimate=cost(0, 0),
+        cost_estimate=cost(flops, 0),
         name="merge_rows",
     )(place, inv, keep, keep, got, got, *([] if odd else [near]))
 
@@ -342,24 +347,28 @@
     unit = cols // sum(CHUNKS)
     spans = [(unit * sum(CHUNKS[:j]), unit * size) for j, size in enumerate(CHUNKS)]
     count = len(spans)
+    cuts, near_of = [], []
+    for j, ((first, size), n) in enumerate(zip(spans, SPLIT)):
+        cuts += [(first + i * size // n, size // n) for i in range(n)]
+        near_of += [(j, i) for i in range(n)]
     levels = groups.bit_length() - 1
     made, moved, near, state = {}, {}, {}, {}
-    done, hops = [], []
-
-    def make(pieces, j, *waits):
-        at = after(place, *done[-1:], *hops[-2:-1], *waits)
-        kept, sent = product(at, pieces, integrals, *spans[j], cap)
-        made[j], moved[j] = kept, hop(sent, 1)
-        hops.append(moved[j])
+    done = []
+
+    def make(pieces, span, key, *waits, flops=HEAVY):
+        at = after(place, *done[-1:], *waits)
+        kept, sent = product(at, pieces, integrals, *span, cap, flops)
+        made[key], moved[key] = kept, hop(sent, 1)
         done.append(kept)
 
-    def first_rows(j):
-        sent = merge(after(place, *done[-1:]), inv, made[j], moved[j], None)
+    def first_rows(j, *waits):
+        sent = merge(after(place, *done[-1:], *waits), inv, made["early", j], moved["early", j], None)
         near[j] = hop(sent, 2)
         done.append(sent)
 
-    def second_rows(j):
-        kept, sent = merge(after(place, *done[-1:]), inv, made[j], moved[j], near[j])
+    def second_rows(j, *waits):
+        at = after(place, *done[-1:], *waits)
+        kept, sent = merge(at, inv, made["late", j], moved["late", j], near[near_of[j][0]], near_of[j][1], HEAVY if j >= HM else 0)
         state[j] = (kept, hop(sent, 4))
         done.append(kept)
 
@@ -387,23 +396,24 @@
     share(close[last - 1])
     share(far[last - 1])
     pieces = gather(rows_early, EARLY_JOINED)
-    make(pieces, 0)
+    make(pieces, spans[0], ("early", 0))
     waits = [held[far[last]][0], *shared[-2:]]
     for j in range(1, count):
-        make(pieces, j, *waits)
+        make(pieces, spans[j], ("early", j), *waits)
         if j == 1:
             share(far[last])
         waits = shared[-1:]
         first_rows(j - 1)
-    pieces = gather(rows_late, False, made[1])
-    make(pieces, 0)
+    pieces = gather(rows_late, False, made["early", 1])
+    make(pieces, cuts[0], ("late", 0))
+    make(pieces, cuts[1], ("late", 1), flops=SECOND)
     first_rows(count - 1)
-    for j in range(count):
-        if j + 1 < count:
-            make(pieces, j + 1, near[j])
-        second_rows(j)
+    for j in range(len(cuts)):
+        second_rows(j, *[state[i][1] for i in GATES.get(("M", j), ())])
+        if j + 2 < len(cuts):
+            make(pieces, cuts[j + 2], ("late", j + 2), *[state[i][1] for i in GATES.get(("P", j + 2), ())])
     for level in range(2, levels):
-        for j in range(count):
+        for j in range(len(cuts)):
             more_rows(j, level)
 
     tile = virt_first.shape[1]
@@ -418,9 +428,9 @@
     energy_i = lax.dynamic_slice_in_dim(occ_first, pair * (rows // per_i), rows // per_i, 0)
     occ_sum = (energy_i[:, None] + occ_second[None, :]).reshape(rows, 1)
     out = None
-    for j, (first, _) in enumerate(spans):
+    for j, (first, size) in enumerate(cuts):
         own = after(state[j][0], *done[-1:])
-        out = finish(own, state[j][1], other, occ_sum, virt_sum, first, unit, out)
+        out = finish(own, state[j][1], other, occ_sum, virt_sum, first, size // 2, out)
     return out
 
 

time: 224 us -> 216 us (0.964)
  waiting for transfers between devices: 77.8 us -> 45.3 us
  starting transfers between devices: 41.6 us -> 55.7 us
  Pallas kernels: 80 us -> 89.2 us
    ppermute x18 -> x22, waiting for transfers between devices: 72.9 us -> 37.7 us  [hop(): return lax.ppermute(x, 'pair', [(i, i ^ bits) for i in range(n_pair)])]
    ppermute x18 -> x22, starting transfers between devices: 32.4 us -> 45.3 us  [hop(): return lax.ppermute(x, 'pair', [(i, i ^ bits) for i in range(n_pair)])]
    pallas_call x4 -> x6, Pallas kernels: 49.8 us -> 54.7 us  [product(): pl.pallas_call(functools.partial(product_kernel, layout), grid_spec=pltpu...]
    pallas_call x4 -> x6, Pallas kernels: 18.4 us -> 22.1 us  [merge(): pl.pallas_call(merge_kernel, grid_spec=pltpu.PrefetchScalarGridSpec(num_s...]
    ppermute x18, waiting for transfers between devices: 4.85 us -> 7.56 us  [swap(): return lax.ppermute(x, 'virt', [(i, i ^ bits) for i in range(n_virt)])]
    pallas_call x2 -> x4, Pallas kernels: 5.83 us -> 6.58 us  [finish(): pl.pallas_call(finish_kernel, grid=(cols // step,), in_specs=[here, here,...]
    unnamed x59 -> x81, local copies, waits for them, and re-layouts: 15.3 us -> 15.5 us
  transfers between devices with their start and end apart: 36 -> 40, of which waited for: 14 -> 13; matrix products, arithmetic and copies ran while one was open for 4% -> 5% of each run, Pallas kernels for 33% -> 39%
where the time goes in v4:
time: 216 us
  Pallas kernels  89.2 us (41%)
  starting transfers between devices  55.7 us (26%)
  waiting for transfers between devices  45.3 us (21%)
  local copies, waits for them, and re-layouts  21.6 us (10%)
  matrix products  2.16 us (1%)
    pallas_call x6, Pallas kernels, product(): pl.pallas_call(functools.partial(product_kernel, layout), grid_spec=pltpu...  54.7 us
    ppermute x22, starting transfers between devices, hop(): return lax.ppermute(x, 'pair', [(i, i ^ bits) for i in range(n_pair)])  45.3 us
    ppermute x22, waiting for transfers between devices, hop(): return lax.ppermute(x, 'pair', [(i, i ^ bits) for i in range(n_pair)])  37.7 us
    pallas_call x6, Pallas kernels, merge(): pl.pallas_call(merge_kernel, grid_spec=pltpu.PrefetchScalarGridSpec(num_s...  22.1 us
    unnamed x81, local copies, waits for them, and re-layouts  15.5 us
    ppermute x18, starting transfers between devices, swap(): return lax.ppermute(x, 'virt', [(i, i ^ bits) for i in range(n_virt)])  10.4 us
    ppermute x18, waiting for transfers between devices, swap(): return lax.ppermute(x, 'virt', [(i, i ^ bits) for i in range(n_virt)])  7.56 us
    pallas_call x4, Pallas kernels, finish(): pl.pallas_call(finish_kernel, grid=(cols // step,), in_specs=[here, here,...  6.58 us
  transfers between devices with their start and end apart: 40, of which 13 were waited for; matrix products, arithmetic and copies ran while one was open for 5% of the time, Pallas kernels for 39%

profile of v4, /device:TPU:0, one launch (start us, length us, event | category | flops | bytes accessed | tf_op | source)
XLA Modules:
  0.0 215.6 jit_solution(12256632846507636182)
XLA Ops:
  3.1 3.1 %pack_tiles.1 = (bf16[192,1024]{1,0:T(8,128)(2,1)}, bf16[192,1024]{1,0:T(8,128)(2,1)}, bf16[192,1024]{1,0:T(8,128)(2,1)S(1)}, bf16[192,1024]{1,0:T(8,128)(2,1)S(...) custom-call(s32[3,256]{1,0:T(4,128)S(1)} %fusion.26.codes_ref, ...), custom_call_target="tpu_custom_call" | custom-call | tf_op jit(solution)/shard_map/pack_tiles/pallas_call | solution.py:86
  7.0 3.0 %collective-permute-start.1 = (bf16[192,1024]{1,0:T(8,128)(2,1)S(1)}, bf16[192,1024]{1,0:T(8,128)(2,1)S(1)}, u32[]{:S(2)}, u32[]{:S(2)}) collective-permute-start(bf16[192,1024]{1,0:T(8,128)(2,1)S(1)} %get-tuple-element.59), channel_id=1, source_target_pairs={{0,8},{4,12},{8,0},{12,4},{16,24},{20,28},{24,16},{28,20},{1,9},{5... | collective-permute-start | bytes 1179656 | tf_op jit(solution)/shard_map/ppermute | solution.py:291
  15.4 4.2 %collective-permute-done.1 = bf16[192,1024]{1,0:T(8,128)(2,1)S(1)} collective-permute-done((bf16[192,1024]{1,0:T(8,128)(2,1)S(1)}, bf16[192,1024]{1,0:T(8,128)(2,1)S(1)}, u32[]{:S(2)}, u32[]{:S(2)}) %collective-permute-start.1) | collective-permute-done | bytes 393248 | tf_op jit(solution)/shard_map/ppermute | solution.py:291
  22.0 9.9 %collective-permute-start.8 = (s32[3,256]{1,0:T(4,128)S(1)}, s32[3,256]{1,0:T(4,128)S(1)}, u32[]{:S(2)}, u32[]{:S(2)}) collective-permute-start(s32[3,256]{1,0:T(4,128)S(1)} %bitcast.73), channel_id=1, source_target_pairs={{0,16},{4,20},{8,24},{12,28},{16,0},{20,4},{24,8},{28,12},{1,17},{... | collective-permute-start | bytes 9224 | tf_op jit(solution)/shard_map/ppermute | solution.py:291
  36.3 3.4 %collective-permute-start.3 = (bf16[192,1024]{1,0:T(8,128)(2,1)S(1)}, bf16[192,1024]{1,0:T(8,128)(2,1)}, u32[]{:S(2)}, u32[]{:S(2)}) collective-permute-start(bf16[192,1024]{1,0:T(8,128)(2,1)S(1)} %get-tuple-element.63), channel_id=1, source_target_pairs={{0,28},{4,24},{8,20},{12,16},{16,12},{20,8},{24,4},{28,0},{1,29},{... | collective-permute-start | bytes 1179656 | tf_op jit(solution)/shard_map/ppermute | solution.py:291
  45.1 8.5 %collective-permute-done.3 = bf16[192,1024]{1,0:T(8,128)(2,1)} collective-permute-done((bf16[192,1024]{1,0:T(8,128)(2,1)S(1)}, bf16[192,1024]{1,0:T(8,128)(2,1)}, u32[]{:S(2)}, u32[]{:S(2)}) %collective-permute-start.3) | collective-permute-done | bytes 393248 | tf_op jit(solution)/shard_map/ppermute | solution.py:291
  58.3 3.6 %collective-permute-start.10 = (bf16[192,1024]{1,0:T(8,128)(2,1)}, bf16[192,1024]{1,0:T(8,128)(2,1)}, u32[]{:S(2)}, u32[]{:S(2)}) collective-permute-start(bf16[192,1024]{1,0:T(8,128)(2,1)} %get-tuple-element.69), channel_id=1, source_target_pairs={{0,16},{4,20},{8,24},{12,28},{16,0},{20,4},{24,8},{28,12},{1,17},{... | collective-permute-start | bytes 1179656 | tf_op jit(solution)/shard_map/ppermute | solution.py:291
  69.9 4.2 %collective-permute-done.13 = bf16[192,1024]{1,0:T(8,128)(2,1)S(1)} collective-permute-done((bf16[192,1024]{1,0:T(8,128)(2,1)}, bf16[192,1024]{1,0:T(8,128)(2,1)S(1)}, u32[]{:S(2)}, u32[]{:S(2)}) %collective-permute-start.13) | collective-permute-done | bytes 393248 | tf_op jit(solution)/shard_map/ppermute | solution.py:294
  80.3 12.0 %tile_products.6 = (f32[2,2,96,1024]{3,2,1,0:T(8,128)S(1)}, bf16[2,2,96,1024]{3,2,1,0:T(8,128)(2,1)S(1)}) custom-call(s32[1]{0:T(128)} %pin.5.place_ref, bf16[4,2,96,1024]{3,2,1,0:T(8,128)(2,1)S(1)} %bitcast.68, bf16[4,2,96,1024]{3,2,1,0:T(8,128)(2,1)} %bitcast.6.refs_1_, bf16[4,2,96,1024]{3,2,1,0:T(8,128)(2,1)S(1)} %bitcast.66, ...), custom_call_target="tpu_custom_call" | custom-call | flops 99999997952 | tf_op jit(solution)/shard_map/tile_products/pallas_call | solution.py:126
  92.3 5.2 %collective-permute-done.16 = bf16[192,1024]{1,0:T(8,128)(2,1)} collective-permute-done((bf16[192,1024]{1,0:T(8,128)(2,1)}, bf16[192,1024]{1,0:T(8,128)(2,1)}, u32[]{:S(2)}, u32[]{:S(2)}) %collective-permute-start.16) | collective-permute-done | bytes 393248 | tf_op jit(solution)/shard_map/ppermute | solution.py:291
  102.2 11.9 %tile_products.7 = (f32[2,2,96,1024]{3,2,1,0:T(8,128)S(1)}, bf16[2,2,96,1024]{3,2,1,0:T(8,128)(2,1)S(1)}) custom-call(s32[1]{0:T(128)} %pin.5.place_ref, bf16[4,2,96,1024]{3,2,1,0:T(8,128)(2,1)S(1)} %bitcast.69, bf16[4,2,96,1024]{3,2,1,0:T(8,128)(2,1)} %bitcast.6.refs_1_, bf16[4,2,96,1024]{3,2,1,0:T(8,128)(2,1)S(1)} %bitcast.67, ...), custom_call_target="tpu_custom_call" | custom-call | flops 99999997952 | tf_op jit(solution)/shard_map/tile_products/pallas_call | solution.py:126
  119.9 3.3 %merge_rows.6 = bf16[2,256,1024]{2,1,0:T(8,128)(2,1)S(1)} custom-call(s32[1]{0:T(128)} %pin.5.place_ref, s32[4,256,4]{2,1,0:T(8,128)S(1)} %copy.16.inv_ref, f32[2,2,96,1024]{3,2,1,0:T(8,128)S(1)} %copy-done.4, f32[2,2,96,1024]{3,2,1,0:T(8,128)S(1)} %copy-done.4, bf16[2,2,96,1024]{3,2,1,0:T(8,128)(2,1)S(1)} %collective-permute-done.19.got0.got1, ...), custom_call_target="tpu_custom_call" | custom-call | tf_op jit(solution)/shard_map/merge_rows/pallas_call | solution.py:191
  125.9 7.6 %tile_products.8 = (f32[2,2,96,512]{3,2,1,0:T(8,128)S(1)}, bf16[2,2,96,512]{3,2,1,0:T(8,128)(2,1)S(1)}) custom-call(s32[1]{0:T(128)} %pin.5.place_ref, bf16[1,2,96,1024]{3,2,1,0:T(8,128)(2,1)} %bitcast.15.refs_0_, bf16[1,2,96,1024]{3,2,1,0:T(8,128)(2,1)} %bitcast.16.refs_1_, bf16[1,2,96,1024]{3,2,1,0:T(8,128)(2,1)} %bitcast.17.refs_2_, ...), custom_call_target="tpu_custom_call" | custom-call | flops 99999997952 | tf_op jit(solution)/shard_map/tile_products/pallas_call | solution.py:126
  135.3 7.6 %tile_products.9 = (f32[2,2,96,512]{3,2,1,0:T(8,128)S(1)}, bf16[2,2,96,512]{3,2,1,0:T(8,128)(2,1)S(1)}) custom-call(s32[1]{0:T(128)} %pin.5.place_ref, bf16[1,2,96,1024]{3,2,1,0:T(8,128)(2,1)} %bitcast.15.refs_0_, bf16[1,2,96,1024]{3,2,1,0:T(8,128)(2,1)} %bitcast.16.refs_1_, bf16[1,2,96,1024]{3,2,1,0:T(8,128)(2,1)} %bitcast.17.refs_2_, ...), custom_call_target="tpu_custom_call" | custom-call | flops 8000000000 | tf_op jit(solution)/shard_map/tile_products/pallas_call | solution.py:126
  143.6 4.0 %merge_rows.7 = bf16[2,256,1024]{2,1,0:T(8,128)(2,1)} custom-call(s32[1]{0:T(128)} %pin.5.place_ref, s32[4,256,4]{2,1,0:T(8,128)S(1)} %copy.16.inv_ref, f32[2,2,96,1024]{3,2,1,0:T(8,128)S(1)} %get-tuple-element.77.keep0.keep1, f32[2,2,96,1024]{3,2,1,0:T(8,128)S(1)} %get-tuple-element.77.keep0.keep1, ...), custom_call_target="tpu_custom_call" | custom-call | tf_op jit(solution)/shard_map/merge_rows/pallas_call | solution.py:191
  154.7 7.6 %tile_products.10 = (f32[2,2,96,512]{3,2,1,0:T(8,128)S(1)}, bf16[2,2,96,512]{3,2,1,0:T(8,128)(2,1)S(1)}) custom-call(s32[1]{0:T(128)} %pin.5.place_ref, bf16[1,2,96,1024]{3,2,1,0:T(8,128)(2,1)} %bitcast.15.refs_0_, bf16[1,2,96,1024]{3,2,1,0:T(8,128)(2,1)} %bitcast.16.refs_1_, bf16[1,2,96,1024]{3,2,1,0:T(8,128)(2,1)} %bitcast.17.refs_2_, ...), custom_call_target="tpu_custom_call" | custom-call | flops 99999997952 | tf_op jit(solution)/shard_map/tile_products/pallas_call | solution.py:126
  162.3 3.4 %merge_rows.9 = (f32[1,256,512]{2,1,0:T(8,128)S(1)}, bf16[1,256,512]{2,1,0:T(8,128)(2,1)}) custom-call(s32[1]{0:T(128)} %pin.5.place_ref, s32[4,256,4]{2,1,0:T(8,128)S(1)} %copy.16.inv_ref, f32[2,2,96,512]{3,2,1,0:T(8,128)S(1)} %get-tuple-element.84.keep0.keep1, f32[2,2,96,512]{3,2,1,0:T(8,128)S(1)} %get-tuple-element.84.keep0.keep1, ...), custom_call_target="tpu_custom_call" | custom-call | tf_op jit(solution)/shard_map/merge_rows/pallas_call | solution.py:191
  167.7 7.8 %tile_products.11 = (f32[2,2,96,512]{3,2,1,0:T(8,128)S(1)}, bf16[2,2,96,512]{3,2,1,0:T(8,128)(2,1)S(1)}) custom-call(s32[1]{0:T(128)} %pin.5.place_ref, bf16[1,2,96,1024]{3,2,1,0:T(8,128)(2,1)} %bitcast.15.refs_0_, bf16[1,2,96,1024]{3,2,1,0:T(8,128)(2,1)} %bitcast.16.refs_1_, bf16[1,2,96,1024]{3,2,1,0:T(8,128)(2,1)} %bitcast.17.refs_2_, ...), custom_call_target="tpu_custom_call" | custom-call | flops 99999997952 | tf_op jit(solution)/shard_map/tile_products/pallas_call | solution.py:126
  176.5 2.9 %collective-permute-start.39 = (bf16[1,256,512]{2,1,0:T(8,128)(2,1)}, bf16[1,256,512]{2,1,0:T(8,128)(2,1)}, u32[]{:S(2)}, u32[]{:S(2)}) collective-permute-start(bf16[1,256,512]{2,1,0:T(8,128)(2,1)} %get-tuple-element.109), channel_id=1, source_target_pairs={{0,16},{4,20},{8,24},{12,28},{16,0},{20,4},{24,8},{28,12},{1,17},{... | collective-permute-start | bytes 786440 | tf_op jit(solution)/shard_map/ppermute | solution.py:291
  179.4 8.2 %collective-permute-done.33.got_ref = bf16[1,256,512]{2,1,0:T(8,128)(2,1)S(1)} collective-permute-done((bf16[1,256,512]{2,1,0:T(8,128)(2,1)S(1)}, bf16[1,256,512]{2,1,0:T(8,128)(2,1)S(1)}, u32[]{:S(2)}, u32[]{:S(2)}) %collective-permute-start.33) | collective-permute-done | bytes 262176 | tf_op jit(solution)/shard_map/ppermute | solution.py:291
  187.6 4.3 %merge_rows.10 = (f32[1,256,512]{2,1,0:T(8,128)S(1)}, bf16[1,256,512]{2,1,0:T(8,128)(2,1)}) custom-call(s32[1]{0:T(128)} %pin.5.place_ref, s32[4,256,4]{2,1,0:T(8,128)S(1)} %copy.16.inv_ref, f32[2,2,96,512]{3,2,1,0:T(8,128)S(1)} %get-tuple-element.91.keep0.keep1, f32[2,2,96,512]{3,2,1,0:T(8,128)S(1)} %get-tuple-element.91.keep0.keep1, ...), custom_call_target="tpu_custom_call" | custom-call | flops 99999997952 | tf_op jit(solution)/shard_map/merge_rows/pallas_call | solution.py:191
  192.8 4.4 %merge_rows.11 = (f32[1,256,512]{2,1,0:T(8,128)S(1)}, bf16[1,256,512]{2,1,0:T(8,128)(2,1)}) custom-call(s32[1]{0:T(128)} %pin.5.place_ref, s32[4,256,4]{2,1,0:T(8,128)S(1)} %copy.16.inv_ref, f32[2,2,96,512]{3,2,1,0:T(8,128)S(1)} %get-tuple-element.96.keep0.keep1, f32[2,2,96,512]{3,2,1,0:T(8,128)S(1)} %get-tuple-element.96.keep0.keep1, ...), custom_call_target="tpu_custom_call" | custom-call | flops 99999997952 | tf_op jit(solution)/shard_map/merge_rows/pallas_call | solution.py:191
  198.1 2.9 %collective-permute-start.37 = (bf16[1,256,512]{2,1,0:T(8,128)(2,1)}, bf16[1,256,512]{2,1,0:T(8,128)(2,1)S(1)}, u32[]{:S(2)}, u32[]{:S(2)}) collective-permute-start(bf16[1,256,512]{2,1,0:T(8,128)(2,1)} %get-tuple-element.105), channel_id=1, source_target_pairs={{0,16},{4,20},{8,24},{12,28},{16,0},{20,4},{24,8},{28,12},{1,17},{... | collective-permute-start | bytes 786440 | tf_op jit(solution)/shard_map/ppermute | solution.py:291
  209.4 4.9 %collective-permute-done.37.got_ref = bf16[1,256,512]{2,1,0:T(8,128)(2,1)S(1)} collective-permute-done((bf16[1,256,512]{2,1,0:T(8,128)(2,1)}, bf16[1,256,512]{2,1,0:T(8,128)(2,1)S(1)}, u32[]{:S(2)}, u32[]{:S(2)}) %collective-permute-start.37) | collective-permute-done | bytes 262176 | tf_op jit(solution)/shard_map/ppermute | solution.py:291
  (185 shorter events, 76.8 us)
Async XLA Ops:
  10.0 21.9 %collective-permute-start.2 = (bf16[192,1024]{1,0:T(8,128)(2,1)}, bf16[192,1024]{1,0:T(8,128)(2,1)}, u32[]{:S(2)}, u32[]{:S(2)}) collective-permute-start(bf16[192,1024]{1,0:T(8,128)(2,1)} %get-tuple-element.60), channel_id=1, source_target_pairs={{0,2},{1,3},{2,0},{3,1},{4,6},{5,7},{6,4},{7,5},{8,10},{9,11},{10,... | collective-permute-start | bytes 1179656 | tf_op jit(solution)/shard_map/ppermute | solution.py:294
  11.6 20.4 %collective-permute-start = (bf16[192,1024]{1,0:T(8,128)(2,1)S(1)}, bf16[192,1024]{1,0:T(8,128)(2,1)S(1)}, u32[]{:S(2)}, u32[]{:S(2)}) collective-permute-start(bf16[192,1024]{1,0:T(8,128)(2,1)S(1)} %get-tuple-element.58), channel_id=1, source_target_pairs={{0,24},{4,28},{8,16},{12,20},{16,8},{20,12},{24,0},{28,4},{1,25},{... | collective-permute-start | bytes 1179656 | tf_op jit(solution)/shard_map/ppermute | solution.py:291
  14.0 101.2 %collective-permute-start.20 = (bf16[192,1024]{1,0:T(8,128)(2,1)}, bf16[192,1024]{1,0:T(8,128)(2,1)}, u32[]{:S(2)}, u32[]{:S(2)}) collective-permute-start(bf16[192,1024]{1,0:T(8,128)(2,1)} %get-tuple-element.60), channel_id=1, source_target_pairs={{0,1},{1,0},{2,3},{3,2},{4,5},{5,4},{6,7},{7,6},{8,9},{9,8},{10,11... | collective-permute-start | bytes 1179656 | tf_op jit(solution)/shard_map/ppermute | solution.py:294
  19.6 16.7 %collective-permute-start.7 = (s32[3,256]{1,0:T(4,128)S(1)}, s32[3,256]{1,0:T(4,128)S(1)}, u32[]{:S(2)}, u32[]{:S(2)}) collective-permute-start(s32[3,256]{1,0:T(4,128)S(1)} %bitcast.72), channel_id=1, source_target_pairs={{0,8},{4,12},{8,0},{12,4},{16,24},{20,28},{24,16},{28,20},{1,9},{5... | collective-permute-start | bytes 9224 | tf_op jit(solution)/shard_map/ppermute | solution.py:291
  22.0 17.7 %collective-permute-start.8 = (s32[3,256]{1,0:T(4,128)S(1)}, s32[3,256]{1,0:T(4,128)S(1)}, u32[]{:S(2)}, u32[]{:S(2)}) collective-permute-start(s32[3,256]{1,0:T(4,128)S(1)} %bitcast.73), channel_id=1, source_target_pairs={{0,16},{4,20},{8,24},{12,28},{16,0},{20,4},{24,8},{28,12},{1,17},{... | collective-permute-start | bytes 9224 | tf_op jit(solution)/shard_map/ppermute | solution.py:291
  36.3 17.3 %collective-permute-start.3 = (bf16[192,1024]{1,0:T(8,128)(2,1)S(1)}, bf16[192,1024]{1,0:T(8,128)(2,1)}, u32[]{:S(2)}, u32[]{:S(2)}) collective-permute-start(bf16[192,1024]{1,0:T(8,128)(2,1)S(1)} %get-tuple-element.63), channel_id=1, source_target_pairs={{0,28},{4,24},{8,20},{12,16},{16,12},{20,8},{24,4},{28,0},{1,29},{... | collective-permute-start | bytes 1179656 | tf_op jit(solution)/shard_map/ppermute | solution.py:291
  41.3 14.3 %collective-permute-start.6 = (bf16[192,1024]{1,0:T(8,128)(2,1)S(1)}, bf16[192,1024]{1,0:T(8,128)(2,1)}, u32[]{:S(2)}, u32[]{:S(2)}) collective-permute-start(bf16[192,1024]{1,0:T(8,128)(2,1)S(1)} %copy-done.27), channel_id=1, source_target_pairs={{0,2},{1,3},{2,0},{3,1},{4,6},{5,7},{6,4},{7,5},{8,10},{9,11},{10,... | collective-permute-start | bytes 1179656 | tf_op jit(solution)/shard_map/ppermute | solution.py:294
  68.1 47.5 %collective-permute-start.21 = (bf16[192,1024]{1,0:T(8,128)(2,1)}, bf16[192,1024]{1,0:T(8,128)(2,1)}, u32[]{:S(2)}, u32[]{:S(2)}) collective-permute-start(bf16[192,1024]{1,0:T(8,128)(2,1)} %collective-permute-done.2), channel_id=1, source_target_pairs={{0,1},{1,0},{2,3},{3,2},{4,5},{5,4},{6,7},{7,6},{8,9},{9,8},{10,11... | collective-permute-start | bytes 1179656 | tf_op jit(solution)/shard_map/ppermute | solution.py:294
  75.4 22.1 %collective-permute-start.16 = (bf16[192,1024]{1,0:T(8,128)(2,1)}, bf16[192,1024]{1,0:T(8,128)(2,1)}, u32[]{:S(2)}, u32[]{:S(2)}) collective-permute-start(bf16[192,1024]{1,0:T(8,128)(2,1)} %copy-done.23), channel_id=1, source_target_pairs={{0,20},{4,16},{8,28},{12,24},{16,4},{20,0},{24,12},{28,8},{1,21},{... | collective-permute-start | bytes 1179656 | tf_op jit(solution)/shard_map/ppermute | solution.py:291
  77.9 19.7 %collective-permute-start.17 = (bf16[192,1024]{1,0:T(8,128)(2,1)S(1)}, bf16[192,1024]{1,0:T(8,128)(2,1)}, u32[]{:S(2)}, u32[]{:S(2)}) collective-permute-start(bf16[192,1024]{1,0:T(8,128)(2,1)S(1)} %collective-permute-done.11), channel_id=1, source_target_pairs={{0,2},{1,3},{2,0},{3,1},{4,6},{5,7},{6,4},{7,5},{8,10},{9,11},{10,... | collective-permute-start | bytes 1179656 | tf_op jit(solution)/shard_map/ppermute | solution.py:294
  78.2 20.3 %collective-permute-start.18 = (bf16[192,1024]{1,0:T(8,128)(2,1)}, bf16[192,1024]{1,0:T(8,128)(2,1)}, u32[]{:S(2)}, u32[]{:S(2)}) collective-permute-start(bf16[192,1024]{1,0:T(8,128)(2,1)} %collective-permute-done.10), channel_id=1, source_target_pairs={{0,2},{1,3},{2,0},{3,1},{4,6},{5,7},{6,4},{7,5},{8,10},{9,11},{10,... | collective-permute-start | bytes 1179656 | tf_op jit(solution)/shard_map/ppermute | solution.py:294
  97.5 18.2 %collective-permute-start.24 = (bf16[192,1024]{1,0:T(8,128)(2,1)S(1)}, bf16[192,1024]{1,0:T(8,128)(2,1)S(1)}, u32[]{:S(2)}, u32[]{:S(2)}) collective-permute-start(bf16[192,1024]{1,0:T(8,128)(2,1)S(1)} %collective-permute-done.11), channel_id=1, source_target_pairs={{0,1},{1,0},{2,3},{3,2},{4,5},{5,4},{6,7},{7,6},{8,9},{9,8},{10,11... | collective-permute-start | bytes 1179656 | tf_op jit(solution)/shard_map/ppermute | solution.py:294
  97.5 17.5 %collective-permute-start.27 = (bf16[192,1024]{1,0:T(8,128)(2,1)}, bf16[192,1024]{1,0:T(8,128)(2,1)}, u32[]{:S(2)}, u32[]{:S(2)}) collective-permute-start(bf16[192,1024]{1,0:T(8,128)(2,1)} %collective-permute-done.16), channel_id=1, source_target_pairs={{0,2},{1,3},{2,0},{3,1},{4,6},{5,7},{6,4},{7,5},{8,10},{9,11},{10,... | collective-permute-start | bytes 1179656 | tf_op jit(solution)/shard_map/ppermute | solution.py:294
  98.5 19.7 %collective-permute-start.19 = (bf16[2,2,96,1024]{3,2,1,0:T(8,128)(2,1)S(1)}, bf16[2,2,96,1024]{3,2,1,0:T(8,128)(2,1)S(1)}, u32[]{:S(2)}, u32[]{:S(2)}) collective-permute-start(bf16[2,2,96,1024]{3,2,1,0:T(8,128)(2,1)S(1)} %get-tuple-element.79), channel_id=1, source_target_pairs={{0,4},{4,0},{8,12},{12,8},{16,20},{20,16},{24,28},{28,24},{1,5},{5... | collective-permute-start | bytes 2359304 | tf_op jit(solution)/shard_map/ppermute | solution.py:291
  123.2 20.4 %collective-permute-start.29 = (bf16[2,2,96,1024]{3,2,1,0:T(8,128)(2,1)S(1)}, bf16[2,2,96,1024]{3,2,1,0:T(8,128)(2,1)S(1)}, u32[]{:S(2)}, u32[]{:S(2)}) collective-permute-start(bf16[2,2,96,1024]{3,2,1,0:T(8,128)(2,1)S(1)} %copy-done.22), channel_id=1, source_target_pairs={{0,4},{4,0},{8,12},{12,8},{16,20},{20,16},{24,28},{28,24},{1,5},{5... | collective-permute-start | bytes 2359304 | tf_op jit(solution)/shard_map/ppermute | solution.py:291
  124.4 27.6 %collective-permute-start.31 = (bf16[2,256,1024]{2,1,0:T(8,128)(2,1)S(1)}, bf16[2,256,1024]{2,1,0:T(8,128)(2,1)S(1)}, u32[]{:S(2)}, u32[]{:S(2)}) collective-permute-start(bf16[2,256,1024]{2,1,0:T(8,128)(2,1)S(1)} %merge_rows.6), channel_id=1, source_target_pairs={{0,8},{4,12},{8,0},{12,4},{16,24},{20,28},{24,16},{28,20},{1,9},{5... | collective-permute-start | bytes 3145736 | tf_op jit(solution)/shard_map/ppermute | solution.py:291
  133.5 18.5 %collective-permute-start.30 = (bf16[2,2,96,512]{3,2,1,0:T(8,128)(2,1)S(1)}, bf16[2,2,96,512]{3,2,1,0:T(8,128)(2,1)S(1)}, u32[]{:S(2)}, u32[]{:S(2)}) collective-permute-start(bf16[2,2,96,512]{3,2,1,0:T(8,128)(2,1)S(1)} %get-tuple-element.88), channel_id=1, source_target_pairs={{0,4},{4,0},{8,12},{12,8},{16,20},{20,16},{24,28},{28,24},{1,5},{5... | collective-permute-start | bytes 1179656 | tf_op jit(solution)/shard_map/ppermute | solution.py:291
  147.6 40.0 %collective-permute-start.35 = (bf16[2,256,1024]{2,1,0:T(8,128)(2,1)}, bf16[2,256,1024]{2,1,0:T(8,128)(2,1)}, u32[]{:S(2)}, u32[]{:S(2)}) collective-permute-start(bf16[2,256,1024]{2,1,0:T(8,128)(2,1)} %merge_rows.7), channel_id=1, source_target_pairs={{0,8},{4,12},{8,0},{12,4},{16,24},{20,28},{24,16},{28,20},{1,9},{5... | collective-permute-start | bytes 3145736 | tf_op jit(solution)/shard_map/ppermute | solution.py:291
  166.5 21.1 %collective-permute-start.33 = (bf16[1,256,512]{2,1,0:T(8,128)(2,1)S(1)}, bf16[1,256,512]{2,1,0:T(8,128)(2,1)S(1)}, u32[]{:S(2)}, u32[]{:S(2)}) collective-permute-start(bf16[1,256,512]{2,1,0:T(8,128)(2,1)S(1)} %get-tuple-element.97), channel_id=1, source_target_pairs={{0,16},{4,20},{8,24},{12,28},{16,0},{20,4},{24,8},{28,12},{1,17},{... | collective-permute-start | bytes 786440 | tf_op jit(solution)/shard_map/ppermute | solution.py:291
  166.5 21.1 %collective-permute-start.34 = (bf16[2,2,96,512]{3,2,1,0:T(8,128)(2,1)S(1)}, bf16[2,2,96,512]{3,2,1,0:T(8,128)(2,1)S(1)}, u32[]{:S(2)}, u32[]{:S(2)}) collective-permute-start(bf16[2,2,96,512]{3,2,1,0:T(8,128)(2,1)S(1)} %get-tuple-element.99), channel_id=1, source_target_pairs={{0,4},{4,0},{8,12},{12,8},{16,20},{20,16},{24,28},{28,24},{1,5},{5... | collective-permute-start | bytes 1179656 | tf_op jit(solution)/shard_map/ppermute | solution.py:291
  175.5 17.3 %collective-permute-start.36 = (bf16[2,2,96,512]{3,2,1,0:T(8,128)(2,1)S(1)}, bf16[2,2,96,512]{3,2,1,0:T(8,128)(2,1)S(1)}, u32[]{:S(2)}, u32[]{:S(2)}) collective-permute-start(bf16[2,2,96,512]{3,2,1,0:T(8,128)(2,1)S(1)} %get-tuple-element.102), channel_id=1, source_target_pairs={{0,4},{4,0},{8,12},{12,8},{16,20},{20,16},{24,28},{28,24},{1,5},{5... | collective-permute-start | bytes 1179656 | tf_op jit(solution)/shard_map/ppermute | solution.py:291
  176.5 26.2 %collective-permute-start.39 = (bf16[1,256,512]{2,1,0:T(8,128)(2,1)}, bf16[1,256,512]{2,1,0:T(8,128)(2,1)}, u32[]{:S(2)}, u32[]{:S(2)}) collective-permute-start(bf16[1,256,512]{2,1,0:T(8,128)(2,1)} %get-tuple-element.109), channel_id=1, source_target_pairs={{0,16},{4,20},{8,24},{12,28},{16,0},{20,4},{24,8},{28,12},{1,17},{... | collective-permute-start | bytes 786440 | tf_op jit(solution)/shard_map/ppermute | solution.py:291
  192.7 14.6 %collective-permute-start.38 = (bf16[1,256,512]{2,1,0:T(8,128)(2,1)}, bf16[1,256,512]{2,1,0:T(8,128)(2,1)}, u32[]{:S(2)}, u32[]{:S(2)}) collective-permute-start(bf16[1,256,512]{2,1,0:T(8,128)(2,1)} %get-tuple-element.107), channel_id=1, source_target_pairs={{0,16},{4,20},{8,24},{12,28},{16,0},{20,4},{24,8},{28,12},{1,17},{... | collective-permute-start | bytes 786440 | tf_op jit(solution)/shard_map/ppermute | solution.py:291
  198.1 16.3 %collective-permute-start.37 = (bf16[1,256,512]{2,1,0:T(8,128)(2,1)}, bf16[1,256,512]{2,1,0:T(8,128)(2,1)S(1)}, u32[]{:S(2)}, u32[]{:S(2)}) collective-permute-start(bf16[1,256,512]{2,1,0:T(8,128)(2,1)} %get-tuple-element.105), channel_id=1, source_target_pairs={{0,16},{4,20},{8,24},{12,28},{16,0},{20,4},{24,8},{28,12},{1,17},{... | collective-permute-start | bytes 786440 | tf_op jit(solution)/shard_map/ppermute | solution.py:291
  (53 other events, 432.9 us)

commit v5 on v4

--- a/solution.py
+++ b/solution.py
@@ -142,26 +142,26 @@
     )(place, *lhs, integrals)
 
 
-def dense_rows(inv_ref, values):
-    rows = inv_ref.shape[1]
-    slots = values.shape[0]
-    cap = slots // 4
-    lane = lax.broadcasted_iota(jnp.int32, (rows, slots), 1)
+def placement(inv, cap):
+    lane = jnp.arange(4 * cap, dtype=jnp.int32)
     hit = None
     for c in range(4):
-        slot = inv_ref[0, :, c : c + 1]
+        slot = inv[:, :, c : c + 1]
         one = lane == jnp.where(slot < 0, -1, slot + c * cap)
         hit = one if hit is None else hit | one
-    pick = hit.astype(F32).astype(BF16)
+    return hit.astype(BF16)
+
+
+def dense_rows(pick, values):
     high = values.astype(BF16)
     low = (values - high.astype(F32)).astype(BF16)
     dense = jnp.dot(pick, high, preferred_element_type=F32)
     return dense + jnp.dot(pick, low, preferred_element_type=F32)
 
 
-def merge_kernel(place_ref, inv_ref, keep0, keep1, got0, got1, *refs):
+def merge_kernel(place_ref, pick_ref, keep0, keep1, got0, got1, *refs):
     values = [keep0[0, 0], keep1[0, 0], decode(got0[0, 0]), decode(got1[0, 0])]
-    dense = dense_rows(inv_ref, jnp.concatenate(values, axis=0))
+    dense = dense_rows(pick_ref[0], jnp.concatenate(values, axis=0))
     if len(refs) == 1:
         refs[0][0] = encode(dense)
         return
@@ -177,9 +177,9 @@
         send_ref[0] = encode(dense)
 
 
-def merge(place, inv, keep, got, near, at=0, flops=0):
+def merge(place, pick, keep, got, near, at=0, flops=0):
     _, half, cap, cols = keep.shape
-    rows = inv.shape[1]
+    rows = pick.shape[1]
     odd = near is None
 
     def spec(c):
@@ -193,7 +193,7 @@
         grid_spec=pltpu.PrefetchScalarGridSpec(
             num_scalar_prefetch=1,
             grid=(half,),
-            in_specs=[pl.BlockSpec((1, rows, 4), lambda i, s: (2 * i + odd, 0, 0))]
+            in_specs=[pl.BlockSpec((1, rows, 4 * cap), lambda i, s: (2 * i + odd, 0, 0))]
             + [spec(0), spec(1)] * 2
             + [pl.BlockSpec((1, rows, cols), lambda i, s: (i, 0, at))] * (not odd),
             out_specs=each if odd else [second, second],
@@ -202,7 +202,7 @@
         compiler_params=params(),
         cost_estimate=cost(flops, 0),
         name="merge_rows",
-    )(place, inv, keep, keep, got, got, *([] if odd else [near]))
+    )(place, pick, keep, keep, got, got, *([] if odd else [near]))
 
 
 def halve_kernel(kept_ref, got_ref, out_ref, send_ref):
@@ -342,7 +342,7 @@
     inv = jnp.sum(jnp.where(all_hot, all_rank + 1, 0), axis=1) - 1
     mine = lax.dynamic_slice_in_dim(inv, pair * cd_dev, cd_dev, 2)
     theirs = lax.dynamic_slice_in_dim(inv, lax.bitwise_xor(pair, 1) * cd_dev, cd_dev, 2)
-    inv = jnp.concatenate([mine, theirs], axis=2)
+    inv = placement(jnp.concatenate([mine, theirs], axis=2), cap)
 
     unit = cols // sum(CHUNKS)
     spans = [(unit * sum(CHUNKS[:j]), unit * size) for j, size in enumerate(CHUNKS)]

time: 216 us -> 213 us (0.986)
  local copies, waits for them, and re-layouts: 21.6 us -> 14.3 us
  waiting for transfers between devices: 45.3 us -> 49.3 us
  Pallas kernels: 89.2 us -> 86.5 us
    unnamed x81 -> x55, local copies, waits for them, and re-layouts: 15.5 us -> 7.69 us
    ppermute x22, waiting for transfers between devices: 37.7 us -> 44.7 us  [hop(): return lax.ppermute(x, 'pair', [(i, i ^ bits) for i in range(n_pair)])]
    ppermute x18, waiting for transfers between devices: 7.56 us -> 4.61 us  [swap(): return lax.ppermute(x, 'virt', [(i, i ^ bits) for i in range(n_virt)])]
    ppermute x22, starting transfers between devices: 45.3 us -> 48 us  [hop(): return lax.ppermute(x, 'pair', [(i, i ^ bits) for i in range(n_pair)])]
  transfers between devices with their start and end apart: 40 -> 40, of which waited for: 13 -> 12; matrix products, arithmetic and copies ran while one was open for 5% -> 6% of each run, Pallas kernels for 39% -> 38%
where the time goes in v5:
time: 213 us; the launch traced here: 212 us
  Pallas kernels  86.5 us (41%)
  starting transfers between devices  57.8 us (27%)
  waiting for transfers between devices  49.3 us (23%)
  local copies, waits for them, and re-layouts  14.3 us (7%)
  matrix products  2.15 us (1%)
    pallas_call x6, Pallas kernels, product(): pl.pallas_call(functools.partial(product_kernel, layout), grid_spec=pltpu...  53.2 us
    ppermute x22, starting transfers between devices, hop(): return lax.ppermute(x, 'pair', [(i, i ^ bits) for i in range(n_pair)])  48 us
    ppermute x22, waiting for transfers between devices, hop(): return lax.ppermute(x, 'pair', [(i, i ^ bits) for i in range(n_pair)])  44.7 us
    pallas_call x6, Pallas kernels, merge(): pl.pallas_call(merge_kernel, grid_spec=pltpu.PrefetchScalarGridSpec(num_s...  20.3 us
    ppermute x18, starting transfers between devices, swap(): return lax.ppermute(x, 'virt', [(i, i ^ bits) for i in range(n_virt)])  9.75 us
    unnamed x55, local copies, waits for them, and re-layouts  7.69 us
    pallas_call x4, Pallas kernels, finish(): pl.pallas_call(finish_kernel, grid=(cols // step,), in_specs=[here, here,...  7.36 us
    ppermute x18, waiting for transfers between devices, swap(): return lax.ppermute(x, 'virt', [(i, i ^ bits) for i in range(n_virt)])  4.61 us
  transfers between devices with their start and end apart: 40, of which 12 were waited for; matrix products, arithmetic and copies ran while one was open for 6% of the time, Pallas kernels for 38%

profile of v5, /device:TPU:0, one launch (start us, length us, event | category | flops | bytes accessed | tf_op | source)
XLA Modules:
  0.0 212.3 jit_solution(10107013413034540142)
XLA Ops:
  3.1 2.8 %pack_tiles.1 = (bf16[192,1024]{1,0:T(8,128)(2,1)}, bf16[192,1024]{1,0:T(8,128)(2,1)S(1)}, bf16[192,1024]{1,0:T(8,128)(2,1)S(1)}, bf16[192,1024]{1,0:T(8,128)(2,...) custom-call(s32[3,256]{1,0:T(4,128)S(1)} %fusion.30.codes_ref, ...), custom_call_target="tpu_custom_call" | custom-call | tf_op jit(solution)/shard_map/pack_tiles/pallas_call | solution.py:86
  5.9 3.0 %collective-permute-start.1 = (bf16[192,1024]{1,0:T(8,128)(2,1)S(1)}, bf16[192,1024]{1,0:T(8,128)(2,1)S(1)}, u32[]{:S(2)}, u32[]{:S(2)}) collective-permute-start(bf16[192,1024]{1,0:T(8,128)(2,1)S(1)} %get-tuple-element.59), channel_id=1, source_target_pairs={{0,8},{4,12},{8,0},{12,4},{16,24},{20,28},{24,16},{28,20},{1,9},{5... | collective-permute-start | bytes 1179656 | tf_op jit(solution)/shard_map/ppermute | solution.py:291
  14.2 4.3 %collective-permute-done.1 = bf16[192,1024]{1,0:T(8,128)(2,1)S(1)} collective-permute-done((bf16[192,1024]{1,0:T(8,128)(2,1)S(1)}, bf16[192,1024]{1,0:T(8,128)(2,1)S(1)}, u32[]{:S(2)}, u32[]{:S(2)}) %collective-permute-start.1) | collective-permute-done | bytes 393248 | tf_op jit(solution)/shard_map/ppermute | solution.py:291
  21.0 9.3 %collective-permute-start.8 = (s32[3,256]{1,0:T(4,128)S(1)}, s32[3,256]{1,0:T(4,128)S(1)}, u32[]{:S(2)}, u32[]{:S(2)}) collective-permute-start(s32[3,256]{1,0:T(4,128)S(1)} %bitcast.119), channel_id=1, source_target_pairs={{0,16},{4,20},{8,24},{12,28},{16,0},{20,4},{24,8},{28,12},{1,17},{... | collective-permute-start | bytes 9224 | tf_op jit(solution)/shard_map/ppermute | solution.py:291
  34.5 3.3 %collective-permute-start.3 = (bf16[192,1024]{1,0:T(8,128)(2,1)S(1)}, bf16[192,1024]{1,0:T(8,128)(2,1)}, u32[]{:S(2)}, u32[]{:S(2)}) collective-permute-start(bf16[192,1024]{1,0:T(8,128)(2,1)S(1)} %get-tuple-element.63), channel_id=1, source_target_pairs={{0,28},{4,24},{8,20},{12,16},{16,12},{20,8},{24,4},{28,0},{1,29},{... | collective-permute-start | bytes 1179656 | tf_op jit(solution)/shard_map/ppermute | solution.py:291
  43.8 9.3 %collective-permute-done.3 = bf16[192,1024]{1,0:T(8,128)(2,1)} collective-permute-done((bf16[192,1024]{1,0:T(8,128)(2,1)S(1)}, bf16[192,1024]{1,0:T(8,128)(2,1)}, u32[]{:S(2)}, u32[]{:S(2)}) %collective-permute-start.3) | collective-permute-done | bytes 393248 | tf_op jit(solution)/shard_map/ppermute | solution.py:291
  57.5 3.5 %collective-permute-start.10 = (bf16[192,1024]{1,0:T(8,128)(2,1)S(1)}, bf16[192,1024]{1,0:T(8,128)(2,1)S(1)}, u32[]{:S(2)}, u32[]{:S(2)}) collective-permute-start(bf16[192,1024]{1,0:T(8,128)(2,1)S(1)} %get-tuple-element.69), channel_id=1, source_target_pairs={{0,16},{4,20},{8,24},{12,28},{16,0},{20,4},{24,8},{28,12},{1,17},{... | collective-permute-start | bytes 1179656 | tf_op jit(solution)/shard_map/ppermute | solution.py:291
  69.1 4.1 %collective-permute-done.13 = bf16[192,1024]{1,0:T(8,128)(2,1)S(1)} collective-permute-done((bf16[192,1024]{1,0:T(8,128)(2,1)}, bf16[192,1024]{1,0:T(8,128)(2,1)S(1)}, u32[]{:S(2)}, u32[]{:S(2)}) %collective-permute-start.13) | collective-permute-done | bytes 393248 | tf_op jit(solution)/shard_map/ppermute | solution.py:294
  78.9 12.5 %tile_products.6 = (f32[2,2,96,1024]{3,2,1,0:T(8,128)S(1)}, bf16[2,2,96,1024]{3,2,1,0:T(8,128)(2,1)S(1)}) custom-call(s32[1]{0:T(128)} %pin.5.place_ref, bf16[4,2,96,1024]{3,2,1,0:T(8,128)(2,1)} %bitcast.5.refs_0_, bf16[4,2,96,1024]{3,2,1,0:T(8,128)(2,1)} %bitcast.6.refs_1_, bf16[4,2,96,1024]{3,2,1,0:T(8,128)(2,1)S(1)} %bitcast.114, ...), custom_call_target="tpu_custom_call" | custom-call | flops 99999997952 | tf_op jit(solution)/shard_map/tile_products/pallas_call | solution.py:126
  91.4 5.1 %collective-permute-done.16 = bf16[192,1024]{1,0:T(8,128)(2,1)S(1)} collective-permute-done((bf16[192,1024]{1,0:T(8,128)(2,1)}, bf16[192,1024]{1,0:T(8,128)(2,1)S(1)}, u32[]{:S(2)}, u32[]{:S(2)}) %collective-permute-start.16) | collective-permute-done | bytes 393248 | tf_op jit(solution)/shard_map/ppermute | solution.py:291
  98.5 12.3 %tile_products.7 = (f32[2,2,96,1024]{3,2,1,0:T(8,128)S(1)}, bf16[2,2,96,1024]{3,2,1,0:T(8,128)(2,1)S(1)}) custom-call(s32[1]{0:T(128)} %pin.5.place_ref, bf16[4,2,96,1024]{3,2,1,0:T(8,128)(2,1)} %bitcast.5.refs_0_, bf16[4,2,96,1024]{3,2,1,0:T(8,128)(2,1)} %bitcast.6.refs_1_, bf16[4,2,96,1024]{3,2,1,0:T(8,128)(2,1)S(1)} %bitcast.115, ...), custom_call_target="tpu_custom_call" | custom-call | flops 99999997952 | tf_op jit(solution)/shard_map/tile_products/pallas_call | solution.py:126
  111.9 4.8 %collective-permute-done.19.got0.got1 = bf16[2,2,96,1024]{3,2,1,0:T(8,128)(2,1)S(1)} collective-permute-done((bf16[2,2,96,1024]{3,2,1,0:T(8,128)(2,1)S(1)}, bf16[2,2,96,1024]{3,2,1,0:T(8,128)(2,1)S(1)}, u32[]{:S(2)}, u32[]{:S(2)}) %collective-permute-start.19) | collective-permute-done | bytes 786464 | tf_op jit(solution)/shard_map/ppermute | solution.py:291
  117.5 2.9 %merge_rows.6 = bf16[2,256,1024]{2,1,0:T(8,128)(2,1)S(1)} custom-call(s32[1]{0:T(128)} %pin.5.place_ref, bf16[4,256,384]{2,1,0:T(8,128)(2,1)S(1)} %fusion.7.pick_ref, f32[2,2,96,1024]{3,2,1,0:T(8,128)S(1)} %get-tuple-element.73.keep0.keep1, f32[2,2,96,1024]{3,2,1,0:T(8,128)S(1)} %get-tuple-element.73.keep0.keep1, ...), custom_call_target="tpu_custom_call" | custom-call | tf_op jit(solution)/shard_map/merge_rows/pallas_call | solution.py:191
  123.8 7.0 %tile_products.8 = (f32[2,2,96,512]{3,2,1,0:T(8,128)S(1)}, bf16[2,2,96,512]{3,2,1,0:T(8,128)(2,1)S(1)}) custom-call(s32[1]{0:T(128)} %pin.5.place_ref, bf16[1,2,96,1024]{3,2,1,0:T(8,128)(2,1)} %bitcast.15.refs_0_, bf16[1,2,96,1024]{3,2,1,0:T(8,128)(2,1)} %bitcast.16.refs_1_, bf16[1,2,96,1024]{3,2,1,0:T(8,128)(2,1)} %bitcast.17.refs_2_, ...), custom_call_target="tpu_custom_call" | custom-call | flops 99999997952 | tf_op jit(solution)/shard_map/tile_products/pallas_call | solution.py:126
  131.2 7.0 %tile_products.9 = (f32[2,2,96,512]{3,2,1,0:T(8,128)S(1)}, bf16[2,2,96,512]{3,2,1,0:T(8,128)(2,1)S(1)}) custom-call(s32[1]{0:T(128)} %pin.5.place_ref, bf16[1,2,96,1024]{3,2,1,0:T(8,128)(2,1)} %bitcast.15.refs_0_, bf16[1,2,96,1024]{3,2,1,0:T(8,128)(2,1)} %bitcast.16.refs_1_, bf16[1,2,96,1024]{3,2,1,0:T(8,128)(2,1)} %bitcast.17.refs_2_, ...), custom_call_target="tpu_custom_call" | custom-call | flops 8000000000 | tf_op jit(solution)/shard_map/tile_products/pallas_call | solution.py:126
  140.9 3.7 %merge_rows.7 = bf16[2,256,1024]{2,1,0:T(8,128)(2,1)} custom-call(s32[1]{0:T(128)} %pin.5.place_ref, bf16[4,256,384]{2,1,0:T(8,128)(2,1)S(1)} %fusion.7.pick_ref, f32[2,2,96,1024]{3,2,1,0:T(8,128)S(1)} %get-tuple-element.77.keep0.keep1, f32[2,2,96,1024]{3,2,1,0:T(8,128)S(1)} %get-tuple-element.77.keep0.keep1, ...), custom_call_target="tpu_custom_call" | custom-call | tf_op jit(solution)/shard_map/merge_rows/pallas_call | solution.py:191
  151.7 7.0 %tile_products.10 = (f32[2,2,96,512]{3,2,1,0:T(8,128)S(1)}, bf16[2,2,96,512]{3,2,1,0:T(8,128)(2,1)S(1)}) custom-call(s32[1]{0:T(128)} %pin.5.place_ref, bf16[1,2,96,1024]{3,2,1,0:T(8,128)(2,1)} %bitcast.15.refs_0_, bf16[1,2,96,1024]{3,2,1,0:T(8,128)(2,1)} %bitcast.16.refs_1_, bf16[1,2,96,1024]{3,2,1,0:T(8,128)(2,1)} %bitcast.17.refs_2_, ...), custom_call_target="tpu_custom_call" | custom-call | flops 99999997952 | tf_op jit(solution)/shard_map/tile_products/pallas_call | solution.py:126
  158.7 3.1 %merge_rows.9 = (f32[1,256,512]{2,1,0:T(8,128)S(1)}, bf16[1,256,512]{2,1,0:T(8,128)(2,1)}) custom-call(s32[1]{0:T(128)} %pin.5.place_ref, bf16[4,256,384]{2,1,0:T(8,128)(2,1)S(1)} %fusion.7.pick_ref, f32[2,2,96,512]{3,2,1,0:T(8,128)S(1)} %get-tuple-element.84.keep0.keep1, f32[2,2,96,512]{3,2,1,0:T(8,128)S(1)} %get-tuple-element.84.keep0.keep1, ...), custom_call_target="tpu_custom_call" | custom-call | tf_op jit(solution)/shard_map/merge_rows/pallas_call | solution.py:191
  163.6 7.3 %tile_products.11 = (f32[2,2,96,512]{3,2,1,0:T(8,128)S(1)}, bf16[2,2,96,512]{3,2,1,0:T(8,128)(2,1)S(1)}) custom-call(s32[1]{0:T(128)} %pin.5.place_ref, bf16[1,2,96,1024]{3,2,1,0:T(8,128)(2,1)} %bitcast.15.refs_0_, bf16[1,2,96,1024]{3,2,1,0:T(8,128)(2,1)} %bitcast.16.refs_1_, bf16[1,2,96,1024]{3,2,1,0:T(8,128)(2,1)} %bitcast.17.refs_2_, ...), custom_call_target="tpu_custom_call" | custom-call | flops 99999997952 | tf_op jit(solution)/shard_map/tile_products/pallas_call | solution.py:126
  175.8 4.0 %merge_rows.10 = (f32[1,256,512]{2,1,0:T(8,128)S(1)}, bf16[1,256,512]{2,1,0:T(8,128)(2,1)}) custom-call(s32[1]{0:T(128)} %pin.5.place_ref, bf16[4,256,384]{2,1,0:T(8,128)(2,1)S(1)} %fusion.7.pick_ref, f32[2,2,96,512]{3,2,1,0:T(8,128)S(1)} %get-tuple-element.91.keep0.keep1, f32[2,2,96,512]{3,2,1,0:T(8,128)S(1)} %get-tuple-element.91.keep0.keep1, ...), custom_call_target="tpu_custom_call" | custom-call | flops 99999997952 | tf_op jit(solution)/shard_map/merge_rows/pallas_call | solution.py:191
  180.7 3.3 %collective-permute-start.38 = (bf16[1,256,512]{2,1,0:T(8,128)(2,1)}, bf16[1,256,512]{2,1,0:T(8,128)(2,1)}, u32[]{:S(2)}, u32[]{:S(2)}) collective-permute-start(bf16[1,256,512]{2,1,0:T(8,128)(2,1)} %get-tuple-element.107), channel_id=1, source_target_pairs={{0,16},{4,20},{8,24},{12,28},{16,0},{20,4},{24,8},{28,12},{1,17},{... | collective-permute-start | bytes 786440 | tf_op jit(solution)/shard_map/ppermute | solution.py:291
  183.9 4.2 %merge_rows.11 = (f32[1,256,512]{2,1,0:T(8,128)S(1)}, bf16[1,256,512]{2,1,0:T(8,128)(2,1)}) custom-call(s32[1]{0:T(128)} %pin.5.place_ref, bf16[4,256,384]{2,1,0:T(8,128)(2,1)S(1)} %fusion.7.pick_ref, f32[2,2,96,512]{3,2,1,0:T(8,128)S(1)} %get-tuple-element.96.keep0.keep1, f32[2,2,96,512]{3,2,1,0:T(8,128)S(1)} %get-tuple-element.96.keep0.keep1, ...), custom_call_target="tpu_custom_call" | custom-call | flops 99999997952 | tf_op jit(solution)/shard_map/merge_rows/pallas_call | solution.py:191
  192.8 12.0 %collective-permute-done.38.got_ref = bf16[1,256,512]{2,1,0:T(8,128)(2,1)} collective-permute-done((bf16[1,256,512]{2,1,0:T(8,128)(2,1)}, bf16[1,256,512]{2,1,0:T(8,128)(2,1)}, u32[]{:S(2)}, u32[]{:S(2)}) %collective-permute-start.38) | collective-permute-done | bytes 262176 | tf_op jit(solution)/shard_map/ppermute | solution.py:291
  206.8 3.5 %collective-permute-done.37.got_ref = bf16[1,256,512]{2,1,0:T(8,128)(2,1)} collective-permute-done((bf16[1,256,512]{2,1,0:T(8,128)(2,1)}, bf16[1,256,512]{2,1,0:T(8,128)(2,1)}, u32[]{:S(2)}, u32[]{:S(2)}) %collective-permute-start.37) | collective-permute-done | bytes 262176 | tf_op jit(solution)/shard_map/ppermute | solution.py:291
  (158 shorter events, 72.6 us)
Async XLA Ops:
  9.0 21.3 %collective-permute-start.2 = (bf16[192,1024]{1,0:T(8,128)(2,1)}, bf16[192,1024]{1,0:T(8,128)(2,1)}, u32[]{:S(2)}, u32[]{:S(2)}) collective-permute-start(bf16[192,1024]{1,0:T(8,128)(2,1)} %get-tuple-element.60), channel_id=1, source_target_pairs={{0,2},{1,3},{2,0},{3,1},{4,6},{5,7},{6,4},{7,5},{8,10},{9,11},{10,... | collective-permute-start | bytes 1179656 | tf_op jit(solution)/shard_map/ppermute | solution.py:294
  10.5 19.7 %collective-permute-start = (bf16[192,1024]{1,0:T(8,128)(2,1)S(1)}, bf16[192,1024]{1,0:T(8,128)(2,1)S(1)}, u32[]{:S(2)}, u32[]{:S(2)}) collective-permute-start(bf16[192,1024]{1,0:T(8,128)(2,1)S(1)} %get-tuple-element.58), channel_id=1, source_target_pairs={{0,24},{4,28},{8,16},{12,20},{16,8},{20,12},{24,0},{28,4},{1,25},{... | collective-permute-start | bytes 1179656 | tf_op jit(solution)/shard_map/ppermute | solution.py:291
  13.0 98.1 %collective-permute-start.20 = (bf16[192,1024]{1,0:T(8,128)(2,1)}, bf16[192,1024]{1,0:T(8,128)(2,1)}, u32[]{:S(2)}, u32[]{:S(2)}) collective-permute-start(bf16[192,1024]{1,0:T(8,128)(2,1)} %get-tuple-element.60), channel_id=1, source_target_pairs={{0,1},{1,0},{2,3},{3,2},{4,5},{5,4},{6,7},{7,6},{8,9},{9,8},{10,11... | collective-permute-start | bytes 1179656 | tf_op jit(solution)/shard_map/ppermute | solution.py:294
  18.5 16.0 %collective-permute-start.7 = (s32[3,256]{1,0:T(4,128)S(1)}, s32[3,256]{1,0:T(4,128)S(1)}, u32[]{:S(2)}, u32[]{:S(2)}) collective-permute-start(s32[3,256]{1,0:T(4,128)S(1)} %bitcast.118), channel_id=1, source_target_pairs={{0,8},{4,12},{8,0},{12,4},{16,24},{20,28},{24,16},{28,20},{1,9},{5... | collective-permute-start | bytes 9224 | tf_op jit(solution)/shard_map/ppermute | solution.py:291
  21.0 16.8 %collective-permute-start.8 = (s32[3,256]{1,0:T(4,128)S(1)}, s32[3,256]{1,0:T(4,128)S(1)}, u32[]{:S(2)}, u32[]{:S(2)}) collective-permute-start(s32[3,256]{1,0:T(4,128)S(1)} %bitcast.119), channel_id=1, source_target_pairs={{0,16},{4,20},{8,24},{12,28},{16,0},{20,4},{24,8},{28,12},{1,17},{... | collective-permute-start | bytes 9224 | tf_op jit(solution)/shard_map/ppermute | solution.py:291
  34.5 18.7 %collective-permute-start.3 = (bf16[192,1024]{1,0:T(8,128)(2,1)S(1)}, bf16[192,1024]{1,0:T(8,128)(2,1)}, u32[]{:S(2)}, u32[]{:S(2)}) collective-permute-start(bf16[192,1024]{1,0:T(8,128)(2,1)S(1)} %get-tuple-element.63), channel_id=1, source_target_pairs={{0,28},{4,24},{8,20},{12,16},{16,12},{20,8},{24,4},{28,0},{1,29},{... | collective-permute-start | bytes 1179656 | tf_op jit(solution)/shard_map/ppermute | solution.py:291
  37.8 15.4 %collective-permute-start.5 = (bf16[192,1024]{1,0:T(8,128)(2,1)S(1)}, bf16[192,1024]{1,0:T(8,128)(2,1)S(1)}, u32[]{:S(2)}, u32[]{:S(2)}) collective-permute-start(bf16[192,1024]{1,0:T(8,128)(2,1)S(1)} %collective-permute-done.1), channel_id=1, source_target_pairs={{0,2},{1,3},{2,0},{3,1},{4,6},{5,7},{6,4},{7,5},{8,10},{9,11},{10,... | collective-permute-start | bytes 1179656 | tf_op jit(solution)/shard_map/ppermute | solution.py:294
  39.4 14.3 %collective-permute-start.6 = (bf16[192,1024]{1,0:T(8,128)(2,1)S(1)}, bf16[192,1024]{1,0:T(8,128)(2,1)S(1)}, u32[]{:S(2)}, u32[]{:S(2)}) collective-permute-start(bf16[192,1024]{1,0:T(8,128)(2,1)S(1)} %collective-permute-done), channel_id=1, source_target_pairs={{0,2},{1,3},{2,0},{3,1},{4,6},{5,7},{6,4},{7,5},{8,10},{9,11},{10,... | collective-permute-start | bytes 1179656 | tf_op jit(solution)/shard_map/ppermute | solution.py:294
  68.6 42.8 %collective-permute-start.21 = (bf16[192,1024]{1,0:T(8,128)(2,1)}, bf16[192,1024]{1,0:T(8,128)(2,1)}, u32[]{:S(2)}, u32[]{:S(2)}) collective-permute-start(bf16[192,1024]{1,0:T(8,128)(2,1)} %collective-permute-done.2), channel_id=1, source_target_pairs={{0,1},{1,0},{2,3},{3,2},{4,5},{5,4},{6,7},{7,6},{8,9},{9,8},{10,11... | collective-permute-start | bytes 1179656 | tf_op jit(solution)/shard_map/ppermute | solution.py:294
  74.5 22.0 %collective-permute-start.16 = (bf16[192,1024]{1,0:T(8,128)(2,1)}, bf16[192,1024]{1,0:T(8,128)(2,1)S(1)}, u32[]{:S(2)}, u32[]{:S(2)}) collective-permute-start(bf16[192,1024]{1,0:T(8,128)(2,1)} %get-tuple-element.75), channel_id=1, source_target_pairs={{0,20},{4,16},{8,28},{12,24},{16,4},{20,0},{24,12},{28,8},{1,21},{... | collective-permute-start | bytes 1179656 | tf_op jit(solution)/shard_map/ppermute | solution.py:291
  76.9 19.6 %collective-permute-start.17 = (bf16[192,1024]{1,0:T(8,128)(2,1)S(1)}, bf16[192,1024]{1,0:T(8,128)(2,1)S(1)}, u32[]{:S(2)}, u32[]{:S(2)}) collective-permute-start(bf16[192,1024]{1,0:T(8,128)(2,1)S(1)} %collective-permute-done.11), channel_id=1, source_target_pairs={{0,2},{1,3},{2,0},{3,1},{4,6},{5,7},{6,4},{7,5},{8,10},{9,11},{10,... | collective-permute-start | bytes 1179656 | tf_op jit(solution)/shard_map/ppermute | solution.py:294
  77.2 19.7 %collective-permute-start.18 = (bf16[192,1024]{1,0:T(8,128)(2,1)S(1)}, bf16[192,1024]{1,0:T(8,128)(2,1)S(1)}, u32[]{:S(2)}, u32[]{:S(2)}) collective-permute-start(bf16[192,1024]{1,0:T(8,128)(2,1)S(1)} %collective-permute-done.10), channel_id=1, source_target_pairs={{0,2},{1,3},{2,0},{3,1},{4,6},{5,7},{6,4},{7,5},{8,10},{9,11},{10,... | collective-permute-start | bytes 1179656 | tf_op jit(solution)/shard_map/ppermute | solution.py:294
  96.5 15.1 %collective-permute-start.24 = (bf16[192,1024]{1,0:T(8,128)(2,1)S(1)}, bf16[192,1024]{1,0:T(8,128)(2,1)S(1)}, u32[]{:S(2)}, u32[]{:S(2)}) collective-permute-start(bf16[192,1024]{1,0:T(8,128)(2,1)S(1)} %collective-permute-done.11), channel_id=1, source_target_pairs={{0,1},{1,0},{2,3},{3,2},{4,5},{5,4},{6,7},{7,6},{8,9},{9,8},{10,11... | collective-permute-start | bytes 1179656 | tf_op jit(solution)/shard_map/ppermute | solution.py:294
  96.5 14.3 %collective-permute-start.27 = (bf16[192,1024]{1,0:T(8,128)(2,1)S(1)}, bf16[192,1024]{1,0:T(8,128)(2,1)S(1)}, u32[]{:S(2)}, u32[]{:S(2)}) collective-permute-start(bf16[192,1024]{1,0:T(8,128)(2,1)S(1)} %collective-permute-done.16), channel_id=1, source_target_pairs={{0,2},{1,3},{2,0},{3,1},{4,6},{5,7},{6,4},{7,5},{8,10},{9,11},{10,... | collective-permute-start | bytes 1179656 | tf_op jit(solution)/shard_map/ppermute | solution.py:294
  96.9 19.8 %collective-permute-start.19 = (bf16[2,2,96,1024]{3,2,1,0:T(8,128)(2,1)S(1)}, bf16[2,2,96,1024]{3,2,1,0:T(8,128)(2,1)S(1)}, u32[]{:S(2)}, u32[]{:S(2)}) collective-permute-start(bf16[2,2,96,1024]{3,2,1,0:T(8,128)(2,1)S(1)} %get-tuple-element.79), channel_id=1, source_target_pairs={{0,4},{4,0},{8,12},{12,8},{16,20},{20,16},{24,28},{28,24},{1,5},{5... | collective-permute-start | bytes 2359304 | tf_op jit(solution)/shard_map/ppermute | solution.py:291
  120.5 20.4 %collective-permute-start.29 = (bf16[2,2,96,1024]{3,2,1,0:T(8,128)(2,1)S(1)}, bf16[2,2,96,1024]{3,2,1,0:T(8,128)(2,1)S(1)}, u32[]{:S(2)}, u32[]{:S(2)}) collective-permute-start(bf16[2,2,96,1024]{3,2,1,0:T(8,128)(2,1)S(1)} %get-tuple-element.86), channel_id=1, source_target_pairs={{0,4},{4,0},{8,12},{12,8},{16,20},{20,16},{24,28},{28,24},{1,5},{5... | collective-permute-start | bytes 2359304 | tf_op jit(solution)/shard_map/ppermute | solution.py:291
  122.3 27.0 %collective-permute-start.31 = (bf16[2,256,1024]{2,1,0:T(8,128)(2,1)S(1)}, bf16[2,256,1024]{2,1,0:T(8,128)(2,1)S(1)}, u32[]{:S(2)}, u32[]{:S(2)}) collective-permute-start(bf16[2,256,1024]{2,1,0:T(8,128)(2,1)S(1)} %merge_rows.6), channel_id=1, source_target_pairs={{0,8},{4,12},{8,0},{12,4},{16,24},{20,28},{24,16},{28,20},{1,9},{5... | collective-permute-start | bytes 3145736 | tf_op jit(solution)/shard_map/ppermute | solution.py:291
  130.8 18.4 %collective-permute-start.30 = (bf16[2,2,96,512]{3,2,1,0:T(8,128)(2,1)S(1)}, bf16[2,2,96,512]{3,2,1,0:T(8,128)(2,1)S(1)}, u32[]{:S(2)}, u32[]{:S(2)}) collective-permute-start(bf16[2,2,96,512]{3,2,1,0:T(8,128)(2,1)S(1)} %get-tuple-element.88), channel_id=1, source_target_pairs={{0,4},{4,0},{8,12},{12,8},{16,20},{20,16},{24,28},{28,24},{1,5},{5... | collective-permute-start | bytes 1179656 | tf_op jit(solution)/shard_map/ppermute | solution.py:291
  144.6 31.3 %collective-permute-start.35 = (bf16[2,256,1024]{2,1,0:T(8,128)(2,1)}, bf16[2,256,1024]{2,1,0:T(8,128)(2,1)}, u32[]{:S(2)}, u32[]{:S(2)}) collective-permute-start(bf16[2,256,1024]{2,1,0:T(8,128)(2,1)} %merge_rows.7), channel_id=1, source_target_pairs={{0,8},{4,12},{8,0},{12,4},{16,24},{20,28},{24,16},{28,20},{1,9},{5... | collective-permute-start | bytes 3145736 | tf_op jit(solution)/shard_map/ppermute | solution.py:291
  161.9 13.7 %collective-permute-start.33 = (bf16[1,256,512]{2,1,0:T(8,128)(2,1)S(1)}, bf16[1,256,512]{2,1,0:T(8,128)(2,1)S(1)}, u32[]{:S(2)}, u32[]{:S(2)}) collective-permute-start(bf16[1,256,512]{2,1,0:T(8,128)(2,1)S(1)} %get-tuple-element.97), channel_id=1, source_target_pairs={{0,16},{4,20},{8,24},{12,28},{16,0},{20,4},{24,8},{28,12},{1,17},{... | collective-permute-start | bytes 786440 | tf_op jit(solution)/shard_map/ppermute | solution.py:291
  162.1 13.7 %collective-permute-start.34 = (bf16[2,2,96,512]{3,2,1,0:T(8,128)(2,1)S(1)}, bf16[2,2,96,512]{3,2,1,0:T(8,128)(2,1)S(1)}, u32[]{:S(2)}, u32[]{:S(2)}) collective-permute-start(bf16[2,2,96,512]{3,2,1,0:T(8,128)(2,1)S(1)} %get-tuple-element.99), channel_id=1, source_target_pairs={{0,4},{4,0},{8,12},{12,8},{16,20},{20,16},{24,28},{28,24},{1,5},{5... | collective-permute-start | bytes 1179656 | tf_op jit(solution)/shard_map/ppermute | solution.py:291
  171.5 19.2 %collective-permute-start.39 = (bf16[1,256,512]{2,1,0:T(8,128)(2,1)}, bf16[1,256,512]{2,1,0:T(8,128)(2,1)}, u32[]{:S(2)}, u32[]{:S(2)}) collective-permute-start(bf16[1,256,512]{2,1,0:T(8,128)(2,1)} %get-tuple-element.109), channel_id=1, source_target_pairs={{0,16},{4,20},{8,24},{12,28},{16,0},{20,4},{24,8},{28,12},{1,17},{... | collective-permute-start | bytes 786440 | tf_op jit(solution)/shard_map/ppermute | solution.py:291
  180.7 24.1 %collective-permute-start.38 = (bf16[1,256,512]{2,1,0:T(8,128)(2,1)}, bf16[1,256,512]{2,1,0:T(8,128)(2,1)}, u32[]{:S(2)}, u32[]{:S(2)}) collective-permute-start(bf16[1,256,512]{2,1,0:T(8,128)(2,1)} %get-tuple-element.107), channel_id=1, source_target_pairs={{0,16},{4,20},{8,24},{12,28},{16,0},{20,4},{24,8},{28,12},{1,17},{... | collective-permute-start | bytes 786440 | tf_op jit(solution)/shard_map/ppermute | solution.py:291
  188.9 21.4 %collective-permute-start.37 = (bf16[1,256,512]{2,1,0:T(8,128)(2,1)}, bf16[1,256,512]{2,1,0:T(8,128)(2,1)}, u32[]{:S(2)}, u32[]{:S(2)}) collective-permute-start(bf16[1,256,512]{2,1,0:T(8,128)(2,1)} %get-tuple-element.105), channel_id=1, source_target_pairs={{0,16},{4,20},{8,24},{12,28},{16,0},{20,4},{24,8},{28,12},{1,17},{... | collective-permute-start | bytes 786440 | tf_op jit(solution)/shard_map/ppermute | solution.py:291
  (39 other events, 387.5 us)
